TPU v7x, 256 devices: a whole 4x4x8 slice. The times are simulated.
256 devices in a mesh: tok: 16 (over z_lo, y, core), feat: 16 (over x, z_hi).
Axes of the slice: x: 4, y: 4, z: 8 (z_hi: 4, z_lo: 2; z = z_hi * 2 + z_lo), core: 2. Of those that a mesh axis runs over, the one named last changes fastest.
Arguments:
- tokens: bfloat16 [16384, 2048], P('tok', 'feat'), may hold values from -6 to 6
- level_bits: int32 [2, 4], replicated, may hold values from 0 to 3, each once within a row
- up_blocks: bfloat16 [2, 16, 5, 128, 512], P(None, 'feat', None, None, 'tok'), may hold values from -0.21875 to 0.21875
- down_blocks: bfloat16 [2, 16, 5, 512, 128], P(None, 'feat', None, None, 'tok'), may hold values from -0.109375 to 0.109375
- rank_in: bfloat16 [2, 2048, 256], replicated, may hold values from -0.125 to 0.125
- rank_up: bfloat16 [2, 256, 8192], P(None, None, 'feat'), may hold values from -0.15625 to 0.15625
- rank_down: bfloat16 [2, 8192, 256], P(None, 'feat'), may hold values from -0.0625 to 0.0625
- rank_out: bfloat16 [2, 256, 2048], P(None, None, 'feat'), may hold values from -0.15625 to 0.15625
Outputs:
- outputs: bfloat16 [16384, 2048], P('tok', 'feat')
Inputs may be any that keep to these rules, and one draw needn't show every extreme that they name: `level_bits`: each row is a permutation of the bits 0 to 3.
All inputs are finite; a program needn't handle non-finite values.
Results may differ from a plain program's by a relative error of at most 0.015.
Values may be sent and summed in bfloat16 or wider, within the bound.
No kernel may reach another device: no remote copies, remote signals or barrier semaphores. Data moves between devices by JAX's collectives and lax.ppermute only.
A program may use at most 64 MiB of HBM per device.

v0:
```python
import jax
import jax.numpy as jnp
from jax import lax
from jax.sharding import PartitionSpec as P

D = 2048
HID = 8192
NB = 16
LAYERS = 2


def from_partner(value, axis, distance):
    return lax.ppermute(value, axis, [(i, i ^ 1 << distance) for i in range(lax.axis_size(axis))])


def block_product(left, right):
    return jnp.einsum("tjd,jdh->tjh", left, right, preferred_element_type=jnp.float32)


def level_weight(weights, bits_row, bit_num):
    level_num = jnp.sum(
        jnp.where(bits_row == bit_num, jnp.arange(bits_row.shape[0], dtype=jnp.int32), 0)
    )
    return lax.dynamic_index_in_dim(weights, 1 + level_num, 1, keepdims=False)


def per_device(tokens, level_bits, up_blocks, down_blocks, rank_in, rank_up, rank_down, rank_out):
    width_block = D // NB
    hidden_block = HID // NB
    local_width = tokens.shape[1]
    local_blocks = local_width // width_block
    local_bits = local_blocks.bit_length() - 1
    all_bits = NB.bit_length() - 1
    rows = tokens.shape[0]
    my_index = lax.axis_index("feat")
    current = tokens
    for layer_num in range(LAYERS):
        bits_row = level_bits[layer_num]
        up_whole, down_whole = (
            lax.all_gather(up_blocks[layer_num], "tok", axis=3, tiled=True),
            lax.all_gather(down_blocks[layer_num], "tok", axis=3, tiled=True),
        )
        blocked = current.reshape(rows, local_blocks, width_block)
        pre_act = block_product(blocked, up_whole[:, 0])
        for bit_num in range(all_bits):
            partner = from_partner(blocked, "feat", bit_num - local_bits)
            pre_act = pre_act + block_product(partner, level_weight(up_whole, bits_row, bit_num))
        rows_in = lax.dynamic_slice_in_dim(
            rank_in[layer_num], my_index * local_width, local_width, 0
        )
        partial_latent = jnp.dot(current, rows_in, preferred_element_type=jnp.float32)
        latent = lax.psum(partial_latent.astype(jnp.bfloat16), "feat")
        pre_act = pre_act + jnp.dot(
            latent, rank_up[layer_num], preferred_element_type=jnp.float32
        ).reshape(rows, local_blocks, hidden_block)
        hidden = jax.nn.gelu(pre_act, approximate=False).astype(jnp.bfloat16)
        partial_back = jnp.dot(
            hidden.reshape(rows, -1), rank_down[layer_num], preferred_element_type=jnp.float32
        )
        latent_back = lax.psum(partial_back.astype(jnp.bfloat16), "feat")
        result = jnp.dot(
            latent_back, rank_out[layer_num], preferred_element_type=jnp.float32
        ).reshape(rows, local_blocks, width_block)
        result = result + block_product(hidden, down_whole[:, 0])
        for bit_num in range(all_bits):
            weight = level_weight(down_whole, bits_row, bit_num)
            term = block_product(hidden, weight)
            term = from_partner(term.astype(jnp.bfloat16), "feat", bit_num - local_bits).astype(
                term.dtype
            )
            result = result + term
        current = (current.astype(jnp.float32) + result.reshape(rows, -1)).astype(jnp.bfloat16)
    return current


def solution(mesh):
    return jax.shard_map(
        per_device,
        mesh=mesh,
        in_specs=(
            P("tok", "feat"),
            P(),
            P(None, "feat", None, None, "tok"),
            P(None, "feat", None, None, "tok"),
            P(),
            P(None, None, "feat"),
            P(None, "feat", None),
            P(None, None, "feat"),
        ),
        out_specs=P("tok", "feat"),
        check_vma=False,
    )
```

profile of v0, /device:TPU:1, one launch (start us, length us, event | category | flops | bytes accessed | tf_op | source)
XLA Modules:
  0.0 724.6 jit_solution(13783253793936195851)
XLA Ops:
  6.5 2.0 collective-permute-start.2
  8.6 6.9 collective-permute-start.1
  16.7 2.5 collective-permute-start.3
  19.1 2.8 fusion.150
  28.7 25.5 %all-gather = bf16[1,1,5,128,512]{3,4,2,1,0:T(8,128)(2,1)S(1)} all-gather(bf16[1,1,5,128,32]{3,4,2,1,0:T(8,128)(2,1)S(1)} %get-tuple-element.18), channel_id=2, replica_groups=mesh['tok'=16,'feat'=16] {'tok'}, dimensions={4}, use_global_device_ids=true | all-gather | bytes 696320 | tf_op jit(solution)/shard_map/all_gather | solution.py:40
  54.8 18.3 %all-gather.1 = bf16[1,1,5,512,128]{3,4,2,1,0:T(8,128)(2,1)S(1)} all-gather(bf16[1,1,5,512,8]{3,4,2,1,0:T(8,128)(2,1)S(1)} %get-tuple-element.16), channel_id=3, replica_groups=mesh['tok'=16,'feat'=16] {'tok'}, dimensions={4}, use_global_device_ids=true | all-gather | bytes 696320 | tf_op jit(solution)/shard_map/all_gather | solution.py:41
  73.0 21.4 %all-gather.2 = bf16[1,1,5,128,512]{3,4,2,1,0:T(8,128)(2,1)S(1)} all-gather(bf16[1,1,5,128,32]{3,4,2,1,0:T(8,128)(2,1)S(1)} %get-tuple-element.17), channel_id=4, replica_groups=mesh['tok'=16,'feat'=16] {'tok'}, dimensions={4}, use_global_device_ids=true | all-gather | bytes 696320 | tf_op jit(solution)/shard_map/all_gather | solution.py:40
  96.2 1.8 fusion.68
  99.7 1.8 fusion.72
  101.5 78.9 %all-reduce.5.cloned.1.call-done = bf16[1024,256]{0,1:T(8,128)(2,1)} async-done(((bf16[1024,256]{0,1:T(8,128)(2,1)}), bf16[1024,256]{0,1:T(8,128)(2,1)}) %all-reduce.5.cloned.1.call-update) | async-done | bytes 524304 | tf_op jit(solution)/shard_map/psum | solution.py:52
  182.1 7.0 fusion.2
  195.9 5.5 collective-permute-start.7
  201.5 35.0 %all-gather.3 = bf16[1,1,5,512,128]{3,4,2,1,0:T(8,128)(2,1)S(1)} all-gather(bf16[1,1,5,512,8]{3,4,2,1,0:T(8,128)(2,1)} %get-tuple-element.15), channel_id=5, replica_groups=mesh['tok'=16,'feat'=16] {'tok'}, dimensions={4}, use_global_device_ids=true | all-gather | bytes 696320 | tf_op jit(solution)/shard_map/all_gather | solution.py:41
  242.7 116.6 %all-reduce.7.cloned.1.call-done = bf16[1024,256]{1,0:T(8,128)(2,1)} async-done(((bf16[1024,256]{1,0:T(8,128)(2,1)}), bf16[1024,256]{1,0:T(8,128)(2,1)}) %all-reduce.7.cloned.1.call-update) | async-done | bytes 524304 | tf_op jit(solution)/shard_map/psum | solution.py:60
  359.3 1.9 fusion.47
  362.5 5.4 collective-permute-start.11
  367.9 1.9 convolution_convert_fusion.2
  369.9 1.8 fusion.78
  377.1 161.9 %all-reduce.9.cloned.1.call-done = bf16[1024,256]{1,0:T(8,128)(2,1)} async-done(((bf16[1024,256]{1,0:T(8,128)(2,1)}), bf16[1024,256]{1,0:T(8,128)(2,1)}) %all-reduce.9.cloned.1.call-update) | async-done | bytes 524304 | tf_op jit(solution)/shard_map/psum | solution.py:52
  540.7 7.0 fusion.5
  552.5 5.5 collective-permute-start.15
  558.5 7.5 %collective-permute-done.12 = bf16[1024,1,128]{2,0,1:T(8,128)(2,1)S(1)} collective-permute-done((bf16[1024,1,128]{2,0,1:T(8,128)(2,1)S(1)}, bf16[1024,1,128]{2,0,1:T(8,128)(2,1)S(1)}, u32[]{:S(2)}, u32[]{:S(2)}) %collective-permute-start.12) | collective-permute-done | bytes 262176 | tf_op jit(solution)/shard_map/ppermute | solution.py:13
  567.4 148.3 %all-reduce.11.cloned.1.call-done = bf16[1024,256]{1,0:T(8,128)(2,1)} async-done(((bf16[1024,256]{1,0:T(8,128)(2,1)}), bf16[1024,256]{1,0:T(8,128)(2,1)}) %all-reduce.11.cloned.1.call-update) | async-done | bytes 524304 | tf_op jit(solution)/shard_map/psum | solution.py:60
  715.7 2.3 fusion.46
  (82 shorter events, 32.1 us)
Async XLA Ops:
  6.5 173.9 %all-reduce.5.cloned.1.call-start = ((), (), s32[]{:S(2)}) async-start(), calls=%async_computation | async-start | bytes 1048576 | tf_op jit(solution)/shard_map/psum | solution.py:52
  6.5 89.7 %collective-permute-start.2 = (bf16[1024,1,128]{2,0,1:T(8,128)(2,1)}, bf16[1024,1,128]{2,0,1:T(8,128)(2,1)S(1)}, u32[]{:S(2)}, u32[]{:S(2)}) collective-permute-start(bf16[1024,1,128]{2,0,1:T(8,128)(2,1)} %bitcast.292), channel_id=1, source_target_pairs={{0,4},{1,5},{2,6},{3,7},{4,0},{5,1},{6,2},{7,3},{8,12},{9,13},{10,... | collective-permute-start | bytes 786440 | tf_op jit(solution)/shard_map/ppermute | solution.py:13
  8.6 89.4 %collective-permute-start.1 = (bf16[1024,1,128]{2,0,1:T(8,128)(2,1)}, bf16[1024,1,128]{2,0,1:T(8,128)(2,1)S(1)}, u32[]{:S(2)}, u32[]{:S(2)}) collective-permute-start(bf16[1024,1,128]{2,0,1:T(8,128)(2,1)} %bitcast.293), channel_id=1, source_target_pairs={{0,2},{1,3},{2,0},{3,1},{4,6},{5,7},{6,4},{7,5},{8,10},{9,11},{10,... | collective-permute-start | bytes 786440 | tf_op jit(solution)/shard_map/ppermute | solution.py:13
  15.5 84.3 %collective-permute-start = (bf16[1024,1,128]{2,0,1:T(8,128)(2,1)}, bf16[1024,1,128]{2,0,1:T(8,128)(2,1)S(1)}, u32[]{:S(2)}, u32[]{:S(2)}) collective-permute-start(bf16[1024,1,128]{2,0,1:T(8,128)(2,1)} %bitcast.294), channel_id=1, source_target_pairs={{0,1},{1,0},{2,3},{3,2},{4,5},{5,4},{6,7},{7,6},{8,9},{9,8},{10,11... | collective-permute-start | bytes 786440 | tf_op jit(solution)/shard_map/ppermute | solution.py:13
  16.7 165.4 %collective-permute-start.3 = (bf16[1024,1,128]{2,0,1:T(8,128)(2,1)}, bf16[1024,1,128]{2,0,1:T(8,128)(2,1)S(1)}, u32[]{:S(2)}, u32[]{:S(2)}) collective-permute-start(bf16[1024,1,128]{2,0,1:T(8,128)(2,1)} %bitcast.295), channel_id=1, source_target_pairs={{0,8},{1,9},{2,10},{3,11},{4,12},{5,13},{6,14},{7,15},{8,0},{9,1},... | collective-permute-start | bytes 786440 | tf_op jit(solution)/shard_map/ppermute | solution.py:13
  21.9 32.2 %copy-start.9 = (bf16[2,1,5,512,8]{3,4,2,1,0:T(8,128)(2,1)S(1)}, bf16[2,1,5,512,8]{3,4,2,1,0:T(8,128)(2,1)}, u32[]{:S(2)}) copy-start(bf16[2,1,5,512,8]{3,4,2,1,0:T(8,128)(2,1)} %param.11) | copy-start | bytes 245764
  23.1 336.2 %all-reduce.7.cloned.1.call-start = ((), (), s32[]{:S(2)}) async-start(), calls=%async_computation.1 | async-start | bytes 1048576 | tf_op jit(solution)/shard_map/psum | solution.py:60
  98.0 82.4 %copy-start.3 = (bf16[2,256,512]{2,1,0:T(8,128)(2,1)S(1)}, bf16[2,256,512]{2,1,0:T(8,128)(2,1)}, u32[]{:S(2)}) copy-start(bf16[2,256,512]{2,1,0:T(8,128)(2,1)} %param.13) | copy-start | bytes 1572868
  193.5 345.4 %all-reduce.9.cloned.1.call-start = ((), (), s32[]{:S(2)}) async-start(), calls=%async_computation.2 | async-start | bytes 1048576 | tf_op jit(solution)/shard_map/psum | solution.py:52
  194.9 47.8 %collective-permute-start.4 = (bf16[1024,1,128]{2,0,1:T(8,128)(2,1)}, bf16[1024,1,128]{2,0,1:T(8,128)(2,1)}, u32[]{:S(2)}, u32[]{:S(2)}) collective-permute-start(bf16[1024,1,128]{2,0,1:T(8,128)(2,1)} %fusion.26), channel_id=1, source_target_pairs={{0,1},{1,0},{2,3},{3,2},{4,5},{5,4},{6,7},{7,6},{8,9},{9,8},{10,11... | collective-permute-start | bytes 786440 | tf_op jit(solution)/shard_map/ppermute | solution.py:13
  194.9 47.8 %collective-permute-start.5 = (bf16[1024,1,128]{2,0,1:T(8,128)(2,1)}, bf16[1024,1,128]{2,0,1:T(8,128)(2,1)}, u32[]{:S(2)}, u32[]{:S(2)}) collective-permute-start(bf16[1024,1,128]{2,0,1:T(8,128)(2,1)} %fusion.27), channel_id=1, source_target_pairs={{0,2},{1,3},{2,0},{3,1},{4,6},{5,7},{6,4},{7,5},{8,10},{9,11},{10,... | collective-permute-start | bytes 786440 | tf_op jit(solution)/shard_map/ppermute | solution.py:13
  195.9 46.7 %collective-permute-start.6 = (bf16[1024,1,128]{2,0,1:T(8,128)(2,1)S(1)}, bf16[1024,1,128]{2,0,1:T(8,128)(2,1)}, u32[]{:S(2)}, u32[]{:S(2)}) collective-permute-start(bf16[1024,1,128]{2,0,1:T(8,128)(2,1)S(1)} %fusion.28), channel_id=1, source_target_pairs={{0,4},{1,5},{2,6},{3,7},{4,0},{5,1},{6,2},{7,3},{8,12},{9,13},{10,... | collective-permute-start | bytes 786440 | tf_op jit(solution)/shard_map/ppermute | solution.py:13
  195.9 46.7 %collective-permute-start.7 = (bf16[1024,1,128]{2,0,1:T(8,128)(2,1)}, bf16[1024,1,128]{2,0,1:T(8,128)(2,1)}, u32[]{:S(2)}, u32[]{:S(2)}) collective-permute-start(bf16[1024,1,128]{2,0,1:T(8,128)(2,1)} %fusion.29), channel_id=1, source_target_pairs={{0,8},{1,9},{2,10},{3,11},{4,12},{5,13},{6,14},{7,15},{8,0},{9,1},... | collective-permute-start | bytes 786440 | tf_op jit(solution)/shard_map/ppermute | solution.py:13
  361.2 10.5 %collective-permute-start.10 = (bf16[1024,1,128]{2,0,1:T(8,128)(2,1)S(1)}, bf16[1024,1,128]{2,0,1:T(8,128)(2,1)S(1)}, u32[]{:S(2)}, u32[]{:S(2)}) collective-permute-start(bf16[1024,1,128]{2,0,1:T(8,128)(2,1)S(1)} %bitcast.286), channel_id=1, source_target_pairs={{0,4},{1,5},{2,6},{3,7},{4,0},{5,1},{6,2},{7,3},{8,12},{9,13},{10,... | collective-permute-start | bytes 786440 | tf_op jit(solution)/shard_map/ppermute | solution.py:13
  361.3 12.1 %collective-permute-start.9 = (bf16[1024,1,128]{2,0,1:T(8,128)(2,1)S(1)}, bf16[1024,1,128]{2,0,1:T(8,128)(2,1)S(1)}, u32[]{:S(2)}, u32[]{:S(2)}) collective-permute-start(bf16[1024,1,128]{2,0,1:T(8,128)(2,1)S(1)} %bitcast.287), channel_id=1, source_target_pairs={{0,2},{1,3},{2,0},{3,1},{4,6},{5,7},{6,4},{7,5},{8,10},{9,11},{10,... | collective-permute-start | bytes 786440 | tf_op jit(solution)/shard_map/ppermute | solution.py:13
  361.6 13.8 %collective-permute-start.8 = (bf16[1024,1,128]{2,0,1:T(8,128)(2,1)S(1)}, bf16[1024,1,128]{2,0,1:T(8,128)(2,1)S(1)}, u32[]{:S(2)}, u32[]{:S(2)}) collective-permute-start(bf16[1024,1,128]{2,0,1:T(8,128)(2,1)S(1)} %bitcast.288), channel_id=1, source_target_pairs={{0,1},{1,0},{2,3},{3,2},{4,5},{5,4},{6,7},{7,6},{8,9},{9,8},{10,11... | collective-permute-start | bytes 786440 | tf_op jit(solution)/shard_map/ppermute | solution.py:13
  362.5 178.2 %collective-permute-start.11 = (bf16[1024,1,128]{2,0,1:T(8,128)(2,1)S(1)}, bf16[1024,1,128]{2,0,1:T(8,128)(2,1)S(1)}, u32[]{:S(2)}, u32[]{:S(2)}) collective-permute-start(bf16[1024,1,128]{2,0,1:T(8,128)(2,1)S(1)} %bitcast.289), channel_id=1, source_target_pairs={{0,8},{1,9},{2,10},{3,11},{4,12},{5,13},{6,14},{7,15},{8,0},{9,1},... | collective-permute-start | bytes 786440 | tf_op jit(solution)/shard_map/ppermute | solution.py:13
  369.8 345.9 %all-reduce.11.cloned.1.call-start = ((), (), s32[]{:S(2)}) async-start(), calls=%async_computation.3 | async-start | bytes 1048576 | tf_op jit(solution)/shard_map/psum | solution.py:60
  373.5 165.5 %copy-start.4 = (bf16[2,256,512]{2,1,0:T(8,128)(2,1)S(1)}, bf16[2,256,512]{2,1,0:T(8,128)(2,1)}, u32[]{:S(2)}) copy-start(bf16[2,256,512]{2,1,0:T(8,128)(2,1)} %param.13) | copy-start | bytes 1572868
  550.2 165.5 %copy-start.7 = (bf16[2,256,128]{2,1,0:T(8,128)(2,1)S(1)}, bf16[2,256,128]{2,1,0:T(8,128)(2,1)}, u32[]{:S(2)}) copy-start(bf16[2,256,128]{2,1,0:T(8,128)(2,1)} %param.15) | copy-start | bytes 393220
  551.3 14.6 %collective-permute-start.12 = (bf16[1024,1,128]{2,0,1:T(8,128)(2,1)S(1)}, bf16[1024,1,128]{2,0,1:T(8,128)(2,1)S(1)}, u32[]{:S(2)}, u32[]{:S(2)}) collective-permute-start(bf16[1024,1,128]{2,0,1:T(8,128)(2,1)S(1)} %fusion.30), channel_id=1, source_target_pairs={{0,1},{1,0},{2,3},{3,2},{4,5},{5,4},{6,7},{7,6},{8,9},{9,8},{10,11... | collective-permute-start | bytes 786440 | tf_op jit(solution)/shard_map/ppermute | solution.py:13
  551.4 14.5 %collective-permute-start.13 = (bf16[1024,1,128]{2,0,1:T(8,128)(2,1)S(1)}, bf16[1024,1,128]{2,0,1:T(8,128)(2,1)S(1)}, u32[]{:S(2)}, u32[]{:S(2)}) collective-permute-start(bf16[1024,1,128]{2,0,1:T(8,128)(2,1)S(1)} %fusion.31), channel_id=1, source_target_pairs={{0,2},{1,3},{2,0},{3,1},{4,6},{5,7},{6,4},{7,5},{8,10},{9,11},{10,... | collective-permute-start | bytes 786440 | tf_op jit(solution)/shard_map/ppermute | solution.py:13
  552.5 13.5 %collective-permute-start.14 = (bf16[1024,1,128]{2,0,1:T(8,128)(2,1)S(1)}, bf16[1024,1,128]{2,0,1:T(8,128)(2,1)S(1)}, u32[]{:S(2)}, u32[]{:S(2)}) collective-permute-start(bf16[1024,1,128]{2,0,1:T(8,128)(2,1)S(1)} %fusion.32), channel_id=1, source_target_pairs={{0,4},{1,5},{2,6},{3,7},{4,0},{5,1},{6,2},{7,3},{8,12},{9,13},{10,... | collective-permute-start | bytes 786440 | tf_op jit(solution)/shard_map/ppermute | solution.py:13
  552.5 14.9 %collective-permute-start.15 = (bf16[1024,1,128]{2,0,1:T(8,128)(2,1)S(1)}, bf16[1024,1,128]{2,0,1:T(8,128)(2,1)}, u32[]{:S(2)}, u32[]{:S(2)}) collective-permute-start(bf16[1024,1,128]{2,0,1:T(8,128)(2,1)S(1)} %fusion.33), channel_id=1, source_target_pairs={{0,8},{1,9},{2,10},{3,11},{4,12},{5,13},{6,14},{7,15},{8,0},{9,1},... | collective-permute-start | bytes 786440 | tf_op jit(solution)/shard_map/ppermute | solution.py:13
  (9 other events, 25.4 us)
Sparse Core Ops, SparseCore 0:
  23.2 157.1 all-reduce.4
  193.7 165.5 all-reduce.6
  370.0 168.9 all-reduce.8
  550.3 165.3 all-reduce.10
where the time goes:
time: 735 us; the launch traced here: 725 us
  waiting for transfers between devices  513 us (70%)
  blocking collectives  100 us (14%)
  matrix products  49.7 us (7%)
  starting transfers between devices  32.7 us (4%)
  between operations  23 us (3%)
    psum x2, waiting for transfers between devices, per_device(): latent_back = lax.psum(partial_back.astype(jnp.bfloat16), 'feat')  265 us
    psum x2, waiting for transfers between devices, per_device(): latent = lax.psum(partial_latent.astype(jnp.bfloat16), 'feat')  241 us
    all_gather x2, blocking collectives, per_device(): lax.all_gather(down_blocks[layer_num], 'tok', axis=3, tiled=True)  53.2 us
    all_gather x2, blocking collectives, per_device(): lax.all_gather(up_blocks[layer_num], 'tok', axis=3, tiled=True)  46.9 us
    dot_general x20, matrix products, block_product(): jnp.einsum('tjd,jdh->tjh', left, right, preferred_element_type=jnp.float32)  36.5 us
    ppermute x16, starting transfers between devices, from_partner(): lax.ppermute(value, axis, [(i, i ^ 1 << distance) for i in range(lax.axis...  32.5 us
  transfers between devices with their start and end apart: 20, of which 6 were waited for; matrix products, arithmetic and copies ran while one was open for 4% of the time, Pallas kernels for 0%

commit v1 on v0

v1 whole, which is shorter than its diff:
```python
import jax
import jax.numpy as jnp
from jax import lax
from jax.sharding import Mesh, PartitionSpec as P

BF = jnp.bfloat16
F32 = jnp.float32
TOK = ("zl", "y1", "y0", "core")
FEAT = ("x1", "x0", "zh1", "zh0")
SWAPPED = ("zl", "core", "zh1", "zh0")
BIT_AXES = ("zl", "core", "x0", "x1")
CUBE = ("x1", "x0", "zl")


def pair(value, axis):
    return lax.ppermute(value, axis, [(0, 1), (1, 0)])


def bits(i):
    return i >> 3 & 1, i >> 2 & 1, i >> 1 & 1, i & 1


def index(zl, core, zh1, zh0):
    return zl << 3 | core << 2 | zh1 << 1 | zh0


def swap(value, k0=0, k1=0):
    perm = []
    for dst in range(16):
        zl, core, zh1, zh0 = bits(dst)
        perm.append((index(zh0 ^ k0, zh1 ^ k1, core, zl), dst))
    return lax.ppermute(value, SWAPPED, perm)


def swap_copied(value):
    perm = []
    for dst in range(16):
        zl, core, zh1, zh0 = bits(dst)
        perm.append((index(zh0 ^ zh1 ^ core, zh1, core, zl), dst))
    return lax.ppermute(value, SWAPPED, perm)


def gather_planes(shard):
    zh0, zh1 = lax.axis_index("zh0"), lax.axis_index("zh1")
    out = jnp.zeros((2, 2) + shard.shape, shard.dtype)
    zero = jnp.int32(0)
    for k0 in range(2):
        for k1 in range(2):
            got = swap(shard, k0, k1)
            out = lax.dynamic_update_slice(
                out, got[None, None], (zh0 ^ k0, zh1 ^ k1) + (zero,) * shard.ndim
            )
    return out


def gather_y(part):
    y = lax.axis_index(("y1", "y0"))
    zero = jnp.int32(0)
    out = jnp.zeros((4,) + part.shape, part.dtype)
    out = lax.dynamic_update_slice(out, part[None], (y,) + (zero,) * part.ndim)
    for step in range(1, 4):
        got = lax.ppermute(part, ("y1", "y0"), [(i, (i + step) % 4) for i in range(4)])
        out = lax.dynamic_update_slice(
            out, got[None], ((y - step) % 4,) + (zero,) * part.ndim
        )
    return out


def all_sum(part):
    core = lax.axis_index("core")
    half = part.shape[0] // 2
    mine = lax.dynamic_slice_in_dim(part, core * half, half, 0)
    other = lax.dynamic_slice_in_dim(part, (1 - core) * half, half, 0)
    mine = (mine.astype(F32) + pair(other, "core").astype(F32)).astype(BF)
    mine = mine.reshape(8, half // 8, part.shape[1])
    terms = lax.all_to_all(mine, CUBE, 0, 0)
    total = jnp.sum(terms.astype(F32), axis=0).astype(BF)
    mine = lax.all_to_all(jnp.broadcast_to(total[None], mine.shape), CUBE, 0, 0)
    mine = mine.reshape(half, part.shape[1])
    other = pair(mine, "core")
    first = core == 0
    return jnp.concatenate(
        [jnp.where(first, mine, other), jnp.where(first, other, mine)], axis=0
    )


def per_device(tokens, level_bits, up_blocks, down_blocks, rank_in, rank_up, rank_down, rank_out):
    layers = level_bits.shape[0]
    block = (
        lax.axis_index("x1") * 8
        + lax.axis_index("x0") * 4
        + lax.axis_index("core") * 2
        + lax.axis_index("zl")
    )
    width = tokens.shape[1]
    x = swap(tokens)
    up_shard = up_blocks[:, 0].transpose(0, 1, 3, 2).reshape(layers, 160, 128)
    down_shard = (
        down_blocks[:, 0].reshape(layers, 5, 4, 128, 8).transpose(0, 1, 2, 4, 3)
    ).reshape(layers, 160, 128)
    shard = jnp.concatenate([up_shard, down_shard], axis=1)
    planes = gather_planes(shard)
    rank_up, rank_down, rank_out = (swap_copied(v) for v in (rank_up, rank_down, rank_out))
    for layer in range(layers):
        got = gather_y(planes[:, :, layer])
        got = got.transpose(1, 0, 2, 3, 4)
        up_t = got[:, :, :, :160].reshape(16, 5, 32, 128).transpose(1, 0, 2, 3).reshape(5, 512, 128)
        down_t = (
            got[:, :, :, 160:].reshape(16, 5, 4, 8, 128).transpose(1, 0, 3, 2, 4)
        ).reshape(5, 128, 512)
        row = level_bits[layer]
        places = [
            1 + jnp.sum(jnp.where(row == bit, jnp.arange(4, dtype=jnp.int32), 0))
            for bit in range(4)
        ]
        order = jnp.stack([jnp.int32(0)] + places)
        up_t = jnp.take(up_t, order, axis=0)
        down_t = jnp.take(down_t, order, axis=0).reshape(640, 512)
        up_w = jnp.concatenate([up_t[i] for i in range(5)], axis=1)

        rows_in = lax.dynamic_slice_in_dim(rank_in[layer], block * width, width, 0)
        part = jnp.dot(x, rows_in, preferred_element_type=F32).astype(BF)
        latent = all_sum(part)
        partners = [pair(x, axis) for axis in BIT_AXES]
        pre = lax.dot_general(
            jnp.concatenate([x] + partners, axis=1), up_w, (((1,), (1,)), ((), ())),
            preferred_element_type=F32,
        ) + jnp.dot(latent, rank_up[layer], preferred_element_type=F32)
        hidden = jax.nn.gelu(pre, approximate=False).astype(BF)
        back = all_sum(
            jnp.dot(hidden, rank_down[layer], preferred_element_type=F32).astype(BF)
        )
        terms = lax.dot_general(
            hidden, down_t, (((1,), (1,)), ((), ())), preferred_element_type=F32
        )
        result = terms[:, :width] + jnp.dot(back, rank_out[layer], preferred_element_type=F32)
        for bit, axis in enumerate(BIT_AXES):
            term = terms[:, (1 + bit) * width : (2 + bit) * width].astype(BF)
            result = result + pair(term, axis).astype(F32)
        x = (x.astype(F32) + result).astype(BF)
    return swap(x)


def solution(mesh):
    fine = Mesh(mesh.devices.reshape((2,) * 8), TOK + FEAT)
    return jax.shard_map(
        per_device,
        mesh=fine,
        in_specs=(
            P(TOK, FEAT),
            P(),
            P(None, FEAT, None, None, TOK),
            P(None, FEAT, None, None, TOK),
            P(),
            P(None, None, FEAT),
            P(None, FEAT, None),
            P(None, None, FEAT),
        ),
        out_specs=P(TOK, FEAT),
        check_vma=False,
    )
```

time: 735 us -> 277 us (0.38); the launches traced: 725 us -> 275 us
  waiting for transfers between devices: 513 us -> 92 us
  blocking collectives: 100 us -> 0 us
  starting transfers between devices: 32.7 us -> 110 us
  local copies, waits for them, and re-layouts: 4.98 us -> 32.6 us
  matrix products: 49.7 us -> 26 us
  between operations: 23 us -> 5.82 us
  other arithmetic: 0.78 us -> 8.32 us
    psum x4 -> x0, waiting for transfers between devices: 506 us -> none  [the longest x2 265 us: per_device(): latent_back = lax.psum(partial_back.astype(jnp.bfloat16), 'feat')]
    all_gather x4 -> x0, blocking collectives: 100 us -> none  [the longest x2 53.2 us: per_device(): lax.all_gather(down_blocks[layer_num], 'tok', axis=3, tiled=True)]
    ppermute x16 -> x39, waiting for transfers between devices: 7.67 us -> 64.9 us  [the longest x24 25.8 us: pair(): return lax.ppermute(value, axis, [(0, 1), (1, 0)])]
    ppermute x16 -> x39, starting transfers between devices: 32.5 us -> 81.7 us  [the longest x24 32.3 us: pair(): return lax.ppermute(value, axis, [(0, 1), (1, 0)])]
    all_to_all x0 -> x8, starting transfers between devices: none -> 28.2 us  [the longest x4 14.3 us: all_sum(): mine = lax.all_to_all(jnp.broadcast_to(total[None], mine.shape), CUBE, 0, 0)]
    all_to_all x0 -> x8, waiting for transfers between devices: none -> 27.1 us  [the longest x4 22.7 us: all_sum(): terms = lax.all_to_all(mine, CUBE, 0, 0)]
    dot_general x28 -> x12, matrix products: 49.7 us -> 26 us  [the longest x2 10.7 us: per_device(): lax.dot_general(jnp.concatenate([x] + partners, axis=1), up_w, (((1,), (1...]
    unnamed x26 -> x40, local copies, waits for them, and re-layouts: 1.57 us -> 11.9 us
  transfers between devices with their start and end apart: 20 -> 47, of which waited for: 6 -> 22; matrix products, arithmetic and copies ran while one was open for 4% -> 16% of each run, Pallas kernels for 0% -> 0%
where the time goes in v1:
time: 277 us; the launch traced here: 275 us
  starting transfers between devices  110 us (40%)
  waiting for transfers between devices  92 us (33%)
  local copies, waits for them, and re-layouts  32.6 us (12%)
  matrix products  26 us (9%)
  other arithmetic  8.32 us (3%)
  between operations  5.82 us (2%)
    ppermute x24, starting transfers between devices, pair(): return lax.ppermute(value, axis, [(0, 1), (1, 0)])  32.3 us
    ppermute x24, waiting for transfers between devices, pair(): return lax.ppermute(value, axis, [(0, 1), (1, 0)])  25.8 us
    ppermute x6, starting transfers between devices, swap(): return lax.ppermute(value, SWAPPED, perm)  24.1 us
    all_to_all x4, waiting for transfers between devices, all_sum(): terms = lax.all_to_all(mine, CUBE, 0, 0)  22.7 us
    ppermute x6, waiting for transfers between devices, gather_y(): lax.ppermute(part, ('y1', 'y0'), [(i, (i + step) % 4) for i in range(4)])  22.5 us
    ppermute x6, starting transfers between devices, gather_y(): lax.ppermute(part, ('y1', 'y0'), [(i, (i + step) % 4) for i in range(4)])  15.3 us
    all_to_all x4, starting transfers between devices, all_sum(): mine = lax.all_to_all(jnp.broadcast_to(total[None], mine.shape), CUBE, 0, 0)  14.3 us
    all_to_all x4, starting transfers between devices, all_sum(): terms = lax.all_to_all(mine, CUBE, 0, 0)  14 us
  transfers between devices with their start and end apart: 47, of which 22 were waited for; matrix products, arithmetic and copies ran while one was open for 16% of the time, Pallas kernels for 0%

profile of v1, /device:TPU:1, one launch (start us, length us, event | category | flops | bytes accessed | tf_op | source)
XLA Modules:
  0.0 274.7 jit_solution(17006402128999526239)
XLA Ops:
  0.9 10.2 %collective-permute-start.5 = (bf16[2,320,128]{2,1,0:T(8,128)(2,1)S(1)}, bf16[2,320,128]{2,1,0:T(8,128)(2,1)S(1)}, u32[]{:S(2)}, u32[]{:S(2)}) collective-permute-start(bf16[2,320,128]{2,1,0:T(8,128)(2,1)S(1)} %pad_maximum_fusion), channel_id=1, source_target_pairs={{0,0},{128,1},{16,2},{144,3},{2,16},{130,17},{18,18},{146,19},{1,1... | collective-permute-start | bytes 491528 | tf_op jit(solution)/shard_map/ppermute | solution.py:32
  15.7 6.1 %collective-permute-start = (bf16[1024,128]{0,1:T(8,128)(2,1)S(1)}, bf16[1024,128]{0,1:T(8,128)(2,1)S(1)}, u32[]{:S(2)}, u32[]{:S(2)}) collective-permute-start(bf16[1024,128]{0,1:T(8,128)(2,1)S(1)} %copy.14), channel_id=1, source_target_pairs={{0,0},{128,1},{16,2},{144,3},{2,16},{130,17},{18,18},{146,19},{1,1... | collective-permute-start | bytes 786440 | tf_op jit(solution)/shard_map/ppermute | solution.py:32
  34.0 6.2 %collective-permute-start.15 = (bf16[2,512,256]{2,1,0:T(8,128)(2,1)}, bf16[2,512,256]{2,1,0:T(8,128)(2,1)}, u32[]{:S(2)}, u32[]{:S(2)}) collective-permute-start(bf16[2,512,256]{2,1,0:T(8,128)(2,1)} %param.18), channel_id=1, source_target_pairs={{0,0},{128,1},{144,2},{16,3},{130,16},{2,17},{18,18},{146,19},{1,1... | collective-permute-start | bytes 1572872 | tf_op jit(solution)/shard_map/ppermute | solution.py:40
  46.9 5.3 %collective-permute-done.27 = bf16[2,2,320,128]{3,2,1,0:T(8,128)(2,1)S(1)} collective-permute-done((bf16[2,2,320,128]{3,2,1,0:T(8,128)(2,1)S(1)}, bf16[2,2,320,128]{3,2,1,0:T(8,128)(2,1)S(1)}, u32[]{:S(2)}, u32[]{:S(2)}) %collective-permute-start.27) | collective-permute-done | bytes 327712 | tf_op jit(solution)/shard_map/ppermute | solution.py:62
  52.1 8.0 %collective-permute-start.10 = (bf16[2,2,320,128]{3,2,1,0:T(8,128)(2,1)S(1)}, bf16[2,2,320,128]{3,2,1,0:T(8,128)(2,1)S(1)}, u32[]{:S(2)}, u32[]{:S(2)}) collective-permute-start(bf16[2,2,320,128]{3,2,1,0:T(8,128)(2,1)S(1)} %get-tuple-element.30), channel_id=1, source_target_pairs={{0,64},{32,96},{64,0},{96,32},{1,65},{33,97},{65,1},{97,33},{2,66}... | collective-permute-start | bytes 983048 | tf_op jit(solution)/shard_map/ppermute | solution.py:62
  60.2 4.1 %collective-permute-done.9 = bf16[2,2,320,128]{3,2,1,0:T(8,128)(2,1)S(1)} collective-permute-done((bf16[2,2,320,128]{3,2,1,0:T(8,128)(2,1)S(1)}, bf16[2,2,320,128]{3,2,1,0:T(8,128)(2,1)S(1)}, u32[]{:S(2)}, u32[]{:S(2)}) %collective-permute-start.9) | collective-permute-done | bytes 327712 | tf_op jit(solution)/shard_map/ppermute | solution.py:62
  67.6 4.9 %collective-permute-done.10 = bf16[2,2,320,128]{3,2,1,0:T(8,128)(2,1)S(1)} collective-permute-done((bf16[2,2,320,128]{3,2,1,0:T(8,128)(2,1)S(1)}, bf16[2,2,320,128]{3,2,1,0:T(8,128)(2,1)S(1)}, u32[]{:S(2)}, u32[]{:S(2)}) %collective-permute-start.10) | collective-permute-done | bytes 327712 | tf_op jit(solution)/shard_map/ppermute | solution.py:62
  74.2 6.6 %collective-permute-done.29 = bf16[2,2,320,128]{3,2,1,0:T(8,128)(2,1)S(1)} collective-permute-done((bf16[2,2,320,128]{3,2,1,0:T(8,128)(2,1)S(1)}, bf16[2,2,320,128]{3,2,1,0:T(8,128)(2,1)S(1)}, u32[]{:S(2)}, u32[]{:S(2)}) %collective-permute-start.29) | collective-permute-done | bytes 327712 | tf_op jit(solution)/shard_map/ppermute | solution.py:62
  87.2 3.7 %all-to-all-start = ((bf16[8,64,256]{2,1,0:T(8,128)(2,1)}), bf16[8,64,256]{2,1,0:T(8,128)(2,1)S(1)}, u32[]{:S(2)}, u32[]{:S(2)}) async-start(bf16[8,64,256]{2,1,0:T(8,128)(2,1)} %bitcast.41), calls=%async_computation | async-start | bytes 524288 | tf_op jit(solution)/shard_map/all_to_all | solution.py:76
  92.3 5.2 %all-to-all-done = bf16[8,64,256]{2,1,0:T(8,128)(2,1)S(1)} async-done(((bf16[8,64,256]{2,1,0:T(8,128)(2,1)}), bf16[8,64,256]{2,1,0:T(8,128)(2,1)S(1)}, u32[]{:S(2)}, u32[]{:S(2)}) %all-to-all-start) | async-done | bytes 262176 | tf_op jit(solution)/shard_map/all_to_all | solution.py:76
  98.2 3.4 %all-to-all-start.1 = ((bf16[8,64,256]{2,1,0:T(8,128)(2,1)}), bf16[8,64,256]{2,1,0:T(8,128)(2,1)S(1)}, u32[]{:S(2)}, u32[]{:S(2)}) async-start(bf16[8,64,256]{2,1,0:T(8,128)(2,1)} %broadcast_in_dim.92), calls=%async_computation.1 | async-start | bytes 524288 | tf_op jit(solution)/shard_map/all_to_all | solution.py:78
  116.3 5.3 %fusion.2 = bf16[1024,512]{1,0:T(8,128)(2,1)S(1)} fusion(f32[1024,512]{1,0:T(8,128)S(1)} %fusion.28, bf16[1024,640]{0,1:T(8,128)(2,1)S(1)} %copy-done.9, bf16[512,640]{1,0:T(8,128)(2,1)S(1)} %copy-done.10), kind=kOutput, calls=%fused_computation.8 | convolution fusion | flops 705691648 | bytes 5111808 | tf_op jit(solution)/shard_map/dot_general | solution.py:125
  131.7 5.7 %all-to-all-done.2 = bf16[8,64,256]{2,1,0:T(8,128)(2,1)S(1)} async-done(((bf16[8,64,256]{2,1,0:T(8,128)(2,1)}), bf16[8,64,256]{2,1,0:T(8,128)(2,1)S(1)}, u32[]{:S(2)}, u32[]{:S(2)}) %all-to-all-start.2) | async-done | bytes 262176 | tf_op jit(solution)/shard_map/all_to_all | solution.py:76
  138.1 4.1 %all-to-all-start.3 = ((bf16[8,64,256]{2,1,0:T(8,128)(2,1)}), bf16[8,64,256]{2,1,0:T(8,128)(2,1)}, u32[]{:S(2)}, u32[]{:S(2)}) async-start(bf16[8,64,256]{2,1,0:T(8,128)(2,1)} %broadcast_in_dim.93), calls=%async_computation.3 | async-start | bytes 524288 | tf_op jit(solution)/shard_map/all_to_all | solution.py:78
  160.9 6.5 %collective-permute-done.18 = bf16[2,256,128]{2,1,0:T(8,128)(2,1)S(1)} collective-permute-done((bf16[2,256,128]{2,1,0:T(8,128)(2,1)}, bf16[2,256,128]{2,1,0:T(8,128)(2,1)S(1)}, u32[]{:S(2)}, u32[]{:S(2)}) %collective-permute-start.18) | collective-permute-done | bytes 131104 | tf_op jit(solution)/shard_map/ppermute | solution.py:40
  178.6 5.5 %all-to-all-done.4 = bf16[8,64,256]{2,1,0:T(8,128)(2,1)S(1)} async-done(((bf16[8,64,256]{2,1,0:T(8,128)(2,1)}), bf16[8,64,256]{2,1,0:T(8,128)(2,1)S(1)}, u32[]{:S(2)}, u32[]{:S(2)}) %all-to-all-start.4) | async-done | bytes 262176 | tf_op jit(solution)/shard_map/all_to_all | solution.py:76
  200.0 7.1 %collective-permute-done.26 = bf16[1024,128]{0,1:T(8,128)(2,1)S(1)} collective-permute-done((bf16[1024,128]{0,1:T(8,128)(2,1)S(1)}, bf16[1024,128]{0,1:T(8,128)(2,1)S(1)}, u32[]{:S(2)}, u32[]{:S(2)}) %collective-permute-start.26) | collective-permute-done | bytes 262176 | tf_op jit(solution)/shard_map/ppermute | solution.py:16
  209.4 5.4 %fusion.5 = bf16[1024,512]{1,0:T(8,128)(2,1)S(1)} fusion(f32[1024,512]{1,0:T(8,128)S(1)} %fusion.35, bf16[1024,640]{0,1:T(8,128)(2,1)S(1)} %copy-done.8, bf16[512,640]{1,0:T(8,128)(2,1)S(1)} %fusion.43), kind=kOutput, calls=%fused_computation.11 | convolution fusion | flops 705691648 | bytes 5111808 | tf_op jit(solution)/shard_map/dot_general | solution.py:125
  224.1 6.3 %all-to-all-done.6 = bf16[8,64,256]{2,1,0:T(8,128)(2,1)S(1)} async-done(((bf16[8,64,256]{2,1,0:T(8,128)(2,1)}), bf16[8,64,256]{2,1,0:T(8,128)(2,1)S(1)}, u32[]{:S(2)}, u32[]{:S(2)}) %all-to-all-start.6) | async-done | bytes 262176 | tf_op jit(solution)/shard_map/all_to_all | solution.py:76
  231.2 3.4 %all-to-all-start.7 = ((bf16[8,64,256]{2,1,0:T(8,128)(2,1)}), bf16[8,64,256]{2,1,0:T(8,128)(2,1)S(1)}, u32[]{:S(2)}, u32[]{:S(2)}) async-start(bf16[8,64,256]{2,1,0:T(8,128)(2,1)} %broadcast_in_dim.98), calls=%async_computation.7 | async-start | bytes 524288 | tf_op jit(solution)/shard_map/all_to_all | solution.py:78
  247.3 5.0 %collective-permute-done.34 = bf16[1024,128]{0,1:T(8,128)(2,1)S(1)} collective-permute-done((bf16[1024,128]{0,1:T(8,128)(2,1)S(1)}, bf16[1024,128]{0,1:T(8,128)(2,1)S(1)}, u32[]{:S(2)}, u32[]{:S(2)}) %collective-permute-start.34) | collective-permute-done | bytes 262176 | tf_op jit(solution)/shard_map/ppermute | solution.py:16
  252.9 6.2 %collective-permute-done.37 = bf16[1024,128]{0,1:T(8,128)(2,1)S(1)} collective-permute-done((bf16[1024,128]{0,1:T(8,128)(2,1)S(1)}, bf16[1024,128]{0,1:T(8,128)(2,1)S(1)}, u32[]{:S(2)}, u32[]{:S(2)}) %collective-permute-start.37) | collective-permute-done | bytes 262176 | tf_op jit(solution)/shard_map/ppermute | solution.py:16
  259.5 4.3 %collective-permute-start.38 = (bf16[1024,128]{0,1:T(8,128)(2,1)S(1)}, bf16[1024,128]{0,1:T(8,128)(2,1)S(1)}, u32[]{:S(2)}, u32[]{:S(2)}) collective-permute-start(bf16[1024,128]{0,1:T(8,128)(2,1)S(1)} %add_convert_fusion), channel_id=1, source_target_pairs={{0,0},{128,1},{16,2},{144,3},{2,16},{130,17},{18,18},{146,19},{1,1... | collective-permute-start | bytes 786440 | tf_op jit(solution)/shard_map/ppermute | solution.py:32
  263.8 10.1 %collective-permute-done.38 = bf16[1024,128]{0,1:T(8,128)(2,1)S(1)} collective-permute-done((bf16[1024,128]{0,1:T(8,128)(2,1)S(1)}, bf16[1024,128]{0,1:T(8,128)(2,1)S(1)}, u32[]{:S(2)}, u32[]{:S(2)}) %collective-permute-start.38) | collective-permute-done | bytes 262176 | tf_op jit(solution)/shard_map/ppermute | solution.py:32
  (188 shorter events, 130.4 us)
Async XLA Ops:
  0.9 31.0 %collective-permute-start.5 = (bf16[2,320,128]{2,1,0:T(8,128)(2,1)S(1)}, bf16[2,320,128]{2,1,0:T(8,128)(2,1)S(1)}, u32[]{:S(2)}, u32[]{:S(2)}) collective-permute-start(bf16[2,320,128]{2,1,0:T(8,128)(2,1)S(1)} %pad_maximum_fusion), channel_id=1, source_target_pairs={{0,0},{128,1},{16,2},{144,3},{2,16},{130,17},{18,18},{146,19},{1,1... | collective-permute-start | bytes 491528 | tf_op jit(solution)/shard_map/ppermute | solution.py:32
  11.2 22.8 %collective-permute-start.6 = (bf16[2,320,128]{2,1,0:T(8,128)(2,1)S(1)}, bf16[2,320,128]{2,1,0:T(8,128)(2,1)S(1)}, u32[]{:S(2)}, u32[]{:S(2)}) collective-permute-start(bf16[2,320,128]{2,1,0:T(8,128)(2,1)S(1)} %pad_maximum_fusion), channel_id=1, source_target_pairs={{16,0},{144,1},{0,2},{128,3},{18,16},{146,17},{2,18},{130,19},{17,... | collective-permute-start | bytes 491528 | tf_op jit(solution)/shard_map/ppermute | solution.py:32
  11.3 29.0 %collective-permute-start.7 = (bf16[2,320,128]{2,1,0:T(8,128)(2,1)S(1)}, bf16[2,320,128]{2,1,0:T(8,128)(2,1)S(1)}, u32[]{:S(2)}, u32[]{:S(2)}) collective-permute-start(bf16[2,320,128]{2,1,0:T(8,128)(2,1)S(1)} %pad_maximum_fusion), channel_id=1, source_target_pairs={{128,0},{0,1},{144,2},{16,3},{130,16},{2,17},{146,18},{18,19},{129... | collective-permute-start | bytes 491528 | tf_op jit(solution)/shard_map/ppermute | solution.py:32
  11.5 28.7 %collective-permute-start.8 = (bf16[2,320,128]{2,1,0:T(8,128)(2,1)S(1)}, bf16[2,320,128]{2,1,0:T(8,128)(2,1)S(1)}, u32[]{:S(2)}, u32[]{:S(2)}) collective-permute-start(bf16[2,320,128]{2,1,0:T(8,128)(2,1)S(1)} %pad_maximum_fusion), channel_id=1, source_target_pairs={{144,0},{16,1},{128,2},{0,3},{146,16},{18,17},{130,18},{2,19},{145... | collective-permute-start | bytes 491528 | tf_op jit(solution)/shard_map/ppermute | solution.py:32
  15.7 29.3 %collective-permute-start = (bf16[1024,128]{0,1:T(8,128)(2,1)S(1)}, bf16[1024,128]{0,1:T(8,128)(2,1)S(1)}, u32[]{:S(2)}, u32[]{:S(2)}) collective-permute-start(bf16[1024,128]{0,1:T(8,128)(2,1)S(1)} %copy.14), channel_id=1, source_target_pairs={{0,0},{128,1},{16,2},{144,3},{2,16},{130,17},{18,18},{146,19},{1,1... | collective-permute-start | bytes 786440 | tf_op jit(solution)/shard_map/ppermute | solution.py:32
  31.9 82.8 %collective-permute-start.14 = (bf16[2,256,512]{2,1,0:T(8,128)(2,1)}, bf16[2,256,512]{2,1,0:T(8,128)(2,1)}, u32[]{:S(2)}, u32[]{:S(2)}) collective-permute-start(bf16[2,256,512]{2,1,0:T(8,128)(2,1)} %param.17), channel_id=1, source_target_pairs={{0,0},{128,1},{144,2},{16,3},{130,16},{2,17},{18,18},{146,19},{1,1... | collective-permute-start | bytes 1572872 | tf_op jit(solution)/shard_map/ppermute | solution.py:40
  34.0 87.6 %collective-permute-start.15 = (bf16[2,512,256]{2,1,0:T(8,128)(2,1)}, bf16[2,512,256]{2,1,0:T(8,128)(2,1)}, u32[]{:S(2)}, u32[]{:S(2)}) collective-permute-start(bf16[2,512,256]{2,1,0:T(8,128)(2,1)} %param.18), channel_id=1, source_target_pairs={{0,0},{128,1},{144,2},{16,3},{130,16},{2,17},{18,18},{146,19},{1,1... | collective-permute-start | bytes 1572872 | tf_op jit(solution)/shard_map/ppermute | solution.py:40
  41.8 25.0 %collective-permute-start.28 = (bf16[2,2,320,128]{3,2,1,0:T(8,128)(2,1)S(1)}, bf16[2,2,320,128]{3,2,1,0:T(8,128)(2,1)S(1)}, u32[]{:S(2)}, u32[]{:S(2)}) collective-permute-start(bf16[2,2,320,128]{3,2,1,0:T(8,128)(2,1)S(1)} %get-tuple-element.29), channel_id=1, source_target_pairs={{0,64},{32,96},{64,0},{96,32},{1,65},{33,97},{65,1},{97,33},{2,66}... | collective-permute-start | bytes 983048 | tf_op jit(solution)/shard_map/ppermute | solution.py:62
  45.0 19.2 %collective-permute-start.9 = (bf16[2,2,320,128]{3,2,1,0:T(8,128)(2,1)S(1)}, bf16[2,2,320,128]{3,2,1,0:T(8,128)(2,1)S(1)}, u32[]{:S(2)}, u32[]{:S(2)}) collective-permute-start(bf16[2,2,320,128]{3,2,1,0:T(8,128)(2,1)S(1)} %get-tuple-element.30), channel_id=1, source_target_pairs={{0,32},{32,64},{64,96},{96,0},{1,33},{33,65},{65,97},{97,1},{2,34}... | collective-permute-start | bytes 983048 | tf_op jit(solution)/shard_map/ppermute | solution.py:62
  52.1 20.4 %collective-permute-start.10 = (bf16[2,2,320,128]{3,2,1,0:T(8,128)(2,1)S(1)}, bf16[2,2,320,128]{3,2,1,0:T(8,128)(2,1)S(1)}, u32[]{:S(2)}, u32[]{:S(2)}) collective-permute-start(bf16[2,2,320,128]{3,2,1,0:T(8,128)(2,1)S(1)} %get-tuple-element.30), channel_id=1, source_target_pairs={{0,64},{32,96},{64,0},{96,32},{1,65},{33,97},{65,1},{97,33},{2,66}... | collective-permute-start | bytes 983048 | tf_op jit(solution)/shard_map/ppermute | solution.py:62
  66.8 14.1 %collective-permute-start.29 = (bf16[2,2,320,128]{3,2,1,0:T(8,128)(2,1)S(1)}, bf16[2,2,320,128]{3,2,1,0:T(8,128)(2,1)S(1)}, u32[]{:S(2)}, u32[]{:S(2)}) collective-permute-start(bf16[2,2,320,128]{3,2,1,0:T(8,128)(2,1)S(1)} %get-tuple-element.29), channel_id=1, source_target_pairs={{0,96},{32,0},{64,32},{96,64},{1,97},{33,1},{65,33},{97,65},{2,98}... | collective-permute-start | bytes 983048 | tf_op jit(solution)/shard_map/ppermute | solution.py:62
  74.2 28.9 %collective-permute-start.1 = (bf16[1024,128]{0,1:T(8,128)(2,1)S(1)}, bf16[1024,128]{0,1:T(8,128)(2,1)S(1)}, u32[]{:S(2)}, u32[]{:S(2)}) collective-permute-start(bf16[1024,128]{0,1:T(8,128)(2,1)S(1)} %collective-permute-done), channel_id=1, source_target_pairs={{0,128},{128,0},{1,129},{129,1},{2,130},{130,2},{3,131},{131,3},{4... | collective-permute-start | bytes 786440 | tf_op jit(solution)/shard_map/ppermute | solution.py:16
  80.8 25.8 %collective-permute-start.2 = (bf16[1024,128]{0,1:T(8,128)(2,1)S(1)}, bf16[1024,128]{0,1:T(8,128)(2,1)S(1)}, u32[]{:S(2)}, u32[]{:S(2)}) collective-permute-start(bf16[1024,128]{0,1:T(8,128)(2,1)S(1)} %collective-permute-done), channel_id=1, source_target_pairs={{0,16},{16,0},{1,17},{17,1},{2,18},{18,2},{3,19},{19,3},{4,20},{20... | collective-permute-start | bytes 786440 | tf_op jit(solution)/shard_map/ppermute | solution.py:16
  84.1 27.5 %collective-permute-start.3 = (bf16[1024,128]{0,1:T(8,128)(2,1)S(1)}, bf16[1024,128]{0,1:T(8,128)(2,1)S(1)}, u32[]{:S(2)}, u32[]{:S(2)}) collective-permute-start(bf16[1024,128]{0,1:T(8,128)(2,1)S(1)} %collective-permute-done), channel_id=1, source_target_pairs={{0,4},{4,0},{1,5},{5,1},{2,6},{6,2},{3,7},{7,3},{8,12},{12,8},{9,1... | collective-permute-start | bytes 786440 | tf_op jit(solution)/shard_map/ppermute | solution.py:16
  138.1 14.3 %all-to-all-start.3 = ((bf16[8,64,256]{2,1,0:T(8,128)(2,1)}), bf16[8,64,256]{2,1,0:T(8,128)(2,1)}, u32[]{:S(2)}, u32[]{:S(2)}) async-start(bf16[8,64,256]{2,1,0:T(8,128)(2,1)} %broadcast_in_dim.93), calls=%async_computation.3 | async-start | bytes 524288 | tf_op jit(solution)/shard_map/all_to_all | solution.py:78
  145.3 22.1 %collective-permute-start.19 = (bf16[1024,128]{0,1:T(8,128)(2,1)}, bf16[1024,128]{0,1:T(8,128)(2,1)}, u32[]{:S(2)}, u32[]{:S(2)}) collective-permute-start(bf16[1024,128]{0,1:T(8,128)(2,1)} %get-tuple-element.23), channel_id=1, source_target_pairs={{0,128},{128,0},{1,129},{129,1},{2,130},{130,2},{3,131},{131,3},{4... | collective-permute-start | bytes 786440 | tf_op jit(solution)/shard_map/ppermute | solution.py:16
  146.6 20.8 %collective-permute-start.20 = (bf16[1024,128]{0,1:T(8,128)(2,1)}, bf16[1024,128]{0,1:T(8,128)(2,1)}, u32[]{:S(2)}, u32[]{:S(2)}) collective-permute-start(bf16[1024,128]{0,1:T(8,128)(2,1)} %get-tuple-element.26), channel_id=1, source_target_pairs={{0,16},{16,0},{1,17},{17,1},{2,18},{18,2},{3,19},{19,3},{4,20},{20... | collective-permute-start | bytes 786440 | tf_op jit(solution)/shard_map/ppermute | solution.py:16
  148.8 18.6 %collective-permute-start.21 = (bf16[1024,128]{0,1:T(8,128)(2,1)}, bf16[1024,128]{0,1:T(8,128)(2,1)}, u32[]{:S(2)}, u32[]{:S(2)}) collective-permute-start(bf16[1024,128]{0,1:T(8,128)(2,1)} %get-tuple-element.25), channel_id=1, source_target_pairs={{0,4},{4,0},{1,5},{5,1},{2,6},{6,2},{3,7},{7,3},{8,12},{12,8},{9,1... | collective-permute-start | bytes 786440 | tf_op jit(solution)/shard_map/ppermute | solution.py:16
  150.0 17.4 %collective-permute-start.22 = (bf16[1024,128]{0,1:T(8,128)(2,1)}, bf16[1024,128]{0,1:T(8,128)(2,1)}, u32[]{:S(2)}, u32[]{:S(2)}) collective-permute-start(bf16[1024,128]{0,1:T(8,128)(2,1)} %get-tuple-element.24), channel_id=1, source_target_pairs={{0,8},{8,0},{1,9},{9,1},{2,10},{10,2},{3,11},{11,3},{4,12},{12,4},... | collective-permute-start | bytes 786440 | tf_op jit(solution)/shard_map/ppermute | solution.py:16
  177.0 17.2 %collective-permute-start.23 = (bf16[1024,128]{0,1:T(8,128)(2,1)}, bf16[1024,128]{0,1:T(8,128)(2,1)S(1)}, u32[]{:S(2)}, u32[]{:S(2)}) collective-permute-start(bf16[1024,128]{0,1:T(8,128)(2,1)} %copy-done.4), channel_id=1, source_target_pairs={{0,128},{128,0},{1,129},{129,1},{2,130},{130,2},{3,131},{131,3},{4... | collective-permute-start | bytes 786440 | tf_op jit(solution)/shard_map/ppermute | solution.py:16
  191.6 15.6 %collective-permute-start.26 = (bf16[1024,128]{0,1:T(8,128)(2,1)S(1)}, bf16[1024,128]{0,1:T(8,128)(2,1)S(1)}, u32[]{:S(2)}, u32[]{:S(2)}) collective-permute-start(bf16[1024,128]{0,1:T(8,128)(2,1)S(1)} %copy-done.5), channel_id=1, source_target_pairs={{0,8},{8,0},{1,9},{9,1},{2,10},{10,2},{3,11},{11,3},{4,12},{12,4},... | collective-permute-start | bytes 786440 | tf_op jit(solution)/shard_map/ppermute | solution.py:16
  194.9 13.0 %collective-permute-start.31 = (bf16[512,256]{1,0:T(8,128)(2,1)S(1)}, bf16[512,256]{1,0:T(8,128)(2,1)S(1)}, u32[]{:S(2)}, u32[]{:S(2)}) collective-permute-start(bf16[512,256]{1,0:T(8,128)(2,1)S(1)} %bitcast.238), channel_id=1, source_target_pairs={{0,16},{16,0},{1,17},{17,1},{2,18},{18,2},{3,19},{19,3},{4,20},{20... | collective-permute-start | bytes 786440 | tf_op jit(solution)/shard_map/ppermute | solution.py:16
  245.5 13.6 %collective-permute-start.37 = (bf16[1024,128]{0,1:T(8,128)(2,1)S(1)}, bf16[1024,128]{0,1:T(8,128)(2,1)S(1)}, u32[]{:S(2)}, u32[]{:S(2)}) collective-permute-start(bf16[1024,128]{0,1:T(8,128)(2,1)S(1)} %get-tuple-element.18), channel_id=1, source_target_pairs={{0,8},{8,0},{1,9},{9,1},{2,10},{10,2},{3,11},{11,3},{4,12},{12,4},... | collective-permute-start | bytes 786440 | tf_op jit(solution)/shard_map/ppermute | solution.py:16
  259.5 14.4 %collective-permute-start.38 = (bf16[1024,128]{0,1:T(8,128)(2,1)S(1)}, bf16[1024,128]{0,1:T(8,128)(2,1)S(1)}, u32[]{:S(2)}, u32[]{:S(2)}) collective-permute-start(bf16[1024,128]{0,1:T(8,128)(2,1)S(1)} %add_convert_fusion), channel_id=1, source_target_pairs={{0,0},{128,1},{16,2},{144,3},{2,16},{130,17},{18,18},{146,19},{1,1... | collective-permute-start | bytes 786440 | tf_op jit(solution)/shard_map/ppermute | solution.py:32
  (35 other events, 254.5 us)

commit v2 on v1

v2 whole, which is shorter than its diff:
```python
import jax
import jax.numpy as jnp
from jax import lax
from jax.experimental import pallas as pl
from jax.experimental.pallas import tpu as pltpu
from jax.sharding import Mesh, PartitionSpec as P

BF = jnp.bfloat16
F32 = jnp.float32
TOK = ("zl", "y1", "y0", "core")
FEAT = ("x1", "x0", "zh1", "zh0")
SWAPPED = ("zl", "core", "zh1", "zh0")
BIT_AXES = ("zl", "core", "x0", "x1")
CUBE = ("x1", "x0", "zl")


def pair(value, axis):
    return lax.ppermute(value, axis, [(0, 1), (1, 0)])


def bits(i):
    return i >> 3 & 1, i >> 2 & 1, i >> 1 & 1, i & 1


def index(zl, core, zh1, zh0):
    return zl << 3 | core << 2 | zh1 << 1 | zh0


def swap(value, k0=0, k1=0):
    perm = []
    for dst in range(16):
        zl, core, zh1, zh0 = bits(dst)
        perm.append((index(zh0 ^ k0, zh1 ^ k1, core, zl), dst))
    return lax.ppermute(value, SWAPPED, perm)


def swap_copied(value):
    perm = []
    for dst in range(16):
        zl, core, zh1, zh0 = bits(dst)
        perm.append((index(zh0 ^ zh1 ^ core, zh1, core, zl), dst))
    return lax.ppermute(value, SWAPPED, perm)


def copied_all_to_all(value, count, axes):
    return lax.all_to_all(jnp.broadcast_to(value[None], (count,) + value.shape), axes, 0, 0)


def after(value, *others):
    return lax.optimization_barrier((value,) + others)[0]


def nt_dot(left, right):
    return lax.dot_general(left, right, (((1,), (1,)), ((), ())), preferred_element_type=F32)


def dot(left, right):
    return jnp.dot(left, right, preferred_element_type=F32)


TILE = 256
TILES = 4
TOKENS = TILE * TILES
HALF = TOKENS // 2
WIDTH = 128
HIDDEN = 512
RANK = 256
LIMIT = pltpu.CompilerParams(vmem_limit_bytes=56 << 20)


def ordered(rows):
    core = lax.axis_index("core")
    half = rows.shape[0] // 2
    return jnp.where(core == 0, rows, jnp.concatenate([rows[half:], rows[:half]], axis=0))


def prep_kernel(order, cols, up_w, down_w):
    for place in range(5):
        at = pl.multiple_of(order[place] * 32, 32)
        for zl in range(2):
            for y in range(4):
                for core in range(2):
                    t = zl * 8 + y * 2 + core
                    up_w[t * 32 : (t + 1) * 32, place * WIDTH : (place + 1) * WIDTH] = cols[
                        y, zl * 2 + core, pl.ds(at, 32), :
                    ]
                pieces = [
                    cols[y, zl * 2 + core, pl.ds(160 + at, 32), :].astype(F32) for core in range(2)
                ]
                top = place * WIDTH + zl * 64 + y * 16
                for q in range(4):
                    down_w[top : top + 16, q * 128 : (q + 1) * 128] = jnp.concatenate(
                        [piece[q * 8 : (q + 1) * 8] for piece in pieces], axis=0
                    ).astype(BF)


def prep(order, cols):
    shapes = [(HIDDEN, 5 * WIDTH), (5 * WIDTH, HIDDEN)]
    return pl.pallas_call(
        prep_kernel,
        grid_spec=pltpu.PrefetchScalarGridSpec(
            num_scalar_prefetch=1,
            grid=(1,),
            in_specs=[pl.BlockSpec((4, 4, 320, 128), lambda i, order: (0, 0, 0, 0))],
            out_specs=[pl.BlockSpec(shape, lambda i, order: (0, 0)) for shape in shapes],
        ),
        out_shape=[jax.ShapeDtypeStruct(shape, BF) for shape in shapes],
        compiler_params=LIMIT,
        cost_estimate=pl.CostEstimate(flops=1 << 20, bytes_accessed=3 << 20, transcendentals=0),
        name="prep",
    )(order, cols)


def gelu(value):
    return 0.5 * value * (1.0 + lax.erf(value * (0.5**0.5)))


def mlp_kernel(
    x, p_zl, p_core, p_x0, p_x1, mine, other, up_w, down_w, rank_up, rank_down,
    mine_back, other_back, own, t_zl, t_core, t_x0, t_x1,
):
    i = pl.program_id(0)
    value = x[...]
    left = jnp.concatenate([value, p_zl[...], p_core[...], p_x0[...], p_x1[...]], axis=1)
    latent = jnp.where(i < 2, mine[...], other[...])
    pre = nt_dot(left, up_w[...]) + dot(latent, rank_up[...])
    hidden = gelu(pre).astype(BF)
    share = dot(hidden, rank_down[...]).astype(BF)

    @pl.when(i < 2)
    def _():
        mine_back[...] = share

    @pl.when(i >= 2)
    def _():
        other_back[...] = share

    terms = nt_dot(hidden, down_w[...])
    own[...] = value.astype(F32) + terms[:, :WIDTH]
    for bit, out in enumerate((t_zl, t_core, t_x0, t_x1)):
        out[...] = terms[:, (1 + bit) * WIDTH : (2 + bit) * WIDTH].astype(BF)


def mlp(x, partners, latent, weights, rank_up, rank_down):
    row = pl.BlockSpec((TILE, WIDTH), lambda i: (i, 0))
    partner_row = pl.BlockSpec((TILE, WIDTH), lambda i: ((i + 2) % TILES, 0))
    halves = [
        pl.BlockSpec((TILE, RANK), lambda i: (jnp.minimum(i, 1), 0)),
        pl.BlockSpec((TILE, RANK), lambda i: (jnp.maximum(i - 2, 0), 0)),
    ]
    whole = lambda *shape: pl.BlockSpec(shape, lambda i: (0,) * len(shape))
    shape = jax.ShapeDtypeStruct
    return pl.pallas_call(
        mlp_kernel,
        grid=(TILES,),
        in_specs=[row, row, partner_row, row, row]
        + halves
        + [
            whole(HIDDEN, 5 * WIDTH),
            whole(5 * WIDTH, HIDDEN),
            whole(RANK, HIDDEN),
            whole(HIDDEN, RANK),
        ],
        out_specs=halves + [row] * 5,
        out_shape=[shape((HALF, RANK), BF)] * 2
        + [shape((TOKENS, WIDTH), F32)]
        + [shape((TOKENS, WIDTH), BF)] * 4,
        compiler_params=LIMIT,
        cost_estimate=pl.CostEstimate(
            flops=4 * TOKENS * HIDDEN * (5 * WIDTH + RANK),
            bytes_accessed=6 << 20,
            transcendentals=0,
        ),
        name="mlp",
    )(x, *partners, *latent, *weights, rank_up, rank_down)


def chip_sums(parts):
    return jnp.sum(lax.all_to_all(parts, CUBE, 0, 0).astype(F32), axis=0)


def core_sum(mine, other):
    return mine.astype(F32) + pair(other.astype(BF), "core").astype(F32)


def share_of_core(rows):
    core = lax.axis_index("core")
    half = rows.shape[0] // 2
    return (
        lax.dynamic_slice_in_dim(rows, core * half, half, 0),
        lax.dynamic_slice_in_dim(rows, (1 - core) * half, half, 0),
    )


def block_shards(up_blocks, down_blocks):
    layers = up_blocks.shape[0]
    up_shard = up_blocks[:, 0].transpose(0, 1, 3, 2).reshape(layers, 160, 128)
    down_shard = down_blocks[:, 0].reshape(layers, 5, 4, 128, 8).transpose(0, 1, 2, 4, 3)
    return jnp.concatenate([up_shard, down_shard.reshape(layers, 160, 128)], axis=1)


def gather_planes(shards):
    zh0, zh1 = lax.axis_index("zh0"), lax.axis_index("zh1")
    out = jnp.zeros(shards.shape[:1] + (2, 2) + shards.shape[1:], shards.dtype)
    for k0 in range(2):
        for k1 in range(2):
            got = swap(shards, k0, k1)
            out = lax.dynamic_update_slice(out, got[:, None, None], (0, zh0 ^ k0, zh1 ^ k1, 0, 0))
    return out


def gather_columns(plane):
    y = lax.axis_index(("y1", "y0"))
    plane = plane.reshape((1, 4) + plane.shape[2:])
    out = jnp.zeros((4,) + plane.shape[1:], plane.dtype)
    out = lax.dynamic_update_slice(out, plane, (y, 0, 0, 0))
    for step in range(1, 4):
        got = lax.ppermute(plane, ("y1", "y0"), [(i, (i + step) % 4) for i in range(4)])
        out = lax.dynamic_update_slice(out, got, ((y - step) % 4, 0, 0, 0))
    return out


def low_rank_part(x, rows_in):
    other = dot(x[HALF:], rows_in)
    return core_sum(dot(x[:HALF], rows_in), other).astype(BF).reshape(8, HALF // 8, RANK)


def exchange(blocks):
    return [pair(value, axis) for value, axis in zip(blocks, BIT_AXES)]


def per_device(tokens, level_bits, up_blocks, down_blocks, rank_in, rank_up, rank_down, rank_out):
    layers = level_bits.shape[0]
    core = lax.axis_index("core")
    block = lax.axis_index("x1") * 8 + lax.axis_index("x0") * 4 + core * 2 + lax.axis_index("zl")
    levels = jnp.arange(4, dtype=jnp.int32)
    orders = [
        jnp.stack(
            [jnp.int32(0)]
            + [1 + jnp.sum(jnp.where(level_bits[layer] == bit, levels, 0)) for bit in range(4)]
        )
        for layer in range(layers)
    ]
    rows_in = lax.dynamic_slice(rank_in, (0, block * WIDTH, 0), (layers, WIDTH, RANK))
    x = swap(tokens)
    planes = gather_planes(block_shards(up_blocks, down_blocks))
    x, planes = lax.optimization_barrier((x, planes))
    x = ordered(x)
    rank_out = swap_copied(after(rank_out, x))
    ranks = [[swap_copied(after(value[0], x)) for value in (rank_up, rank_down)]]
    partners = exchange([x] * 4)
    parts = low_rank_part(x, rows_in[0])
    gathered = [gather_columns(planes[0])]
    share = after(chip_sums(parts).astype(BF), gathered[0], partners[0], partners[2])
    latent = copied_all_to_all(share, 8, CUBE).reshape(HALF, RANK)
    latent = latent, pair(latent, "core")
    for layer in range(layers):
        last = layer == layers - 1
        weights = prep(orders[layer], gathered[layer])
        mine, other, own, *terms = mlp(x, partners, latent, weights, *ranks[layer])
        parts = core_sum(mine, other).astype(BF).reshape(8, HALF // 8, RANK)
        if not last:
            mine, other = share_of_core(dot(rank_out[layer], rows_in[layer + 1]))
            small = core_sum(mine, other).astype(BF).reshape(8, RANK // 16, RANK)
            parts = jnp.concatenate([parts, small], axis=1)
            gathered.append(gather_columns(after(planes[layer + 1], parts)))
            ranks.append(
                [swap_copied(after(value[layer + 1], own)) for value in (rank_up, rank_down)]
            )
        share = chip_sums(parts).astype(BF)
        terms = exchange(terms)
        t_zl, t_core, t_x0, t_x1 = terms
        t_core = jnp.concatenate([t_core[HALF:], t_core[:HALF]], axis=0)
        if last:
            share = after(share, terms[0], terms[3])
            back = copied_all_to_all(share, 8, CUBE).reshape(HALF, RANK)
            back = back, pair(back, "core")
        for term in (t_zl, t_core, t_x0, t_x1):
            own = own + term.astype(F32)
        if not last:
            parts = low_rank_part(own.astype(BF), rows_in[layer + 1])
            got = lax.all_to_all(
                jnp.concatenate(
                    [jnp.broadcast_to(share[None], (8,) + share.shape), parts], axis=1
                ),
                CUBE, 0, 0,
            )
            both = got[:, : HALF // 8 + RANK // 16]
            pair_both = pair(both, "core")
            back = both[:, : HALF // 8].reshape(HALF, RANK), pair_both[:, : HALF // 8].reshape(HALF, RANK)
            small = jnp.concatenate([both[:, HALF // 8 :], pair_both[:, HALF // 8 :]], axis=0)
            small = ordered(small.reshape(RANK, RANK))
            latent = jnp.sum(got[:, HALF // 8 + RANK // 16 :].astype(F32), axis=0)
            latent = latent + dot(share[: HALF // 8], small)
            latent = after(latent.astype(BF), gathered[layer + 1], *ranks[layer + 1])
            latent = copied_all_to_all(latent, 8, CUBE).reshape(HALF, RANK)
            latent = latent, pair(latent, "core")
        own = own + dot(jnp.concatenate(back, axis=0), rank_out[layer])
        x = own.astype(BF)
        if not last:
            partners = exchange([x] * 4)
    return swap(ordered(x))


def solution(mesh):
    fine = Mesh(mesh.devices.reshape((2,) * 8), TOK + FEAT)
    return jax.shard_map(
        per_device,
        mesh=fine,
        in_specs=(
            P(TOK, FEAT),
            P(),
            P(None, FEAT, None, None, TOK),
            P(None, FEAT, None, None, TOK),
            P(),
            P(None, None, FEAT),
            P(None, FEAT, None),
            P(None, None, FEAT),
        ),
        out_specs=P(TOK, FEAT),
        check_vma=False,
    )
```

time: 277 us -> 248 us (0.90)
  waiting for transfers between devices: 92 us -> 52.7 us
  Pallas kernels: 0 us -> 21.4 us
  matrix products: 26 us -> 6.86 us
  starting transfers between devices: 110 us -> 123 us
  local copies, waits for them, and re-layouts: 32.6 us -> 25.5 us
    pallas_call x0 -> x4, Pallas kernels: none -> 21.4 us  [the longest x2 14.8 us: mlp(): pl.pallas_call(mlp_kernel, grid=(TILES,), in_specs=[row, row, partner_row...]
    all_to_all x8 -> x7, waiting for transfers between devices: 27.1 us -> 6.38 us  [the longest x3 3.49 us: copied_all_to_all(): lax.all_to_all(jnp.broadcast_to(value[None], (count,) + value.shape), axe...]
    ppermute x6, waiting for transfers between devices: 22.5 us -> 2.83 us  [gather_columns(): lax.ppermute(plane, ('y1', 'y0'), [(i, (i + step) % 4) for i in range(4)])]
    dot_general x12 -> x8, matrix products: 26 us -> 6.86 us  [dot(): return jnp.dot(left, right, preferred_element_type=F32)]
    ppermute x3 -> x5, starting transfers between devices: 10 us -> 23.8 us  [swap_copied(): return lax.ppermute(value, SWAPPED, perm)]
    ppermute x6, waiting for transfers between devices: 10.1 us -> 19.2 us  [swap(): return lax.ppermute(value, SWAPPED, perm)]
    dynamic_update_slice x11 -> x12, local copies, waits for them, and re-layouts: 0.47 us -> 9.13 us  [the longest x6 5.15 us: gather_columns(): out = lax.dynamic_update_slice(out, got, ((y - step) % 4, 0, 0, 0))]
    unnamed x40 -> x51, local copies, waits for them, and re-layouts: 11.9 us -> 3.75 us
  transfers between devices with their start and end apart: 47 -> 49, of which waited for: 22 -> 16; matrix products, arithmetic and copies ran while one was open for 16% -> 12% of each run, Pallas kernels for 0% -> 6%
where the time goes in v2:
time: 248 us; the launch traced here: 246 us
  starting transfers between devices  123 us (50%)
  waiting for transfers between devices  52.7 us (21%)
  local copies, waits for them, and re-layouts  25.5 us (10%)
  Pallas kernels  21.4 us (9%)
  other arithmetic  10.8 us (4%)
  matrix products  6.86 us (3%)
  between operations  5.84 us (2%)
    ppermute x25, starting transfers between devices, pair(): return lax.ppermute(value, axis, [(0, 1), (1, 0)])  38.1 us
    ppermute x6, starting transfers between devices, swap(): return lax.ppermute(value, SWAPPED, perm)  24 us
    ppermute x5, starting transfers between devices, swap_copied(): return lax.ppermute(value, SWAPPED, perm)  23.8 us
    ppermute x25, waiting for transfers between devices, pair(): return lax.ppermute(value, axis, [(0, 1), (1, 0)])  20.6 us
    ppermute x6, waiting for transfers between devices, swap(): return lax.ppermute(value, SWAPPED, perm)  19.2 us
    pallas_call x2, Pallas kernels, mlp(): pl.pallas_call(mlp_kernel, grid=(TILES,), in_specs=[row, row, partner_row...  14.8 us
    all_to_all x3, starting transfers between devices, copied_all_to_all(): lax.all_to_all(jnp.broadcast_to(value[None], (count,) + value.shape), axe...  13.5 us
    all_to_all x3, starting transfers between devices, chip_sums(): return jnp.sum(lax.all_to_all(parts, CUBE, 0, 0).astype(F32), axis=0)  10.9 us
  transfers between devices with their start and end apart: 49, of which 16 were waited for; matrix products, arithmetic and copies ran while one was open for 12% of the time, Pallas kernels for 6%

profile of v2, /device:TPU:1, one launch (start us, length us, event | category | flops | bytes accessed | tf_op | source)
XLA Modules:
  0.0 246.2 jit_solution(16667886175752091888)
XLA Ops:
  1.1 10.2 %collective-permute-start.1 = (bf16[2,320,128]{2,1,0:T(8,128)(2,1)S(1)}, bf16[2,320,128]{2,1,0:T(8,128)(2,1)}, u32[]{:S(2)}, u32[]{:S(2)}) collective-permute-start(bf16[2,320,128]{2,1,0:T(8,128)(2,1)S(1)} %pad_maximum_fusion.2), channel_id=1, source_target_pairs={{0,0},{128,1},{16,2},{144,3},{2,16},{130,17},{18,18},{146,19},{1,1... | collective-permute-start | bytes 491528 | tf_op jit(solution)/shard_map/ppermute | solution.py:34
  14.8 6.1 %collective-permute-start = (bf16[1024,128]{1,0:T(8,128)(2,1)}, bf16[1024,128]{1,0:T(8,128)(2,1)S(1)}, u32[]{:S(2)}, u32[]{:S(2)}) collective-permute-start(bf16[1024,128]{1,0:T(8,128)(2,1)} %param.8), channel_id=1, source_target_pairs={{0,0},{128,1},{16,2},{144,3},{2,16},{130,17},{18,18},{146,19},{1,1... | collective-permute-start | bytes 786440 | tf_op jit(solution)/shard_map/ppermute | solution.py:34
  22.9 4.6 %collective-permute-done.3 = bf16[2,320,128]{2,1,0:T(8,128)(2,1)S(1)} collective-permute-done((bf16[2,320,128]{2,1,0:T(8,128)(2,1)S(1)}, bf16[2,320,128]{2,1,0:T(8,128)(2,1)S(1)}, u32[]{:S(2)}, u32[]{:S(2)}) %collective-permute-start.3) | collective-permute-done | bytes 163872 | tf_op jit(solution)/shard_map/ppermute | solution.py:34
  27.9 4.1 %collective-permute-done = bf16[1024,128]{1,0:T(8,128)(2,1)S(1)} collective-permute-done((bf16[1024,128]{1,0:T(8,128)(2,1)}, bf16[1024,128]{1,0:T(8,128)(2,1)S(1)}, u32[]{:S(2)}, u32[]{:S(2)}) %collective-permute-start) | collective-permute-done | bytes 262176 | tf_op jit(solution)/shard_map/ppermute | solution.py:34
  48.3 4.0 %all-to-all-start = ((bf16[8,64,256]{2,1,0:T(8,128)(2,1)}), bf16[8,64,256]{2,1,0:T(8,128)(2,1)}, u32[]{:S(2)}, u32[]{:S(2)}) async-start(bf16[8,64,256]{2,1,0:T(8,128)(2,1)} %bitcast.14), calls=%async_computation | async-start | bytes 524288 | tf_op jit(solution)/shard_map/all_to_all | solution.py:179
  61.5 5.1 %all-to-all-start.1 = ((bf16[8,64,256]{2,1,0:T(8,128)(2,1)}), bf16[8,64,256]{2,1,0:T(8,128)(2,1)}, u32[]{:S(2)}, u32[]{:S(2)}) async-start(bf16[8,64,256]{2,1,0:T(8,128)(2,1)} %broadcast_in_dim.53), calls=%async_computation.1 | async-start | bytes 524288 | tf_op jit(solution)/shard_map/all_to_all | solution.py:46
  68.5 6.5 %collective-permute-start.21 = (bf16[2,256,128]{2,1,0:T(8,128)(2,1)}, bf16[2,256,128]{2,1,0:T(8,128)(2,1)S(1)}, u32[]{:S(2)}, u32[]{:S(2)}) collective-permute-start(bf16[2,256,128]{2,1,0:T(8,128)(2,1)} %param.15), channel_id=1, source_target_pairs={{0,0},{128,1},{144,2},{16,3},{130,16},{2,17},{18,18},{146,19},{1,1... | collective-permute-start | bytes 393224 | tf_op jit(solution)/shard_map/ppermute | solution.py:42
  82.0 6.1 %collective-permute-start.15 = (bf16[512,256]{1,0:T(8,128)(2,1)}, bf16[512,256]{1,0:T(8,128)(2,1)S(1)}, u32[]{:S(2)}, u32[]{:S(2)}) collective-permute-start(bf16[512,256]{1,0:T(8,128)(2,1)} %get-tuple-element.40), channel_id=1, source_target_pairs={{0,0},{128,1},{144,2},{16,3},{130,16},{2,17},{18,18},{146,19},{1,1... | collective-permute-start | bytes 786440 | tf_op jit(solution)/shard_map/ppermute | solution.py:42
  96.3 7.3 %mlp.2 = (bf16[512,256]{1,0:T(8,128)(2,1)}, bf16[512,256]{1,0:T(8,128)(2,1)}, f32[1024,128]{1,0:T(8,128)}, bf16[1024,128]{1,0:T(8,128)(2,1)}, bf16[1024,128]{1,0...) custom-call(bf16[1024,128]{1,0:T(8,128)(2,1)} %maximum_select_fusion.x, ...), custom_call_target="tpu_custom_call" | custom-call | flops 1879048192 | bytes 6291456 | tf_op jit(solution)/shard_map/mlp/pallas_call | solution.py:153
  104.6 3.7 %collective-permute-start.16 = (bf16[1024,128]{1,0:T(8,128)(2,1)}, bf16[1024,128]{1,0:T(8,128)(2,1)S(1)}, u32[]{:S(2)}, u32[]{:S(2)}) collective-permute-start(bf16[1024,128]{1,0:T(8,128)(2,1)} %get-tuple-element.42), channel_id=1, source_target_pairs={{0,128},{128,0},{1,129},{129,1},{2,130},{130,2},{3,131},{131,3},{4... | collective-permute-start | bytes 786440 | tf_op jit(solution)/shard_map/ppermute | solution.py:18
  113.0 3.4 %all-to-all-start.2 = ((bf16[8,80,256]{2,1,0:T(8,128)(2,1)}), bf16[8,80,256]{2,1,0:T(8,128)(2,1)S(1)}, u32[]{:S(2)}, u32[]{:S(2)}) async-start(bf16[8,80,256]{2,1,0:T(8,128)(2,1)} %pad_maximum_fusion.1), calls=%async_computation.2 | async-start | bytes 655360 | tf_op jit(solution)/shard_map/all_to_all | solution.py:179
  117.4 5.4 %collective-permute-done.19 = bf16[1024,128]{1,0:T(8,128)(2,1)} collective-permute-done((bf16[1024,128]{1,0:T(8,128)(2,1)}, bf16[1024,128]{1,0:T(8,128)(2,1)}, u32[]{:S(2)}, u32[]{:S(2)}) %collective-permute-start.19) | collective-permute-done | bytes 262176 | tf_op jit(solution)/shard_map/ppermute | solution.py:18
  124.2 3.4 %collective-permute-start.23 = (bf16[512,256]{1,0:T(8,128)(2,1)S(1)}, bf16[512,256]{1,0:T(8,128)(2,1)S(1)}, u32[]{:S(2)}, u32[]{:S(2)}) collective-permute-start(bf16[512,256]{1,0:T(8,128)(2,1)S(1)} %convolution_convert_fusion), channel_id=1, source_target_pairs={{0,16},{16,0},{1,17},{17,1},{2,18},{18,2},{3,19},{19,3},{4,20},{20... | collective-permute-start | bytes 786440 | tf_op jit(solution)/shard_map/ppermute | solution.py:18
  130.0 4.2 %all-to-all-start.3 = ((bf16[8,144,256]{2,1,0:T(8,128)(2,1)}), bf16[8,144,256]{2,1,0:T(8,128)(2,1)}, u32[]{:S(2)}, u32[]{:S(2)}) async-start(bf16[8,144,256]{2,1,0:T(8,128)(2,1)} %pad_maximum_fusion), calls=%async_computation.3 | async-start | bytes 1179648 | tf_op jit(solution)/shard_map/all_to_all | solution.py:282
  139.6 5.0 %collective-permute-start.33 = (bf16[512,256]{1,0:T(8,128)(2,1)}, bf16[512,256]{1,0:T(8,128)(2,1)}, u32[]{:S(2)}, u32[]{:S(2)}) collective-permute-start(bf16[512,256]{1,0:T(8,128)(2,1)} %get-tuple-element.51), channel_id=1, source_target_pairs={{0,0},{128,1},{144,2},{16,3},{130,16},{2,17},{18,18},{146,19},{1,1... | collective-permute-start | bytes 786440 | tf_op jit(solution)/shard_map/ppermute | solution.py:42
  148.7 5.3 %collective-permute-start.24 = (bf16[8,80,256]{2,1,0:T(8,128)(2,1)S(1)}, bf16[8,80,256]{2,1,0:T(8,128)(2,1)S(1)}, u32[]{:S(2)}, u32[]{:S(2)}) collective-permute-start(bf16[8,80,256]{2,1,0:T(8,128)(2,1)S(1)} %slice.152), channel_id=1, source_target_pairs={{0,16},{16,0},{1,17},{17,1},{2,18},{18,2},{3,19},{19,3},{4,20},{20... | collective-permute-start | bytes 983048 | tf_op jit(solution)/shard_map/ppermute | solution.py:18
  159.7 5.0 %all-to-all-start.4 = ((bf16[8,64,256]{2,1,0:T(8,128)(2,1)}), bf16[8,64,256]{2,1,0:T(8,128)(2,1)}, u32[]{:S(2)}, u32[]{:S(2)}) async-start(bf16[8,64,256]{2,1,0:T(8,128)(2,1)} %broadcast_in_dim.55), calls=%async_computation.4 | async-start | bytes 524288 | tf_op jit(solution)/shard_map/all_to_all | solution.py:46
  181.3 5.0 %collective-permute-done.28.p_x1 = bf16[1024,128]{1,0:T(8,128)(2,1)S(1)} collective-permute-done((bf16[1024,128]{1,0:T(8,128)(2,1)S(1)}, bf16[1024,128]{1,0:T(8,128)(2,1)S(1)}, u32[]{:S(2)}, u32[]{:S(2)}) %collective-permute-start.28) | collective-permute-done | bytes 262176 | tf_op jit(solution)/shard_map/ppermute | solution.py:18
  187.1 7.4 %mlp.3 = (bf16[512,256]{1,0:T(8,128)(2,1)}, bf16[512,256]{1,0:T(8,128)(2,1)}, f32[1024,128]{1,0:T(8,128)}, bf16[1024,128]{1,0:T(8,128)(2,1)}, bf16[1024,128]{1,0...) custom-call(bf16[1024,128]{1,0:T(8,128)(2,1)} %copy-done.15, bf16[1024,128]{1,0:T(8,128)(2,1)} %copy-done.17, ...), custom_call_target="tpu_custom_call" | custom-call | flops 1879048192 | bytes 6291456 | tf_op jit(solution)/shard_map/mlp/pallas_call | solution.py:153
  198.7 3.4 %all-to-all-start.5 = ((bf16[8,64,256]{2,1,0:T(8,128)(2,1)}), bf16[8,64,256]{2,1,0:T(8,128)(2,1)S(1)}, u32[]{:S(2)}, u32[]{:S(2)}) async-start(bf16[8,64,256]{2,1,0:T(8,128)(2,1)} %bitcast.50), calls=%async_computation.5 | async-start | bytes 524288 | tf_op jit(solution)/shard_map/all_to_all | solution.py:179
  209.2 3.5 %collective-permute-done.35 = bf16[1024,128]{1,0:T(8,128)(2,1)S(1)} collective-permute-done((bf16[1024,128]{1,0:T(8,128)(2,1)}, bf16[1024,128]{1,0:T(8,128)(2,1)S(1)}, u32[]{:S(2)}, u32[]{:S(2)}) %collective-permute-start.35) | collective-permute-done | bytes 262176 | tf_op jit(solution)/shard_map/ppermute | solution.py:18
  221.4 3.5 %all-to-all-done.6 = bf16[8,64,256]{2,1,0:T(8,128)(2,1)S(1)} async-done(((bf16[8,64,256]{2,1,0:T(8,128)(2,1)}), bf16[8,64,256]{2,1,0:T(8,128)(2,1)S(1)}, u32[]{:S(2)}, u32[]{:S(2)}) %all-to-all-start.6) | async-done | bytes 262176 | tf_op jit(solution)/shard_map/all_to_all | solution.py:46
  231.1 4.2 %collective-permute-start.41 = (bf16[1024,128]{1,0:T(8,128)(2,1)S(1)}, bf16[1024,128]{1,0:T(8,128)(2,1)S(1)}, u32[]{:S(2)}, u32[]{:S(2)}) collective-permute-start(bf16[1024,128]{1,0:T(8,128)(2,1)S(1)} %maximum_select_fusion.1), channel_id=1, source_target_pairs={{0,0},{128,1},{16,2},{144,3},{2,16},{130,17},{18,18},{146,19},{1,1... | collective-permute-start | bytes 786440 | tf_op jit(solution)/shard_map/ppermute | solution.py:34
  235.3 10.2 %collective-permute-done.41 = bf16[1024,128]{1,0:T(8,128)(2,1)S(1)} collective-permute-done((bf16[1024,128]{1,0:T(8,128)(2,1)S(1)}, bf16[1024,128]{1,0:T(8,128)(2,1)S(1)}, u32[]{:S(2)}, u32[]{:S(2)}) %collective-permute-start.41) | collective-permute-done | bytes 262176 | tf_op jit(solution)/shard_map/ppermute | solution.py:34
  (186 shorter events, 113.5 us)
Async XLA Ops:
  1.1 19.8 %collective-permute-start.1 = (bf16[2,320,128]{2,1,0:T(8,128)(2,1)S(1)}, bf16[2,320,128]{2,1,0:T(8,128)(2,1)}, u32[]{:S(2)}, u32[]{:S(2)}) collective-permute-start(bf16[2,320,128]{2,1,0:T(8,128)(2,1)S(1)} %pad_maximum_fusion.2), channel_id=1, source_target_pairs={{0,0},{128,1},{16,2},{144,3},{2,16},{130,17},{18,18},{146,19},{1,1... | collective-permute-start | bytes 491528 | tf_op jit(solution)/shard_map/ppermute | solution.py:34
  11.4 16.2 %collective-permute-start.3 = (bf16[2,320,128]{2,1,0:T(8,128)(2,1)S(1)}, bf16[2,320,128]{2,1,0:T(8,128)(2,1)S(1)}, u32[]{:S(2)}, u32[]{:S(2)}) collective-permute-start(bf16[2,320,128]{2,1,0:T(8,128)(2,1)S(1)} %pad_maximum_fusion.2), channel_id=1, source_target_pairs={{128,0},{0,1},{144,2},{16,3},{130,16},{2,17},{146,18},{18,19},{129... | collective-permute-start | bytes 491528 | tf_op jit(solution)/shard_map/ppermute | solution.py:34
  11.7 16.2 %collective-permute-start.4 = (bf16[2,320,128]{2,1,0:T(8,128)(2,1)S(1)}, bf16[2,320,128]{2,1,0:T(8,128)(2,1)S(1)}, u32[]{:S(2)}, u32[]{:S(2)}) collective-permute-start(bf16[2,320,128]{2,1,0:T(8,128)(2,1)S(1)} %pad_maximum_fusion.2), channel_id=1, source_target_pairs={{144,0},{16,1},{128,2},{0,3},{146,16},{18,17},{130,18},{2,19},{145... | collective-permute-start | bytes 491528 | tf_op jit(solution)/shard_map/ppermute | solution.py:34
  14.8 17.2 %collective-permute-start = (bf16[1024,128]{1,0:T(8,128)(2,1)}, bf16[1024,128]{1,0:T(8,128)(2,1)S(1)}, u32[]{:S(2)}, u32[]{:S(2)}) collective-permute-start(bf16[1024,128]{1,0:T(8,128)(2,1)} %param.8), channel_id=1, source_target_pairs={{0,0},{128,1},{16,2},{144,3},{2,16},{130,17},{18,18},{146,19},{1,1... | collective-permute-start | bytes 786440 | tf_op jit(solution)/shard_map/ppermute | solution.py:34
  38.9 14.7 %collective-permute-start.10 = (bf16[1,4,320,128]{3,2,1,0:T(8,128)(2,1)}, bf16[1,4,320,128]{3,2,1,0:T(8,128)(2,1)}, u32[]{:S(2)}, u32[]{:S(2)}) collective-permute-start(bf16[1,4,320,128]{3,2,1,0:T(8,128)(2,1)} %bitcast.15), channel_id=1, source_target_pairs={{0,32},{32,64},{64,96},{96,0},{1,33},{33,65},{65,97},{97,1},{2,34}... | collective-permute-start | bytes 983048 | tf_op jit(solution)/shard_map/ppermute | solution.py:218
  40.2 17.3 %collective-permute-start.11 = (bf16[1,4,320,128]{3,2,1,0:T(8,128)(2,1)}, bf16[1,4,320,128]{3,2,1,0:T(8,128)(2,1)}, u32[]{:S(2)}, u32[]{:S(2)}) collective-permute-start(bf16[1,4,320,128]{3,2,1,0:T(8,128)(2,1)} %bitcast.15), channel_id=1, source_target_pairs={{0,64},{32,96},{64,0},{96,32},{1,65},{33,97},{65,1},{97,33},{2,66}... | collective-permute-start | bytes 983048 | tf_op jit(solution)/shard_map/ppermute | solution.py:218
  42.8 15.7 %collective-permute-start.12 = (bf16[1,4,320,128]{3,2,1,0:T(8,128)(2,1)}, bf16[1,4,320,128]{3,2,1,0:T(8,128)(2,1)}, u32[]{:S(2)}, u32[]{:S(2)}) collective-permute-start(bf16[1,4,320,128]{3,2,1,0:T(8,128)(2,1)} %bitcast.15), channel_id=1, source_target_pairs={{0,96},{32,0},{64,32},{96,64},{1,97},{33,1},{65,33},{97,65},{2,98}... | collective-permute-start | bytes 983048 | tf_op jit(solution)/shard_map/ppermute | solution.py:218
  43.9 16.9 %collective-permute-start.5 = (bf16[1024,128]{1,0:T(8,128)(2,1)}, bf16[1024,128]{1,0:T(8,128)(2,1)}, u32[]{:S(2)}, u32[]{:S(2)}) collective-permute-start(bf16[1024,128]{1,0:T(8,128)(2,1)} %maximum_select_fusion.x), channel_id=1, source_target_pairs={{0,128},{128,0},{1,129},{129,1},{2,130},{130,2},{3,131},{131,3},{4... | collective-permute-start | bytes 786440 | tf_op jit(solution)/shard_map/ppermute | solution.py:18
  45.2 15.6 %collective-permute-start.7 = (bf16[1024,128]{1,0:T(8,128)(2,1)}, bf16[1024,128]{1,0:T(8,128)(2,1)}, u32[]{:S(2)}, u32[]{:S(2)}) collective-permute-start(bf16[1024,128]{1,0:T(8,128)(2,1)} %maximum_select_fusion.x), channel_id=1, source_target_pairs={{0,4},{4,0},{1,5},{5,1},{2,6},{6,2},{3,7},{7,3},{8,12},{12,8},{9,1... | collective-permute-start | bytes 786440 | tf_op jit(solution)/shard_map/ppermute | solution.py:18
  61.5 26.6 %all-to-all-start.1 = ((bf16[8,64,256]{2,1,0:T(8,128)(2,1)}), bf16[8,64,256]{2,1,0:T(8,128)(2,1)}, u32[]{:S(2)}, u32[]{:S(2)}) async-start(bf16[8,64,256]{2,1,0:T(8,128)(2,1)} %broadcast_in_dim.53), calls=%async_computation.1 | async-start | bytes 524288 | tf_op jit(solution)/shard_map/all_to_all | solution.py:46
  68.5 19.5 %collective-permute-start.21 = (bf16[2,256,128]{2,1,0:T(8,128)(2,1)}, bf16[2,256,128]{2,1,0:T(8,128)(2,1)S(1)}, u32[]{:S(2)}, u32[]{:S(2)}) collective-permute-start(bf16[2,256,128]{2,1,0:T(8,128)(2,1)} %param.15), channel_id=1, source_target_pairs={{0,0},{128,1},{144,2},{16,3},{130,16},{2,17},{18,18},{146,19},{1,1... | collective-permute-start | bytes 393224 | tf_op jit(solution)/shard_map/ppermute | solution.py:42
  75.9 19.5 %collective-permute-start.6 = (bf16[1024,128]{1,0:T(8,128)(2,1)}, bf16[1024,128]{1,0:T(8,128)(2,1)}, u32[]{:S(2)}, u32[]{:S(2)}) collective-permute-start(bf16[1024,128]{1,0:T(8,128)(2,1)} %maximum_select_fusion.x), channel_id=1, source_target_pairs={{0,16},{16,0},{1,17},{17,1},{2,18},{18,2},{3,19},{19,3},{4,20},{20... | collective-permute-start | bytes 786440 | tf_op jit(solution)/shard_map/ppermute | solution.py:18
  75.9 19.5 %collective-permute-start.8 = (bf16[1024,128]{1,0:T(8,128)(2,1)}, bf16[1024,128]{1,0:T(8,128)(2,1)S(1)}, u32[]{:S(2)}, u32[]{:S(2)}) collective-permute-start(bf16[1024,128]{1,0:T(8,128)(2,1)} %maximum_select_fusion.x), channel_id=1, source_target_pairs={{0,8},{8,0},{1,9},{9,1},{2,10},{10,2},{3,11},{11,3},{4,12},{12,4},... | collective-permute-start | bytes 786440 | tf_op jit(solution)/shard_map/ppermute | solution.py:18
  79.1 13.5 %collective-permute-start.14 = (bf16[256,512]{1,0:T(8,128)(2,1)}, bf16[256,512]{1,0:T(8,128)(2,1)S(1)}, u32[]{:S(2)}, u32[]{:S(2)}) collective-permute-start(bf16[256,512]{1,0:T(8,128)(2,1)} %get-tuple-element.39), channel_id=1, source_target_pairs={{0,0},{128,1},{144,2},{16,3},{130,16},{2,17},{18,18},{146,19},{1,1... | collective-permute-start | bytes 786440 | tf_op jit(solution)/shard_map/ppermute | solution.py:42
  82.0 13.5 %collective-permute-start.15 = (bf16[512,256]{1,0:T(8,128)(2,1)}, bf16[512,256]{1,0:T(8,128)(2,1)S(1)}, u32[]{:S(2)}, u32[]{:S(2)}) collective-permute-start(bf16[512,256]{1,0:T(8,128)(2,1)} %get-tuple-element.40), channel_id=1, source_target_pairs={{0,0},{128,1},{144,2},{16,3},{130,16},{2,17},{18,18},{146,19},{1,1... | collective-permute-start | bytes 786440 | tf_op jit(solution)/shard_map/ppermute | solution.py:42
  108.5 14.3 %collective-permute-start.19 = (bf16[1024,128]{1,0:T(8,128)(2,1)}, bf16[1024,128]{1,0:T(8,128)(2,1)}, u32[]{:S(2)}, u32[]{:S(2)}) collective-permute-start(bf16[1024,128]{1,0:T(8,128)(2,1)} %get-tuple-element.45), channel_id=1, source_target_pairs={{0,8},{8,0},{1,9},{9,1},{2,10},{10,2},{3,11},{11,3},{4,12},{12,4},... | collective-permute-start | bytes 786440 | tf_op jit(solution)/shard_map/ppermute | solution.py:18
  113.0 16.1 %all-to-all-start.2 = ((bf16[8,80,256]{2,1,0:T(8,128)(2,1)}), bf16[8,80,256]{2,1,0:T(8,128)(2,1)S(1)}, u32[]{:S(2)}, u32[]{:S(2)}) async-start(bf16[8,80,256]{2,1,0:T(8,128)(2,1)} %pad_maximum_fusion.1), calls=%async_computation.2 | async-start | bytes 655360 | tf_op jit(solution)/shard_map/all_to_all | solution.py:179
  130.0 17.7 %all-to-all-start.3 = ((bf16[8,144,256]{2,1,0:T(8,128)(2,1)}), bf16[8,144,256]{2,1,0:T(8,128)(2,1)}, u32[]{:S(2)}, u32[]{:S(2)}) async-start(bf16[8,144,256]{2,1,0:T(8,128)(2,1)} %pad_maximum_fusion), calls=%async_computation.3 | async-start | bytes 1179648 | tf_op jit(solution)/shard_map/all_to_all | solution.py:282
  134.3 19.7 %collective-permute-start.30 = (bf16[1,4,320,128]{3,2,1,0:T(8,128)(2,1)}, bf16[1,4,320,128]{3,2,1,0:T(8,128)(2,1)}, u32[]{:S(2)}, u32[]{:S(2)}) collective-permute-start(bf16[1,4,320,128]{3,2,1,0:T(8,128)(2,1)} %bitcast.38), channel_id=1, source_target_pairs={{0,64},{32,96},{64,0},{96,32},{1,65},{33,97},{65,1},{97,33},{2,66}... | collective-permute-start | bytes 983048 | tf_op jit(solution)/shard_map/ppermute | solution.py:218
  136.2 22.7 %collective-permute-start.32 = (bf16[256,512]{1,0:T(8,128)(2,1)}, bf16[256,512]{1,0:T(8,128)(2,1)}, u32[]{:S(2)}, u32[]{:S(2)}) collective-permute-start(bf16[256,512]{1,0:T(8,128)(2,1)} %get-tuple-element.50), channel_id=1, source_target_pairs={{0,0},{128,1},{144,2},{16,3},{130,16},{2,17},{18,18},{146,19},{1,1... | collective-permute-start | bytes 786440 | tf_op jit(solution)/shard_map/ppermute | solution.py:42
  139.6 19.4 %collective-permute-start.33 = (bf16[512,256]{1,0:T(8,128)(2,1)}, bf16[512,256]{1,0:T(8,128)(2,1)}, u32[]{:S(2)}, u32[]{:S(2)}) collective-permute-start(bf16[512,256]{1,0:T(8,128)(2,1)} %get-tuple-element.51), channel_id=1, source_target_pairs={{0,0},{128,1},{144,2},{16,3},{130,16},{2,17},{18,18},{146,19},{1,1... | collective-permute-start | bytes 786440 | tf_op jit(solution)/shard_map/ppermute | solution.py:42
  159.7 14.6 %all-to-all-start.4 = ((bf16[8,64,256]{2,1,0:T(8,128)(2,1)}), bf16[8,64,256]{2,1,0:T(8,128)(2,1)}, u32[]{:S(2)}, u32[]{:S(2)}) async-start(bf16[8,64,256]{2,1,0:T(8,128)(2,1)} %broadcast_in_dim.55), calls=%async_computation.4 | async-start | bytes 524288 | tf_op jit(solution)/shard_map/all_to_all | solution.py:46
  171.9 14.5 %collective-permute-start.28 = (bf16[1024,128]{1,0:T(8,128)(2,1)S(1)}, bf16[1024,128]{1,0:T(8,128)(2,1)S(1)}, u32[]{:S(2)}, u32[]{:S(2)}) collective-permute-start(bf16[1024,128]{1,0:T(8,128)(2,1)S(1)} %fusion.1.x), channel_id=1, source_target_pairs={{0,8},{8,0},{1,9},{9,1},{2,10},{10,2},{3,11},{11,3},{4,12},{12,4},... | collective-permute-start | bytes 786440 | tf_op jit(solution)/shard_map/ppermute | solution.py:18
  231.1 14.4 %collective-permute-start.41 = (bf16[1024,128]{1,0:T(8,128)(2,1)S(1)}, bf16[1024,128]{1,0:T(8,128)(2,1)S(1)}, u32[]{:S(2)}, u32[]{:S(2)}) collective-permute-start(bf16[1024,128]{1,0:T(8,128)(2,1)S(1)} %maximum_select_fusion.1), channel_id=1, source_target_pairs={{0,0},{128,1},{16,2},{144,3},{2,16},{130,17},{18,18},{146,19},{1,1... | collective-permute-start | bytes 786440 | tf_op jit(solution)/shard_map/ppermute | solution.py:34
  (50 other events, 509.0 us)

commit v3 on v2

v3 whole, which is shorter than its diff:
```python
import functools

import jax
import jax.numpy as jnp
from jax import lax
from jax.experimental import pallas as pl
from jax.experimental.pallas import tpu as pltpu
from jax.sharding import Mesh, PartitionSpec as P

BF = jnp.bfloat16
F32 = jnp.float32
TOK = ("zl", "y1", "y0", "core")
FEAT = ("x1", "x0", "zh1", "zh0")
SWAPPED = ("zl", "core", "zh1", "zh0")
BIT_AXES = ("zl", "core", "x0", "x1")
CUBE = ("x1", "x0", "zl")


def pair(value, axis):
    return lax.ppermute(value, axis, [(0, 1), (1, 0)])


def bits(i):
    return i >> 3 & 1, i >> 2 & 1, i >> 1 & 1, i & 1


def index(zl, core, zh1, zh0):
    return zl << 3 | core << 2 | zh1 << 1 | zh0


def swap(value, k0=0, k1=0):
    perm = []
    for dst in range(16):
        zl, core, zh1, zh0 = bits(dst)
        perm.append((index(zh0 ^ k0, zh1 ^ k1, core, zl), dst))
    return lax.ppermute(value, SWAPPED, perm)


def swap_copied(value):
    perm = []
    for dst in range(16):
        zl, core, zh1, zh0 = bits(dst)
        perm.append((index(zh0 ^ zh1 ^ core, zh1, core, zl), dst))
    return lax.ppermute(value, SWAPPED, perm)


def copied_all_to_all(value, count, axes):
    return lax.all_to_all(jnp.broadcast_to(value[None], (count,) + value.shape), axes, 0, 0)


def after(value, *others):
    return lax.optimization_barrier((value,) + others)[0]


def nt_dot(left, right):
    return lax.dot_general(left, right, (((1,), (1,)), ((), ())), preferred_element_type=F32)


def dot(left, right):
    return jnp.dot(left, right, preferred_element_type=F32)


TILE = 256
TILES = 4
TOKENS = TILE * TILES
HALF = TOKENS // 2
WIDTH = 128
HIDDEN = 512
RANK = 256
CHUNK = HALF // 8
SMALL = RANK // 16
LIMIT = pltpu.CompilerParams(vmem_limit_bytes=56 << 20)


def ordered(rows):
    core = lax.axis_index("core")
    half = rows.shape[0] // 2
    return jnp.where(core == 0, rows, jnp.concatenate([rows[half:], rows[:half]], axis=0))


def prep_kernel(
    layer, bits, y, own, before, ahead, far0, far1, up_w, down_w, rank_up, rank_down
):
    whole = [
        (step, zl, ref, zl * 2) for step, ref in ((0, own), (3, before), (1, ahead)) for zl in range(2)
    ]
    pairs = whole + [(2, 0, far0, 0), (2, 1, far1, 0)]
    for step, zl, cols, first in pairs:
        chip = (y[0] + step) % 4
        for core in range(2):
            t = zl * 8 + chip * 2 + core
            piece = cols.at[first + core]
            for i in range(4):
                rank_up[pl.ds(pl.multiple_of(t * 16, 16), 16), i * 128 : (i + 1) * 128] = piece[
                    320 + i * 16 : 336 + i * 16, :
                ]
            for i in range(2):
                rank_down[pl.ds(pl.multiple_of(t * 32, 32), 32), i * 128 : (i + 1) * 128] = piece[
                    384 + i * 32 : 416 + i * 32, :
                ]
    for place in range(5):
        level = jnp.int32(0)
        if place > 0:
            for i in range(4):
                level = level + jnp.where(bits[layer, i] == place - 1, jnp.int32(1 + i), 0)
        at = pl.multiple_of(level * 32, 32)
        for step, zl, cols, first in pairs:
            chip = (y[0] + step) % 4
            pieces = []
            for core in range(2):
                t = zl * 8 + chip * 2 + core
                up_w[
                    pl.ds(pl.multiple_of(t * 32, 32), 32), place * WIDTH : (place + 1) * WIDTH
                ] = cols[first + core, pl.ds(at, 32), :]
                pieces.append(cols[first + core, pl.ds(160 + at, 32), :].astype(F32))
            top = pl.multiple_of(place * WIDTH + zl * 64 + chip * 16, 16)
            for q in range(4):
                down_w[pl.ds(top, 16), q * 128 : (q + 1) * 128] = jnp.concatenate(
                    [piece[q * 8 : (q + 1) * 8] for piece in pieces], axis=0
                ).astype(BF)


def prep(layer, level_bits, planes):
    y = lax.axis_index(("y1", "y0")).astype(jnp.int32).reshape(1)
    shapes = [(HIDDEN, 5 * WIDTH), (5 * WIDTH, HIDDEN), (RANK, HIDDEN), (HIDDEN, RANK)]
    return pl.pallas_call(
        functools.partial(prep_kernel, layer),
        grid_spec=pltpu.PrefetchScalarGridSpec(
            num_scalar_prefetch=2,
            grid=(1,),
            in_specs=[
                pl.BlockSpec(plane.shape, lambda i, *_: (0, 0, 0)) for plane in planes
            ],
            out_specs=[pl.BlockSpec(shape, lambda i, *_: (0, 0)) for shape in shapes],
        ),
        out_shape=[jax.ShapeDtypeStruct(shape, BF) for shape in shapes],
        compiler_params=LIMIT,
        cost_estimate=pl.CostEstimate(flops=2 << 30, bytes_accessed=6 << 20, transcendentals=0),
        name="prep",
    )(level_bits, y, *planes)


def gelu(value):
    return 0.5 * value * (1.0 + lax.erf(value * (0.5**0.5)))


def mlp_kernel(
    x, p_zl, p_core, p_x0, p_x1, mine, other, up_w, down_w, rank_up, rank_down, *rest
):
    small, (mine_back, other_back, own, t_zl, t_core, t_x0, t_x1) = rest[:-7], rest[-7:]
    i = pl.program_id(0)
    value = x[...]
    left = jnp.concatenate([value, p_zl[...], p_core[...], p_x0[...], p_x1[...]], axis=1)
    latent = jnp.where(i < 2, mine[...], other[...])
    pre = nt_dot(left, up_w[...]) + dot(latent, rank_up[...])
    hidden = gelu(pre).astype(BF)
    share = dot(hidden, rank_down[...]).astype(BF).reshape(TILE // CHUNK, CHUNK, RANK)
    for half, back in enumerate((mine_back, other_back)):

        @pl.when(i // 2 == half)
        def _():
            back[:, :CHUNK] = share
            if small:
                back[:, CHUNK:] = small[half][...]

    terms = nt_dot(hidden, down_w[...])
    own[...] = value.astype(F32) + terms[:, :WIDTH]
    for bit, out in enumerate((t_zl, t_core, t_x0, t_x1)):
        out[...] = terms[:, (1 + bit) * WIDTH : (2 + bit) * WIDTH].astype(BF)


def mlp(x, partners, latent, weights, small):
    row = pl.BlockSpec((TILE, WIDTH), lambda i: (i, 0))
    partner_row = pl.BlockSpec((TILE, WIDTH), lambda i: ((i + 2) % TILES, 0))
    halves = lambda n: [
        pl.BlockSpec((TILE // CHUNK, n, RANK), lambda i: (jnp.minimum(i, 1), 0, 0)),
        pl.BlockSpec((TILE // CHUNK, n, RANK), lambda i: (jnp.maximum(i - 2, 0), 0, 0)),
    ]
    latents = [
        pl.BlockSpec((TILE, RANK), lambda i: (jnp.minimum(i, 1), 0)),
        pl.BlockSpec((TILE, RANK), lambda i: (jnp.maximum(i - 2, 0), 0)),
    ]
    whole = lambda *shape: pl.BlockSpec(shape, lambda i: (0,) * len(shape))
    shape = jax.ShapeDtypeStruct
    rows = CHUNK + (SMALL if small else 0)
    return pl.pallas_call(
        mlp_kernel,
        grid=(TILES,),
        in_specs=[row, row, partner_row, row, row]
        + latents
        + [
            whole(HIDDEN, 5 * WIDTH),
            whole(5 * WIDTH, HIDDEN),
            whole(RANK, HIDDEN),
            whole(HIDDEN, RANK),
        ]
        + (halves(SMALL) if small else []),
        out_specs=halves(rows) + [row] * 5,
        out_shape=[shape((8, rows, RANK), BF)] * 2
        + [shape((TOKENS, WIDTH), F32)]
        + [shape((TOKENS, WIDTH), BF)] * 4,
        compiler_params=LIMIT,
        cost_estimate=pl.CostEstimate(
            flops=4 * TOKENS * HIDDEN * (5 * WIDTH + RANK),
            bytes_accessed=6 << 20,
            transcendentals=0,
        ),
        name="mlp",
    )(x, *partners, *latent, *weights, *small)


def split_kernel(got, back, small, latent):
    back[...] = got[:, :CHUNK]
    small[...] = got[:, CHUNK : CHUNK + SMALL]
    total = got[0, CHUNK + SMALL :].astype(F32)
    for i in range(1, 8):
        total = total + got[i, CHUNK + SMALL :].astype(F32)
    latent[...] = total


def split(got):
    shapes = [(8, CHUNK, RANK), (8, SMALL, RANK), (CHUNK, RANK)]
    whole = lambda shape: pl.BlockSpec(shape, lambda i: (0,) * len(shape))
    return pl.pallas_call(
        split_kernel,
        grid=(1,),
        in_specs=[whole(got.shape)],
        out_specs=[whole(shape) for shape in shapes],
        out_shape=[jax.ShapeDtypeStruct(s, t) for s, t in zip(shapes, (BF, BF, F32))],
        compiler_params=LIMIT,
        cost_estimate=pl.CostEstimate(flops=1 << 20, bytes_accessed=1 << 20, transcendentals=0),
        name="split",
    )(got)


def chip_sums(parts):
    return jnp.sum(lax.all_to_all(parts, CUBE, 0, 0).astype(F32), axis=0)


def core_sum(mine, other):
    return mine.astype(F32) + pair(other.astype(BF), "core").astype(F32)


def share_of_core(rows):
    core = lax.axis_index("core")
    half = rows.shape[0] // 2
    return (
        lax.dynamic_slice_in_dim(rows, core * half, half, 0),
        lax.dynamic_slice_in_dim(rows, (1 - core) * half, half, 0),
    )


def pack_kernel(t, cols, up_rows, down_rows, out):
    del t
    out[:, :320] = cols[...]
    for i in range(4):
        out[:, 320 + i * 16 : 336 + i * 16] = up_rows[:, :, i * 128 : (i + 1) * 128]
    for i in range(2):
        out[:, 384 + i * 32 : 416 + i * 32] = down_rows[:, :, i * 128 : (i + 1) * 128]


def block_shards(up_blocks, down_blocks, rank_up, rank_down):
    layers = up_blocks.shape[0]
    t = lax.axis_index(TOK)
    up_shard = up_blocks[:, 0].transpose(0, 1, 3, 2).reshape(layers, 160, 128)
    down_shard = down_blocks[:, 0].reshape(layers, 5, 4, 128, 8).transpose(0, 1, 2, 4, 3)
    cols = jnp.concatenate([up_shard, down_shard.reshape(layers, 160, 128)], axis=1)
    shape = (layers, 448, 128)
    return pl.pallas_call(
        pack_kernel,
        grid_spec=pltpu.PrefetchScalarGridSpec(
            num_scalar_prefetch=1,
            grid=(1,),
            in_specs=[
                pl.BlockSpec(cols.shape, lambda i, t: (0, 0, 0)),
                pl.BlockSpec((layers, 16, HIDDEN), lambda i, t: (0, t[0], 0)),
                pl.BlockSpec((layers, 32, RANK), lambda i, t: (0, t[0], 0)),
            ],
            out_specs=pl.BlockSpec(shape, lambda i, t: (0, 0, 0)),
        ),
        out_shape=jax.ShapeDtypeStruct(shape, BF),
        compiler_params=LIMIT,
        cost_estimate=pl.CostEstimate(flops=1 << 20, bytes_accessed=1 << 19, transcendentals=0),
        name="pack",
    )(t.astype(jnp.int32).reshape(1), cols, rank_up, rank_down)


def gather_planes(shards):
    zh0, zh1 = lax.axis_index("zh0"), lax.axis_index("zh1")
    outs = [jnp.zeros((4,) + shards.shape[1:], shards.dtype)] * shards.shape[0]
    for k0 in range(2):
        for k1 in range(2):
            got = swap(shards, k0, k1)
            at = (zh0 ^ k0) * 2 + (zh1 ^ k1)
            outs = [
                lax.dynamic_update_slice(out, got[i : i + 1], (at, 0, 0))
                for i, out in enumerate(outs)
            ]
    return outs


def along_y(value, step):
    return lax.ppermute(value, ("y1", "y0"), [(i, (i + step) % 4) for i in range(4)])


def near_columns(plane):
    return [plane, along_y(plane, 1), along_y(plane, -1)]


def far_columns(before, ahead):
    return [along_y(before[:2], 1), along_y(ahead[2:], -1)]


def low_rank_part(x, rows_in):
    other = dot(x[HALF:], rows_in)
    return core_sum(dot(x[:HALF], rows_in), other).astype(BF).reshape(8, HALF // 8, RANK)


def exchange(blocks):
    return [pair(value, axis) for value, axis in zip(blocks, BIT_AXES)]


def per_device(tokens, level_bits, up_blocks, down_blocks, rank_in, rank_up, rank_down, rank_out):
    layers = level_bits.shape[0]
    core = lax.axis_index("core")
    block = lax.axis_index("x1") * 8 + lax.axis_index("x0") * 4 + core * 2 + lax.axis_index("zl")
    rows_in = lax.dynamic_slice(rank_in, (0, block * WIDTH, 0), (layers, WIDTH, RANK))
    planes = gather_planes(block_shards(up_blocks, down_blocks, rank_up, rank_down))
    x = ordered(swap(tokens))
    partners = exchange([x] * 4)
    parts, rank_out, *planes = lax.optimization_barrier(
        (low_rank_part(x, rows_in[0]), swap_copied(rank_out), *planes)
    )
    near = near_columns(planes[0])
    share = chip_sums(parts).astype(BF)
    share = after(share, *near, partners[0], partners[2])
    gathered = [near + far_columns(*near[1:])]
    latent = copied_all_to_all(share, 8, CUBE).reshape(HALF, RANK)
    for layer in range(layers):
        last = layer == layers - 1
        cols = lax.optimization_barrier((x, *gathered[layer]))[1:]
        weights = prep(layer, level_bits, cols)
        if layer == 0:
            latent = after(latent, *weights)
        small = []
        if not last:
            small = share_of_core(dot(rank_out[layer], rows_in[layer + 1]).astype(BF))
            small = [part.reshape(8, SMALL, RANK) for part in small]
        mine, other, own, *terms = mlp(
            x, partners, (latent, pair(latent, "core")), weights, small
        )
        parts = core_sum(mine, other).astype(BF)
        terms = exchange(terms)
        if not last:
            near = near_columns(after(planes[layer + 1], latent))
        share = chip_sums(parts).astype(BF)
        if not last:
            share, own = lax.optimization_barrier((share, own))
            share = after(share, *near)
            gathered.append(near + far_columns(*near[1:]))
        t_zl, t_core, t_x0, t_x1 = terms
        t_core = jnp.concatenate([t_core[HALF:], t_core[:HALF]], axis=0)
        if last:
            share = after(share, terms[0], terms[3])
            back = copied_all_to_all(share, 8, CUBE)
        for term in (t_zl, t_core, t_x0, t_x1):
            own = own + term.astype(F32)
        if not last:
            parts = low_rank_part(own.astype(BF), rows_in[layer + 1])
            got = lax.all_to_all(
                jnp.concatenate(
                    [jnp.broadcast_to(share[None], (8,) + share.shape), parts], axis=1
                ),
                CUBE, 0, 0,
            )
            back, small, latent = split(after(got, *gathered[layer + 1]))
            small = small.reshape(RANK // 2, RANK)
            small = ordered(jnp.concatenate([small, pair(small, "core")], axis=0))
            back = back.reshape(HALF, RANK)
            back = jnp.concatenate([back, pair(back, "core")], axis=0)
            x = (own + dot(back, rank_out[layer])).astype(BF)
            partners = exchange([x] * 4)
            latent = after(latent, x)
            latent = (latent + dot(share[:CHUNK], small)).astype(BF)
            latent = copied_all_to_all(latent, 8, CUBE).reshape(HALF, RANK)
    back = back.reshape(HALF, RANK)
    back = jnp.concatenate([back, pair(back, "core")], axis=0)
    x = (own + dot(back, rank_out[layers - 1])).astype(BF)
    return swap(ordered(x))


def solution(mesh):
    fine = Mesh(mesh.devices.reshape((2,) * 8), TOK + FEAT)
    return jax.shard_map(
        per_device,
        mesh=fine,
        in_specs=(
            P(TOK, FEAT),
            P(),
            P(None, FEAT, None, None, TOK),
            P(None, FEAT, None, None, TOK),
            P(),
            P(None, None, FEAT),
            P(None, FEAT, None),
            P(None, None, FEAT),
        ),
        out_specs=P(TOK, FEAT),
        check_vma=False,
    )
```

time: 248 us -> 229 us (0.923)
  local copies, waits for them, and re-layouts: 25.5 us -> 15 us
  between operations: 5.84 us -> 0.46 us
  Pallas kernels: 21.4 us -> 25.8 us
  other arithmetic: 10.8 us -> 7.62 us
  starting transfers between devices: 123 us -> 120 us
    ppermute x6, waiting for transfers between devices: 19.2 us -> 5.35 us  [swap(): return lax.ppermute(value, SWAPPED, perm)]
    ppermute x5 -> x1, starting transfers between devices: 23.8 us -> 11.9 us  [swap_copied(): return lax.ppermute(value, SWAPPED, perm)]
    ppermute x25, waiting for transfers between devices: 20.6 us -> 32.2 us  [pair(): return lax.ppermute(value, axis, [(0, 1), (1, 0)])]
    dynamic_update_slice x12 -> x5, local copies, waits for them, and re-layouts: 9.13 us -> 3.62 us  [gather_planes(): lax.dynamic_update_slice(out, got[i:i + 1], (at, 0, 0))]
    pallas_call x2 -> x4, Pallas kernels: 6.59 us -> 11 us  [the longest x2 7.55 us: prep(): pl.pallas_call(functools.partial(prep_kernel, layer), grid_spec=pltpu.Pre...]
    ppermute x6, starting transfers between devices: 24 us -> 27.9 us  [swap(): return lax.ppermute(value, SWAPPED, perm)]
    all_to_all x3, starting transfers between devices: 10.9 us -> 14.8 us  [chip_sums(): return jnp.sum(lax.all_to_all(parts, CUBE, 0, 0).astype(F32), axis=0)]
    squeeze x3 -> x0, local copies, waits for them, and re-layouts: 3.69 us -> none  [the longest x2 2.77 us: per_device(): value[layer + 1]]
  transfers between devices with their start and end apart: 49 -> 47, of which waited for: 16 -> 22; matrix products, arithmetic and copies ran while one was open for 12% -> 6% of each run, Pallas kernels for 6% -> 3%
where the time goes in v3:
time: 229 us; the launch traced here: 228 us
  starting transfers between devices  120 us (52%)
  waiting for transfers between devices  52.6 us (23%)
  Pallas kernels  25.8 us (11%)
  local copies, waits for them, and re-layouts  15 us (7%)
  other arithmetic  7.62 us (3%)
  matrix products  5.75 us (3%)
    ppermute x25, starting transfers between devices, pair(): return lax.ppermute(value, axis, [(0, 1), (1, 0)])  37.3 us
    ppermute x25, waiting for transfers between devices, pair(): return lax.ppermute(value, axis, [(0, 1), (1, 0)])  32.2 us
    ppermute x6, starting transfers between devices, swap(): return lax.ppermute(value, SWAPPED, perm)  27.9 us
    pallas_call x2, Pallas kernels, mlp(): pl.pallas_call(mlp_kernel, grid=(TILES,), in_specs=[row, row, partner_row...  14.8 us
    all_to_all x3, starting transfers between devices, chip_sums(): return jnp.sum(lax.all_to_all(parts, CUBE, 0, 0).astype(F32), axis=0)  14.8 us
    all_to_all x3, starting transfers between devices, copied_all_to_all(): lax.all_to_all(jnp.broadcast_to(value[None], (count,) + value.shape), axe...  13 us
    ppermute x1, starting transfers between devices, swap_copied(): return lax.ppermute(value, SWAPPED, perm)  11.9 us
    ppermute x8, starting transfers between devices, along_y(): lax.ppermute(value, ('y1', 'y0'), [(i, (i + step) % 4) for i in range(4)])  11.2 us
  transfers between devices with their start and end apart: 47, of which 22 were waited for; matrix products, arithmetic and copies ran while one was open for 6% of the time, Pallas kernels for 3%

profile of v3, /device:TPU:1, one launch (start us, length us, event | category | flops | bytes accessed | tf_op | source)
XLA Modules:
  0.0 227.7 jit_solution(13254221711600489414)
XLA Ops:
  3.4 10.2 %collective-permute-start.7 = (bf16[2,448,128]{2,1,0:T(8,128)(2,1)}, bf16[2,448,128]{2,1,0:T(8,128)(2,1)S(1)}, u32[]{:S(2)}, u32[]{:S(2)}) collective-permute-start(bf16[2,448,128]{2,1,0:T(8,128)(2,1)} %pack.1), channel_id=1, source_target_pairs={{0,0},{128,1},{16,2},{144,3},{2,16},{130,17},{18,18},{146,19},{1,1... | collective-permute-start | bytes 688136 | tf_op jit(solution)/shard_map/ppermute | solution.py:36
  17.1 6.1 %collective-permute-start = (bf16[1024,128]{1,0:T(8,128)(2,1)}, bf16[1024,128]{1,0:T(8,128)(2,1)S(1)}, u32[]{:S(2)}, u32[]{:S(2)}) collective-permute-start(bf16[1024,128]{1,0:T(8,128)(2,1)} %param.8), channel_id=1, source_target_pairs={{0,0},{128,1},{16,2},{144,3},{2,16},{130,17},{18,18},{146,19},{1,1... | collective-permute-start | bytes 786440 | tf_op jit(solution)/shard_map/ppermute | solution.py:36
  23.2 11.9 %collective-permute-start.6 = (bf16[2,256,128]{2,1,0:T(8,128)(2,1)}, bf16[2,256,128]{2,1,0:T(8,128)(2,1)}, u32[]{:S(2)}, u32[]{:S(2)}) collective-permute-start(bf16[2,256,128]{2,1,0:T(8,128)(2,1)} %param.15), channel_id=1, source_target_pairs={{0,0},{128,1},{144,2},{16,3},{130,16},{2,17},{18,18},{146,19},{1,1... | collective-permute-start | bytes 393224 | tf_op jit(solution)/shard_map/ppermute | solution.py:44
  42.5 6.2 %all-to-all-start = ((bf16[8,64,256]{2,1,0:T(8,128)(2,1)}), bf16[8,64,256]{2,1,0:T(8,128)(2,1)S(1)}, u32[]{:S(2)}, u32[]{:S(2)}) async-start(bf16[8,64,256]{2,1,0:T(8,128)(2,1)} %bitcast.1), calls=%async_computation | async-start | bytes 524288 | tf_op jit(solution)/shard_map/all_to_all | solution.py:237
  55.4 3.5 %collective-permute-done.1.p_zl = bf16[1024,128]{1,0:T(8,128)(2,1)} collective-permute-done((bf16[1024,128]{1,0:T(8,128)(2,1)S(1)}, bf16[1024,128]{1,0:T(8,128)(2,1)}, u32[]{:S(2)}, u32[]{:S(2)}) %collective-permute-start.1) | collective-permute-done | bytes 262176 | tf_op jit(solution)/shard_map/ppermute | solution.py:20
  62.4 4.8 %all-to-all-start.1 = ((bf16[8,64,256]{2,1,0:T(8,128)(2,1)}), bf16[8,64,256]{2,1,0:T(8,128)(2,1)S(1)}, u32[]{:S(2)}, u32[]{:S(2)}) async-start(bf16[8,64,256]{2,1,0:T(8,128)(2,1)} %broadcast_in_dim.11), calls=%async_computation.1 | async-start | bytes 524288 | tf_op jit(solution)/shard_map/all_to_all | solution.py:48
  74.5 3.2 %collective-permute-start.4 = (bf16[1024,128]{1,0:T(8,128)(2,1)S(1)}, bf16[1024,128]{1,0:T(8,128)(2,1)}, u32[]{:S(2)}, u32[]{:S(2)}) collective-permute-start(bf16[1024,128]{1,0:T(8,128)(2,1)S(1)} %maximum_select_fusion.x), channel_id=1, source_target_pairs={{0,8},{8,0},{1,9},{9,1},{2,10},{10,2},{3,11},{11,3},{4,12},{12,4},... | collective-permute-start | bytes 786440 | tf_op jit(solution)/shard_map/ppermute | solution.py:20
  77.8 3.8 %prep.2 = (bf16[512,640]{1,0:T(8,128)(2,1)}, bf16[640,512]{1,0:T(8,128)(2,1)}, bf16[256,512]{1,0:T(8,128)(2,1)}, bf16[512,256]{1,0:T(8,128)(2,1)}) custom-call(s32[2,4]{1,0:T(2,128)} %bits.3, s32[1]{0:T(128)} %bitcast.10.y, bf16[4,448,128]{2,1,0:T(8,128)(2,1)} %copy-done.4, bf16[4,448,128]{2,1,0:T(8,128)(2,1)} %collective-permute-done.11.before, ...), custom_call_target="tpu_custom_call" | custom-call | flops 2147483648 | bytes 6291456 | tf_op jit(solution)/shard_map/prep/pallas_call | solution.py:126
  85.3 7.5 %mlp.2 = (bf16[8,80,256]{2,1,0:T(8,128)(2,1)}, bf16[8,80,256]{2,1,0:T(8,128)(2,1)}, f32[1024,128]{1,0:T(8,128)}, bf16[1024,128]{1,0:T(8,128)(2,1)}, bf16[1024,12...) custom-call(bf16[1024,128]{1,0:T(8,128)(2,1)} %copy-done.2, ...), custom_call_target="tpu_custom_call" | custom-call | flops 1879048192 | bytes 6291456 | tf_op jit(solution)/shard_map/mlp/pallas_call | solution.py:186
  96.9 5.2 %all-to-all-start.2 = ((bf16[8,80,256]{2,1,0:T(8,128)(2,1)}), bf16[8,80,256]{2,1,0:T(8,128)(2,1)S(1)}, u32[]{:S(2)}, u32[]{:S(2)}) async-start(bf16[8,80,256]{2,1,0:T(8,128)(2,1)} %add_convert_fusion), calls=%async_computation.2 | async-start | bytes 655360 | tf_op jit(solution)/shard_map/all_to_all | solution.py:237
  110.2 4.6 %collective-permute-done.20 = bf16[1024,128]{1,0:T(8,128)(2,1)S(1)} collective-permute-done((bf16[1024,128]{1,0:T(8,128)(2,1)}, bf16[1024,128]{1,0:T(8,128)(2,1)S(1)}, u32[]{:S(2)}, u32[]{:S(2)}) %collective-permute-start.20) | collective-permute-done | bytes 262176 | tf_op jit(solution)/shard_map/ppermute | solution.py:20
  114.8 5.0 %collective-permute-done.19 = bf16[1024,128]{1,0:T(8,128)(2,1)} collective-permute-done((bf16[1024,128]{1,0:T(8,128)(2,1)}, bf16[1024,128]{1,0:T(8,128)(2,1)}, u32[]{:S(2)}, u32[]{:S(2)}) %collective-permute-start.19) | collective-permute-done | bytes 262176 | tf_op jit(solution)/shard_map/ppermute | solution.py:20
  124.2 4.4 %all-to-all-start.3 = ((bf16[8,144,256]{2,1,0:T(8,128)(2,1)}), bf16[8,144,256]{2,1,0:T(8,128)(2,1)S(1)}, u32[]{:S(2)}, u32[]{:S(2)}) async-start(bf16[8,144,256]{2,1,0:T(8,128)(2,1)} %pad_maximum_fusion), calls=%async_computation.3 | async-start | bytes 1179648 | tf_op jit(solution)/shard_map/all_to_all | solution.py:370
  133.4 4.0 %collective-permute-done.24.far0 = bf16[2,448,128]{2,1,0:T(8,128)(2,1)S(1)} collective-permute-done((bf16[2,448,128]{2,1,0:T(8,128)(2,1)S(1)}, bf16[2,448,128]{2,1,0:T(8,128)(2,1)S(1)}, u32[]{:S(2)}, u32[]{:S(2)}) %collective-permute-start.24) | collective-permute-done | bytes 229408 | tf_op jit(solution)/shard_map/ppermute | solution.py:303
  146.9 4.6 %all-to-all-start.4 = ((bf16[8,64,256]{2,1,0:T(8,128)(2,1)}), bf16[8,64,256]{2,1,0:T(8,128)(2,1)S(1)}, u32[]{:S(2)}, u32[]{:S(2)}) async-start(bf16[8,64,256]{2,1,0:T(8,128)(2,1)} %broadcast_in_dim.13), calls=%async_computation.4 | async-start | bytes 524288 | tf_op jit(solution)/shard_map/all_to_all | solution.py:48
  160.9 3.8 %prep.3 = (bf16[512,640]{1,0:T(8,128)(2,1)}, bf16[640,512]{1,0:T(8,128)(2,1)}, bf16[256,512]{1,0:T(8,128)(2,1)}, bf16[512,256]{1,0:T(8,128)(2,1)}) custom-call(s32[2,4]{1,0:T(2,128)} %bits.3, s32[1]{0:T(128)} %bitcast.10.y, bf16[4,448,128]{2,1,0:T(8,128)(2,1)} %get-tuple-element.84.own, bf16[4,448,128]{2,1,0:T(8,128)(2,1)} %collective-permute-done.21.before, ...), custom_call_target="tpu_custom_call" | custom-call | flops 2147483648 | bytes 6291456 | tf_op jit(solution)/shard_map/prep/pallas_call | solution.py:126
  164.7 5.9 %collective-permute-done.30.p_x1 = bf16[1024,128]{1,0:T(8,128)(2,1)} collective-permute-done((bf16[1024,128]{1,0:T(8,128)(2,1)S(1)}, bf16[1024,128]{1,0:T(8,128)(2,1)}, u32[]{:S(2)}, u32[]{:S(2)}) %collective-permute-start.30) | collective-permute-done | bytes 262176 | tf_op jit(solution)/shard_map/ppermute | solution.py:20
  171.3 7.4 %mlp.3 = (bf16[8,64,256]{2,1,0:T(8,128)(2,1)}, bf16[8,64,256]{2,1,0:T(8,128)(2,1)}, f32[1024,128]{1,0:T(8,128)}, bf16[1024,128]{1,0:T(8,128)(2,1)}, bf16[1024,12...) custom-call(bf16[1024,128]{1,0:T(8,128)(2,1)} %copy-done.9, bf16[1024,128]{1,0:T(8,128)(2,1)} %copy-done.11, ...), custom_call_target="tpu_custom_call" | custom-call | flops 1879048192 | bytes 6291456 | tf_op jit(solution)/shard_map/mlp/pallas_call | solution.py:186
  182.6 3.4 %all-to-all-start.5 = ((bf16[8,64,256]{2,1,0:T(8,128)(2,1)}), bf16[8,64,256]{2,1,0:T(8,128)(2,1)S(1)}, u32[]{:S(2)}, u32[]{:S(2)}) async-start(bf16[8,64,256]{2,1,0:T(8,128)(2,1)} %add_convert_fusion.2), calls=%async_computation.5 | async-start | bytes 524288 | tf_op jit(solution)/shard_map/all_to_all | solution.py:237
  193.0 5.0 %collective-permute-done.36 = bf16[1024,128]{1,0:T(8,128)(2,1)S(1)} collective-permute-done((bf16[1024,128]{1,0:T(8,128)(2,1)}, bf16[1024,128]{1,0:T(8,128)(2,1)S(1)}, u32[]{:S(2)}, u32[]{:S(2)}) %collective-permute-start.36) | collective-permute-done | bytes 262176 | tf_op jit(solution)/shard_map/ppermute | solution.py:20
  198.7 3.5 %all-to-all-start.6 = ((bf16[8,64,256]{2,1,0:T(8,128)(2,1)}), bf16[8,64,256]{2,1,0:T(8,128)(2,1)S(1)}, u32[]{:S(2)}, u32[]{:S(2)}) async-start(bf16[8,64,256]{2,1,0:T(8,128)(2,1)} %broadcast_in_dim.14), calls=%async_computation.6 | async-start | bytes 524288 | tf_op jit(solution)/shard_map/all_to_all | solution.py:48
  205.0 3.4 %all-to-all-done.6 = bf16[8,64,256]{2,1,0:T(8,128)(2,1)S(1)} async-done(((bf16[8,64,256]{2,1,0:T(8,128)(2,1)}), bf16[8,64,256]{2,1,0:T(8,128)(2,1)S(1)}, u32[]{:S(2)}, u32[]{:S(2)}) %all-to-all-start.6) | async-done | bytes 262176 | tf_op jit(solution)/shard_map/all_to_all | solution.py:48
  214.7 8.2 %collective-permute-start.39 = (bf16[1024,128]{1,0:T(8,128)(2,1)S(1)}, bf16[1024,128]{1,0:T(8,128)(2,1)S(1)}, u32[]{:S(2)}, u32[]{:S(2)}) collective-permute-start(bf16[1024,128]{1,0:T(8,128)(2,1)S(1)} %maximum_select_fusion.1), channel_id=1, source_target_pairs={{0,0},{128,1},{16,2},{144,3},{2,16},{130,17},{18,18},{146,19},{1,1... | collective-permute-start | bytes 786440 | tf_op jit(solution)/shard_map/ppermute | solution.py:36
  222.9 4.1 %collective-permute-done.39 = bf16[1024,128]{1,0:T(8,128)(2,1)S(1)} collective-permute-done((bf16[1024,128]{1,0:T(8,128)(2,1)S(1)}, bf16[1024,128]{1,0:T(8,128)(2,1)S(1)}, u32[]{:S(2)}, u32[]{:S(2)}) %collective-permute-start.39) | collective-permute-done | bytes 262176 | tf_op jit(solution)/shard_map/ppermute | solution.py:36
  (153 shorter events, 97.5 us)
Async XLA Ops:
  3.4 19.8 %collective-permute-start.7 = (bf16[2,448,128]{2,1,0:T(8,128)(2,1)}, bf16[2,448,128]{2,1,0:T(8,128)(2,1)S(1)}, u32[]{:S(2)}, u32[]{:S(2)}) collective-permute-start(bf16[2,448,128]{2,1,0:T(8,128)(2,1)} %pack.1), channel_id=1, source_target_pairs={{0,0},{128,1},{16,2},{144,3},{2,16},{130,17},{18,18},{146,19},{1,1... | collective-permute-start | bytes 688136 | tf_op jit(solution)/shard_map/ppermute | solution.py:36
  13.6 23.1 %collective-permute-start.8 = (bf16[2,448,128]{2,1,0:T(8,128)(2,1)}, bf16[2,448,128]{2,1,0:T(8,128)(2,1)}, u32[]{:S(2)}, u32[]{:S(2)}) collective-permute-start(bf16[2,448,128]{2,1,0:T(8,128)(2,1)} %pack.1), channel_id=1, source_target_pairs={{16,0},{144,1},{0,2},{128,3},{18,16},{146,17},{2,18},{130,19},{17,... | collective-permute-start | bytes 688136 | tf_op jit(solution)/shard_map/ppermute | solution.py:36
  13.7 26.3 %collective-permute-start.9 = (bf16[2,448,128]{2,1,0:T(8,128)(2,1)}, bf16[2,448,128]{2,1,0:T(8,128)(2,1)S(1)}, u32[]{:S(2)}, u32[]{:S(2)}) collective-permute-start(bf16[2,448,128]{2,1,0:T(8,128)(2,1)} %pack.1), channel_id=1, source_target_pairs={{128,0},{0,1},{144,2},{16,3},{130,16},{2,17},{146,18},{18,19},{129... | collective-permute-start | bytes 688136 | tf_op jit(solution)/shard_map/ppermute | solution.py:36
  14.0 26.7 %collective-permute-start.10 = (bf16[2,448,128]{2,1,0:T(8,128)(2,1)}, bf16[2,448,128]{2,1,0:T(8,128)(2,1)S(1)}, u32[]{:S(2)}, u32[]{:S(2)}) collective-permute-start(bf16[2,448,128]{2,1,0:T(8,128)(2,1)} %pack.1), channel_id=1, source_target_pairs={{144,0},{16,1},{128,2},{0,3},{146,16},{18,17},{130,18},{2,19},{145... | collective-permute-start | bytes 688136 | tf_op jit(solution)/shard_map/ppermute | solution.py:36
  17.1 22.5 %collective-permute-start = (bf16[1024,128]{1,0:T(8,128)(2,1)}, bf16[1024,128]{1,0:T(8,128)(2,1)S(1)}, u32[]{:S(2)}, u32[]{:S(2)}) collective-permute-start(bf16[1024,128]{1,0:T(8,128)(2,1)} %param.8), channel_id=1, source_target_pairs={{0,0},{128,1},{16,2},{144,3},{2,16},{130,17},{18,18},{146,19},{1,1... | collective-permute-start | bytes 786440 | tf_op jit(solution)/shard_map/ppermute | solution.py:36
  23.2 19.3 %collective-permute-start.6 = (bf16[2,256,128]{2,1,0:T(8,128)(2,1)}, bf16[2,256,128]{2,1,0:T(8,128)(2,1)}, u32[]{:S(2)}, u32[]{:S(2)}) collective-permute-start(bf16[2,256,128]{2,1,0:T(8,128)(2,1)} %param.15), channel_id=1, source_target_pairs={{0,0},{128,1},{144,2},{16,3},{130,16},{2,17},{18,18},{146,19},{1,1... | collective-permute-start | bytes 393224 | tf_op jit(solution)/shard_map/ppermute | solution.py:44
  42.5 12.8 %all-to-all-start = ((bf16[8,64,256]{2,1,0:T(8,128)(2,1)}), bf16[8,64,256]{2,1,0:T(8,128)(2,1)S(1)}, u32[]{:S(2)}, u32[]{:S(2)}) async-start(bf16[8,64,256]{2,1,0:T(8,128)(2,1)} %bitcast.1), calls=%async_computation | async-start | bytes 524288 | tf_op jit(solution)/shard_map/all_to_all | solution.py:237
  48.7 12.9 %collective-permute-start.11 = (bf16[4,448,128]{2,1,0:T(8,128)(2,1)S(1)}, bf16[4,448,128]{2,1,0:T(8,128)(2,1)}, u32[]{:S(2)}, u32[]{:S(2)}) collective-permute-start(bf16[4,448,128]{2,1,0:T(8,128)(2,1)S(1)} %get-tuple-element.56.own), channel_id=1, source_target_pairs={{0,32},{32,64},{64,96},{96,0},{1,33},{33,65},{65,97},{97,1},{2,34}... | collective-permute-start | bytes 1376264 | tf_op jit(solution)/shard_map/ppermute | solution.py:303
  50.0 11.7 %collective-permute-start.12 = (bf16[4,448,128]{2,1,0:T(8,128)(2,1)S(1)}, bf16[4,448,128]{2,1,0:T(8,128)(2,1)}, u32[]{:S(2)}, u32[]{:S(2)}) collective-permute-start(bf16[4,448,128]{2,1,0:T(8,128)(2,1)S(1)} %get-tuple-element.56.own), channel_id=1, source_target_pairs={{0,96},{32,0},{64,32},{96,64},{1,97},{33,1},{65,33},{97,65},{2,98}... | collective-permute-start | bytes 1376264 | tf_op jit(solution)/shard_map/ppermute | solution.py:303
  62.4 19.2 %all-to-all-start.1 = ((bf16[8,64,256]{2,1,0:T(8,128)(2,1)}), bf16[8,64,256]{2,1,0:T(8,128)(2,1)S(1)}, u32[]{:S(2)}, u32[]{:S(2)}) async-start(bf16[8,64,256]{2,1,0:T(8,128)(2,1)} %broadcast_in_dim.11), calls=%async_computation.1 | async-start | bytes 524288 | tf_op jit(solution)/shard_map/all_to_all | solution.py:48
  72.0 12.6 %collective-permute-start.2 = (bf16[1024,128]{1,0:T(8,128)(2,1)S(1)}, bf16[1024,128]{1,0:T(8,128)(2,1)}, u32[]{:S(2)}, u32[]{:S(2)}) collective-permute-start(bf16[1024,128]{1,0:T(8,128)(2,1)S(1)} %maximum_select_fusion.x), channel_id=1, source_target_pairs={{0,16},{16,0},{1,17},{17,1},{2,18},{18,2},{3,19},{19,3},{4,20},{20... | collective-permute-start | bytes 786440 | tf_op jit(solution)/shard_map/ppermute | solution.py:20
  96.9 13.2 %all-to-all-start.2 = ((bf16[8,80,256]{2,1,0:T(8,128)(2,1)}), bf16[8,80,256]{2,1,0:T(8,128)(2,1)S(1)}, u32[]{:S(2)}, u32[]{:S(2)}) async-start(bf16[8,80,256]{2,1,0:T(8,128)(2,1)} %add_convert_fusion), calls=%async_computation.2 | async-start | bytes 655360 | tf_op jit(solution)/shard_map/all_to_all | solution.py:237
  102.7 12.1 %collective-permute-start.20 = (bf16[1024,128]{1,0:T(8,128)(2,1)}, bf16[1024,128]{1,0:T(8,128)(2,1)S(1)}, u32[]{:S(2)}, u32[]{:S(2)}) collective-permute-start(bf16[1024,128]{1,0:T(8,128)(2,1)} %get-tuple-element.74), channel_id=1, source_target_pairs={{0,8},{8,0},{1,9},{9,1},{2,10},{10,2},{3,11},{11,3},{4,12},{12,4},... | collective-permute-start | bytes 786440 | tf_op jit(solution)/shard_map/ppermute | solution.py:20
  105.9 13.9 %collective-permute-start.19 = (bf16[1024,128]{1,0:T(8,128)(2,1)}, bf16[1024,128]{1,0:T(8,128)(2,1)}, u32[]{:S(2)}, u32[]{:S(2)}) collective-permute-start(bf16[1024,128]{1,0:T(8,128)(2,1)} %get-tuple-element.73), channel_id=1, source_target_pairs={{0,4},{4,0},{1,5},{5,1},{2,6},{6,2},{3,7},{7,3},{8,12},{12,8},{9,1... | collective-permute-start | bytes 786440 | tf_op jit(solution)/shard_map/ppermute | solution.py:20
  106.2 13.6 %collective-permute-start.17 = (bf16[1024,128]{1,0:T(8,128)(2,1)}, bf16[1024,128]{1,0:T(8,128)(2,1)}, u32[]{:S(2)}, u32[]{:S(2)}) collective-permute-start(bf16[1024,128]{1,0:T(8,128)(2,1)} %get-tuple-element.71), channel_id=1, source_target_pairs={{0,128},{128,0},{1,129},{129,1},{2,130},{130,2},{3,131},{131,3},{4... | collective-permute-start | bytes 786440 | tf_op jit(solution)/shard_map/ppermute | solution.py:20
  107.4 14.5 %collective-permute-start.21 = (bf16[4,448,128]{2,1,0:T(8,128)(2,1)}, bf16[4,448,128]{2,1,0:T(8,128)(2,1)}, u32[]{:S(2)}, u32[]{:S(2)}) collective-permute-start(bf16[4,448,128]{2,1,0:T(8,128)(2,1)} %get-tuple-element.84.own), channel_id=1, source_target_pairs={{0,32},{32,64},{64,96},{96,0},{1,33},{33,65},{65,97},{97,1},{2,34}... | collective-permute-start | bytes 1376264 | tf_op jit(solution)/shard_map/ppermute | solution.py:303
  108.2 13.7 %collective-permute-start.22 = (bf16[4,448,128]{2,1,0:T(8,128)(2,1)}, bf16[4,448,128]{2,1,0:T(8,128)(2,1)}, u32[]{:S(2)}, u32[]{:S(2)}) collective-permute-start(bf16[4,448,128]{2,1,0:T(8,128)(2,1)} %get-tuple-element.84.own), channel_id=1, source_target_pairs={{0,96},{32,0},{64,32},{96,64},{1,97},{33,1},{65,33},{97,65},{2,98}... | collective-permute-start | bytes 1376264 | tf_op jit(solution)/shard_map/ppermute | solution.py:303
  124.2 14.3 %all-to-all-start.3 = ((bf16[8,144,256]{2,1,0:T(8,128)(2,1)}), bf16[8,144,256]{2,1,0:T(8,128)(2,1)S(1)}, u32[]{:S(2)}, u32[]{:S(2)}) async-start(bf16[8,144,256]{2,1,0:T(8,128)(2,1)} %pad_maximum_fusion), calls=%async_computation.3 | async-start | bytes 1179648 | tf_op jit(solution)/shard_map/all_to_all | solution.py:370
  151.5 13.1 %collective-permute-start.27 = (bf16[1024,128]{1,0:T(8,128)(2,1)S(1)}, bf16[1024,128]{1,0:T(8,128)(2,1)S(1)}, u32[]{:S(2)}, u32[]{:S(2)}) collective-permute-start(bf16[1024,128]{1,0:T(8,128)(2,1)S(1)} %fusion.2.x), channel_id=1, source_target_pairs={{0,128},{128,0},{1,129},{129,1},{2,130},{130,2},{3,131},{131,3},{4... | collective-permute-start | bytes 786440 | tf_op jit(solution)/shard_map/ppermute | solution.py:20
  152.9 11.7 %collective-permute-start.28 = (bf16[1024,128]{1,0:T(8,128)(2,1)S(1)}, bf16[1024,128]{1,0:T(8,128)(2,1)S(1)}, u32[]{:S(2)}, u32[]{:S(2)}) collective-permute-start(bf16[1024,128]{1,0:T(8,128)(2,1)S(1)} %fusion.2.x), channel_id=1, source_target_pairs={{0,16},{16,0},{1,17},{17,1},{2,18},{18,2},{3,19},{19,3},{4,20},{20... | collective-permute-start | bytes 786440 | tf_op jit(solution)/shard_map/ppermute | solution.py:20
  155.4 15.2 %collective-permute-start.30 = (bf16[1024,128]{1,0:T(8,128)(2,1)S(1)}, bf16[1024,128]{1,0:T(8,128)(2,1)}, u32[]{:S(2)}, u32[]{:S(2)}) collective-permute-start(bf16[1024,128]{1,0:T(8,128)(2,1)S(1)} %fusion.2.x), channel_id=1, source_target_pairs={{0,8},{8,0},{1,9},{9,1},{2,10},{10,2},{3,11},{11,3},{4,12},{12,4},... | collective-permute-start | bytes 786440 | tf_op jit(solution)/shard_map/ppermute | solution.py:20
  158.2 12.4 %collective-permute-start.32 = (bf16[512,256]{1,0:T(8,128)(2,1)S(1)}, bf16[512,256]{1,0:T(8,128)(2,1)S(1)}, u32[]{:S(2)}, u32[]{:S(2)}) collective-permute-start(bf16[512,256]{1,0:T(8,128)(2,1)S(1)} %bitcast.43), channel_id=1, source_target_pairs={{0,16},{16,0},{1,17},{17,1},{2,18},{18,2},{3,19},{19,3},{4,20},{20... | collective-permute-start | bytes 786440 | tf_op jit(solution)/shard_map/ppermute | solution.py:20
  186.0 12.0 %collective-permute-start.36 = (bf16[1024,128]{1,0:T(8,128)(2,1)}, bf16[1024,128]{1,0:T(8,128)(2,1)S(1)}, u32[]{:S(2)}, u32[]{:S(2)}) collective-permute-start(bf16[1024,128]{1,0:T(8,128)(2,1)} %get-tuple-element.97), channel_id=1, source_target_pairs={{0,8},{8,0},{1,9},{9,1},{2,10},{10,2},{3,11},{11,3},{4,12},{12,4},... | collective-permute-start | bytes 786440 | tf_op jit(solution)/shard_map/ppermute | solution.py:20
  214.7 12.3 %collective-permute-start.39 = (bf16[1024,128]{1,0:T(8,128)(2,1)S(1)}, bf16[1024,128]{1,0:T(8,128)(2,1)S(1)}, u32[]{:S(2)}, u32[]{:S(2)}) collective-permute-start(bf16[1024,128]{1,0:T(8,128)(2,1)S(1)} %maximum_select_fusion.1), channel_id=1, source_target_pairs={{0,0},{128,1},{16,2},{144,3},{2,16},{130,17},{18,18},{146,19},{1,1... | collective-permute-start | bytes 786440 | tf_op jit(solution)/shard_map/ppermute | solution.py:36
  (42 other events, 406.1 us)

commit v4 on v3

--- a/solution.py
+++ b/solution.py
@@ -60,8 +60,8 @@
     return jnp.dot(left, right, preferred_element_type=F32)
 
 
-TILE = 256
-TILES = 4
+TILE = 512
+TILES = 2
 TOKENS = TILE * TILES
 HALF = TOKENS // 2
 WIDTH = 128
@@ -151,13 +151,13 @@
     i = pl.program_id(0)
     value = x[...]
     left = jnp.concatenate([value, p_zl[...], p_core[...], p_x0[...], p_x1[...]], axis=1)
-    latent = jnp.where(i < 2, mine[...], other[...])
+    latent = jnp.where(i < TILES // 2, mine[...], other[...])
     pre = nt_dot(left, up_w[...]) + dot(latent, rank_up[...])
     hidden = gelu(pre).astype(BF)
     share = dot(hidden, rank_down[...]).astype(BF).reshape(TILE // CHUNK, CHUNK, RANK)
     for half, back in enumerate((mine_back, other_back)):
 
-        @pl.when(i // 2 == half)
+        @pl.when(i // (TILES // 2) == half)
         def _():
             back[:, :CHUNK] = share
             if small:
@@ -171,14 +171,14 @@
 
 def mlp(x, partners, latent, weights, small):
     row = pl.BlockSpec((TILE, WIDTH), lambda i: (i, 0))
-    partner_row = pl.BlockSpec((TILE, WIDTH), lambda i: ((i + 2) % TILES, 0))
+    partner_row = pl.BlockSpec((TILE, WIDTH), lambda i: ((i + TILES // 2) % TILES, 0))
     halves = lambda n: [
-        pl.BlockSpec((TILE // CHUNK, n, RANK), lambda i: (jnp.minimum(i, 1), 0, 0)),
-        pl.BlockSpec((TILE // CHUNK, n, RANK), lambda i: (jnp.maximum(i - 2, 0), 0, 0)),
+        pl.BlockSpec((TILE // CHUNK, n, RANK), lambda i: (jnp.minimum(i, TILES // 2 - 1), 0, 0)),
+        pl.BlockSpec((TILE // CHUNK, n, RANK), lambda i: (jnp.maximum(i - TILES // 2, 0), 0, 0)),
     ]
     latents = [
-        pl.BlockSpec((TILE, RANK), lambda i: (jnp.minimum(i, 1), 0)),
-        pl.BlockSpec((TILE, RANK), lambda i: (jnp.maximum(i - 2, 0), 0)),
+        pl.BlockSpec((TILE, RANK), lambda i: (jnp.minimum(i, TILES // 2 - 1), 0)),
+        pl.BlockSpec((TILE, RANK), lambda i: (jnp.maximum(i - TILES // 2, 0), 0)),
     ]
     whole = lambda *shape: pl.BlockSpec(shape, lambda i: (0,) * len(shape))
     shape = jax.ShapeDtypeStruct
@@ -355,7 +355,7 @@
             near = near_columns(after(planes[layer + 1], latent))
         share = chip_sums(parts).astype(BF)
         if not last:
-            share, own = lax.optimization_barrier((share, own))
+            own = after(own, parts, *near)
             share = after(share, *near)
             gathered.append(near + far_columns(*near[1:]))
         t_zl, t_core, t_x0, t_x1 = terms

time: 229 us -> 222 us (0.969)
  waiting for transfers between devices: 52.6 us -> 47.5 us
    ppermute x25, waiting for transfers between devices: 32.2 us -> 26.4 us  [pair(): return lax.ppermute(value, axis, [(0, 1), (1, 0)])]
  transfers between devices with their start and end apart: 47 -> 47, of which waited for: 22 -> 21; matrix products, arithmetic and copies ran while one was open for 6% -> 7% of each run, Pallas kernels for 3% -> 3%
where the time goes in v4:
time: 222 us; the launch traced here: 220 us
  starting transfers between devices  120 us (54%)
  waiting for transfers between devices  47.5 us (21%)
  Pallas kernels  23.8 us (11%)
  local copies, waits for them, and re-layouts  14.9 us (7%)
  other arithmetic  7.6 us (3%)
  matrix products  5.74 us (3%)
    ppermute x25, starting transfers between devices, pair(): return lax.ppermute(value, axis, [(0, 1), (1, 0)])  39.4 us
    ppermute x6, starting transfers between devices, swap(): return lax.ppermute(value, SWAPPED, perm)  28 us
    ppermute x25, waiting for transfers between devices, pair(): return lax.ppermute(value, axis, [(0, 1), (1, 0)])  26.4 us
    all_to_all x3, starting transfers between devices, chip_sums(): return jnp.sum(lax.all_to_all(parts, CUBE, 0, 0).astype(F32), axis=0)  13 us
    pallas_call x2, Pallas kernels, mlp(): pl.pallas_call(mlp_kernel, grid=(TILES,), in_specs=[row, row, partner_row...  12.8 us
    all_to_all x3, starting transfers between devices, copied_all_to_all(): lax.all_to_all(jnp.broadcast_to(value[None], (count,) + value.shape), axe...  12.7 us
    ppermute x1, starting transfers between devices, swap_copied(): return lax.ppermute(value, SWAPPED, perm)  11.9 us
    ppermute x8, starting transfers between devices, along_y(): lax.ppermute(value, ('y1', 'y0'), [(i, (i + step) % 4) for i in range(4)])  11.1 us
  transfers between devices with their start and end apart: 47, of which 21 were waited for; matrix products, arithmetic and copies ran while one was open for 7% of the time, Pallas kernels for 3%

profile of v4, /device:TPU:1, one launch (start us, length us, event | category | flops | bytes accessed | tf_op | source)
XLA Modules:
  0.0 220.1 jit_solution(11975542102406145655)
XLA Ops:
  3.4 10.2 %collective-permute-start.7 = (bf16[2,448,128]{2,1,0:T(8,128)(2,1)}, bf16[2,448,128]{2,1,0:T(8,128)(2,1)S(1)}, u32[]{:S(2)}, u32[]{:S(2)}) collective-permute-start(bf16[2,448,128]{2,1,0:T(8,128)(2,1)} %pack.1), channel_id=1, source_target_pairs={{0,0},{128,1},{16,2},{144,3},{2,16},{130,17},{18,18},{146,19},{1,1... | collective-permute-start | bytes 688136 | tf_op jit(solution)/shard_map/ppermute | solution.py:36
  17.1 6.1 %collective-permute-start = (bf16[1024,128]{1,0:T(8,128)(2,1)}, bf16[1024,128]{1,0:T(8,128)(2,1)S(1)}, u32[]{:S(2)}, u32[]{:S(2)}) collective-permute-start(bf16[1024,128]{1,0:T(8,128)(2,1)} %param.8), channel_id=1, source_target_pairs={{0,0},{128,1},{16,2},{144,3},{2,16},{130,17},{18,18},{146,19},{1,1... | collective-permute-start | bytes 786440 | tf_op jit(solution)/shard_map/ppermute | solution.py:36
  23.2 11.9 %collective-permute-start.6 = (bf16[2,256,128]{2,1,0:T(8,128)(2,1)}, bf16[2,256,128]{2,1,0:T(8,128)(2,1)}, u32[]{:S(2)}, u32[]{:S(2)}) collective-permute-start(bf16[2,256,128]{2,1,0:T(8,128)(2,1)} %param.15), channel_id=1, source_target_pairs={{0,0},{128,1},{144,2},{16,3},{130,16},{2,17},{18,18},{146,19},{1,1... | collective-permute-start | bytes 393224 | tf_op jit(solution)/shard_map/ppermute | solution.py:44
  42.5 6.2 %all-to-all-start = ((bf16[8,64,256]{2,1,0:T(8,128)(2,1)}), bf16[8,64,256]{2,1,0:T(8,128)(2,1)S(1)}, u32[]{:S(2)}, u32[]{:S(2)}) async-start(bf16[8,64,256]{2,1,0:T(8,128)(2,1)} %bitcast.1), calls=%async_computation | async-start | bytes 524288 | tf_op jit(solution)/shard_map/all_to_all | solution.py:237
  55.4 3.4 %collective-permute-done.1.p_zl = bf16[1024,128]{1,0:T(8,128)(2,1)} collective-permute-done((bf16[1024,128]{1,0:T(8,128)(2,1)S(1)}, bf16[1024,128]{1,0:T(8,128)(2,1)}, u32[]{:S(2)}, u32[]{:S(2)}) %collective-permute-start.1) | collective-permute-done | bytes 262176 | tf_op jit(solution)/shard_map/ppermute | solution.py:20
  62.4 4.8 %all-to-all-start.1 = ((bf16[8,64,256]{2,1,0:T(8,128)(2,1)}), bf16[8,64,256]{2,1,0:T(8,128)(2,1)S(1)}, u32[]{:S(2)}, u32[]{:S(2)}) async-start(bf16[8,64,256]{2,1,0:T(8,128)(2,1)} %broadcast_in_dim.11), calls=%async_computation.1 | async-start | bytes 524288 | tf_op jit(solution)/shard_map/all_to_all | solution.py:48
  74.5 3.2 %collective-permute-start.4 = (bf16[1024,128]{1,0:T(8,128)(2,1)S(1)}, bf16[1024,128]{1,0:T(8,128)(2,1)}, u32[]{:S(2)}, u32[]{:S(2)}) collective-permute-start(bf16[1024,128]{1,0:T(8,128)(2,1)S(1)} %maximum_select_fusion.x), channel_id=1, source_target_pairs={{0,8},{8,0},{1,9},{9,1},{2,10},{10,2},{3,11},{11,3},{4,12},{12,4},... | collective-permute-start | bytes 786440 | tf_op jit(solution)/shard_map/ppermute | solution.py:20
  77.8 3.8 %prep.2 = (bf16[512,640]{1,0:T(8,128)(2,1)}, bf16[640,512]{1,0:T(8,128)(2,1)}, bf16[256,512]{1,0:T(8,128)(2,1)}, bf16[512,256]{1,0:T(8,128)(2,1)}) custom-call(s32[2,4]{1,0:T(2,128)} %bits.3, s32[1]{0:T(128)} %bitcast.10.y, bf16[4,448,128]{2,1,0:T(8,128)(2,1)} %copy-done.4, bf16[4,448,128]{2,1,0:T(8,128)(2,1)} %collective-permute-done.11.before, ...), custom_call_target="tpu_custom_call" | custom-call | flops 2147483648 | bytes 6291456 | tf_op jit(solution)/shard_map/prep/pallas_call | solution.py:126
  85.4 6.5 %mlp.2 = (bf16[8,80,256]{2,1,0:T(8,128)(2,1)}, bf16[8,80,256]{2,1,0:T(8,128)(2,1)}, f32[1024,128]{1,0:T(8,128)}, bf16[1024,128]{1,0:T(8,128)(2,1)}, bf16[1024,12...) custom-call(bf16[1024,128]{1,0:T(8,128)(2,1)} %copy-done.2, ...), custom_call_target="tpu_custom_call" | custom-call | flops 1879048192 | bytes 6291456 | tf_op jit(solution)/shard_map/mlp/pallas_call | solution.py:186
  101.8 3.4 %all-to-all-start.2 = ((bf16[8,80,256]{2,1,0:T(8,128)(2,1)}), bf16[8,80,256]{2,1,0:T(8,128)(2,1)S(1)}, u32[]{:S(2)}, u32[]{:S(2)}) async-start(bf16[8,80,256]{2,1,0:T(8,128)(2,1)} %add_convert_fusion), calls=%async_computation.2 | async-start | bytes 655360 | tf_op jit(solution)/shard_map/all_to_all | solution.py:237
  105.7 5.5 %collective-permute-done.21 = bf16[1024,128]{1,0:T(8,128)(2,1)} collective-permute-done((bf16[1024,128]{1,0:T(8,128)(2,1)}, bf16[1024,128]{1,0:T(8,128)(2,1)}, u32[]{:S(2)}, u32[]{:S(2)}) %collective-permute-start.21) | collective-permute-done | bytes 262176 | tf_op jit(solution)/shard_map/ppermute | solution.py:20
  112.6 3.4 %collective-permute-start.23 = (bf16[512,256]{1,0:T(8,128)(2,1)S(1)}, bf16[512,256]{1,0:T(8,128)(2,1)S(1)}, u32[]{:S(2)}, u32[]{:S(2)}) collective-permute-start(bf16[512,256]{1,0:T(8,128)(2,1)S(1)} %convolution_convert_fusion), channel_id=1, source_target_pairs={{0,16},{16,0},{1,17},{17,1},{2,18},{18,2},{3,19},{19,3},{4,20},{20... | collective-permute-start | bytes 786440 | tf_op jit(solution)/shard_map/ppermute | solution.py:20
  118.4 4.0 %all-to-all-start.3 = ((bf16[8,144,256]{2,1,0:T(8,128)(2,1)}), bf16[8,144,256]{2,1,0:T(8,128)(2,1)S(1)}, u32[]{:S(2)}, u32[]{:S(2)}) async-start(bf16[8,144,256]{2,1,0:T(8,128)(2,1)} %pad_maximum_fusion), calls=%async_computation.3 | async-start | bytes 1179648 | tf_op jit(solution)/shard_map/all_to_all | solution.py:370
  127.1 4.0 %collective-permute-done.24.far0 = bf16[2,448,128]{2,1,0:T(8,128)(2,1)S(1)} collective-permute-done((bf16[2,448,128]{2,1,0:T(8,128)(2,1)S(1)}, bf16[2,448,128]{2,1,0:T(8,128)(2,1)S(1)}, u32[]{:S(2)}, u32[]{:S(2)}) %collective-permute-start.24) | collective-permute-done | bytes 229408 | tf_op jit(solution)/shard_map/ppermute | solution.py:303
  140.5 4.4 %all-to-all-start.4 = ((bf16[8,64,256]{2,1,0:T(8,128)(2,1)}), bf16[8,64,256]{2,1,0:T(8,128)(2,1)S(1)}, u32[]{:S(2)}, u32[]{:S(2)}) async-start(bf16[8,64,256]{2,1,0:T(8,128)(2,1)} %broadcast_in_dim.13), calls=%async_computation.4 | async-start | bytes 524288 | tf_op jit(solution)/shard_map/all_to_all | solution.py:48
  154.2 3.8 %prep.3 = (bf16[512,640]{1,0:T(8,128)(2,1)}, bf16[640,512]{1,0:T(8,128)(2,1)}, bf16[256,512]{1,0:T(8,128)(2,1)}, bf16[512,256]{1,0:T(8,128)(2,1)}) custom-call(s32[2,4]{1,0:T(2,128)} %bits.3, s32[1]{0:T(128)} %bitcast.10.y, bf16[4,448,128]{2,1,0:T(8,128)(2,1)} %get-tuple-element.82.own, bf16[4,448,128]{2,1,0:T(8,128)(2,1)} %collective-permute-done.17.before, ...), custom_call_target="tpu_custom_call" | custom-call | flops 2147483648 | bytes 6291456 | tf_op jit(solution)/shard_map/prep/pallas_call | solution.py:126
  158.1 5.9 %collective-permute-done.30.p_x1 = bf16[1024,128]{1,0:T(8,128)(2,1)} collective-permute-done((bf16[1024,128]{1,0:T(8,128)(2,1)S(1)}, bf16[1024,128]{1,0:T(8,128)(2,1)}, u32[]{:S(2)}, u32[]{:S(2)}) %collective-permute-start.30) | collective-permute-done | bytes 262176 | tf_op jit(solution)/shard_map/ppermute | solution.py:20
  164.7 6.3 %mlp.3 = (bf16[8,64,256]{2,1,0:T(8,128)(2,1)}, bf16[8,64,256]{2,1,0:T(8,128)(2,1)}, f32[1024,128]{1,0:T(8,128)}, bf16[1024,128]{1,0:T(8,128)(2,1)}, bf16[1024,12...) custom-call(bf16[1024,128]{1,0:T(8,128)(2,1)} %copy-done.9, bf16[1024,128]{1,0:T(8,128)(2,1)} %copy-done.11, ...), custom_call_target="tpu_custom_call" | custom-call | flops 1879048192 | bytes 6291456 | tf_op jit(solution)/shard_map/mlp/pallas_call | solution.py:186
  174.9 3.4 %all-to-all-start.5 = ((bf16[8,64,256]{2,1,0:T(8,128)(2,1)}), bf16[8,64,256]{2,1,0:T(8,128)(2,1)S(1)}, u32[]{:S(2)}, u32[]{:S(2)}) async-start(bf16[8,64,256]{2,1,0:T(8,128)(2,1)} %add_convert_fusion.2), calls=%async_computation.5 | async-start | bytes 524288 | tf_op jit(solution)/shard_map/all_to_all | solution.py:237
  185.3 5.0 %collective-permute-done.36 = bf16[1024,128]{1,0:T(8,128)(2,1)S(1)} collective-permute-done((bf16[1024,128]{1,0:T(8,128)(2,1)}, bf16[1024,128]{1,0:T(8,128)(2,1)S(1)}, u32[]{:S(2)}, u32[]{:S(2)}) %collective-permute-start.36) | collective-permute-done | bytes 262176 | tf_op jit(solution)/shard_map/ppermute | solution.py:20
  191.0 3.5 %all-to-all-start.6 = ((bf16[8,64,256]{2,1,0:T(8,128)(2,1)}), bf16[8,64,256]{2,1,0:T(8,128)(2,1)S(1)}, u32[]{:S(2)}, u32[]{:S(2)}) async-start(bf16[8,64,256]{2,1,0:T(8,128)(2,1)} %broadcast_in_dim.14), calls=%async_computation.6 | async-start | bytes 524288 | tf_op jit(solution)/shard_map/all_to_all | solution.py:48
  197.3 3.4 %all-to-all-done.6 = bf16[8,64,256]{2,1,0:T(8,128)(2,1)S(1)} async-done(((bf16[8,64,256]{2,1,0:T(8,128)(2,1)}), bf16[8,64,256]{2,1,0:T(8,128)(2,1)S(1)}, u32[]{:S(2)}, u32[]{:S(2)}) %all-to-all-start.6) | async-done | bytes 262176 | tf_op jit(solution)/shard_map/all_to_all | solution.py:48
  207.0 8.3 %collective-permute-start.39 = (bf16[1024,128]{1,0:T(8,128)(2,1)S(1)}, bf16[1024,128]{1,0:T(8,128)(2,1)S(1)}, u32[]{:S(2)}, u32[]{:S(2)}) collective-permute-start(bf16[1024,128]{1,0:T(8,128)(2,1)S(1)} %maximum_select_fusion.1), channel_id=1, source_target_pairs={{0,0},{128,1},{16,2},{144,3},{2,16},{130,17},{18,18},{146,19},{1,1... | collective-permute-start | bytes 786440 | tf_op jit(solution)/shard_map/ppermute | solution.py:36
  215.3 4.2 %collective-permute-done.39 = bf16[1024,128]{1,0:T(8,128)(2,1)S(1)} collective-permute-done((bf16[1024,128]{1,0:T(8,128)(2,1)S(1)}, bf16[1024,128]{1,0:T(8,128)(2,1)S(1)}, u32[]{:S(2)}, u32[]{:S(2)}) %collective-permute-start.39) | collective-permute-done | bytes 262176 | tf_op jit(solution)/shard_map/ppermute | solution.py:36
  (153 shorter events, 95.2 us)
Async XLA Ops:
  3.4 19.8 %collective-permute-start.7 = (bf16[2,448,128]{2,1,0:T(8,128)(2,1)}, bf16[2,448,128]{2,1,0:T(8,128)(2,1)S(1)}, u32[]{:S(2)}, u32[]{:S(2)}) collective-permute-start(bf16[2,448,128]{2,1,0:T(8,128)(2,1)} %pack.1), channel_id=1, source_target_pairs={{0,0},{128,1},{16,2},{144,3},{2,16},{130,17},{18,18},{146,19},{1,1... | collective-permute-start | bytes 688136 | tf_op jit(solution)/shard_map/ppermute | solution.py:36
  13.6 23.1 %collective-permute-start.8 = (bf16[2,448,128]{2,1,0:T(8,128)(2,1)}, bf16[2,448,128]{2,1,0:T(8,128)(2,1)}, u32[]{:S(2)}, u32[]{:S(2)}) collective-permute-start(bf16[2,448,128]{2,1,0:T(8,128)(2,1)} %pack.1), channel_id=1, source_target_pairs={{16,0},{144,1},{0,2},{128,3},{18,16},{146,17},{2,18},{130,19},{17,... | collective-permute-start | bytes 688136 | tf_op jit(solution)/shard_map/ppermute | solution.py:36
  13.7 26.3 %collective-permute-start.9 = (bf16[2,448,128]{2,1,0:T(8,128)(2,1)}, bf16[2,448,128]{2,1,0:T(8,128)(2,1)S(1)}, u32[]{:S(2)}, u32[]{:S(2)}) collective-permute-start(bf16[2,448,128]{2,1,0:T(8,128)(2,1)} %pack.1), channel_id=1, source_target_pairs={{128,0},{0,1},{144,2},{16,3},{130,16},{2,17},{146,18},{18,19},{129... | collective-permute-start | bytes 688136 | tf_op jit(solution)/shard_map/ppermute | solution.py:36
  14.0 26.7 %collective-permute-start.10 = (bf16[2,448,128]{2,1,0:T(8,128)(2,1)}, bf16[2,448,128]{2,1,0:T(8,128)(2,1)S(1)}, u32[]{:S(2)}, u32[]{:S(2)}) collective-permute-start(bf16[2,448,128]{2,1,0:T(8,128)(2,1)} %pack.1), channel_id=1, source_target_pairs={{144,0},{16,1},{128,2},{0,3},{146,16},{18,17},{130,18},{2,19},{145... | collective-permute-start | bytes 688136 | tf_op jit(solution)/shard_map/ppermute | solution.py:36
  17.1 22.5 %collective-permute-start = (bf16[1024,128]{1,0:T(8,128)(2,1)}, bf16[1024,128]{1,0:T(8,128)(2,1)S(1)}, u32[]{:S(2)}, u32[]{:S(2)}) collective-permute-start(bf16[1024,128]{1,0:T(8,128)(2,1)} %param.8), channel_id=1, source_target_pairs={{0,0},{128,1},{16,2},{144,3},{2,16},{130,17},{18,18},{146,19},{1,1... | collective-permute-start | bytes 786440 | tf_op jit(solution)/shard_map/ppermute | solution.py:36
  23.2 19.3 %collective-permute-start.6 = (bf16[2,256,128]{2,1,0:T(8,128)(2,1)}, bf16[2,256,128]{2,1,0:T(8,128)(2,1)}, u32[]{:S(2)}, u32[]{:S(2)}) collective-permute-start(bf16[2,256,128]{2,1,0:T(8,128)(2,1)} %param.15), channel_id=1, source_target_pairs={{0,0},{128,1},{144,2},{16,3},{130,16},{2,17},{18,18},{146,19},{1,1... | collective-permute-start | bytes 393224 | tf_op jit(solution)/shard_map/ppermute | solution.py:44
  42.5 12.9 %all-to-all-start = ((bf16[8,64,256]{2,1,0:T(8,128)(2,1)}), bf16[8,64,256]{2,1,0:T(8,128)(2,1)S(1)}, u32[]{:S(2)}, u32[]{:S(2)}) async-start(bf16[8,64,256]{2,1,0:T(8,128)(2,1)} %bitcast.1), calls=%async_computation | async-start | bytes 524288 | tf_op jit(solution)/shard_map/all_to_all | solution.py:237
  48.7 12.9 %collective-permute-start.11 = (bf16[4,448,128]{2,1,0:T(8,128)(2,1)S(1)}, bf16[4,448,128]{2,1,0:T(8,128)(2,1)}, u32[]{:S(2)}, u32[]{:S(2)}) collective-permute-start(bf16[4,448,128]{2,1,0:T(8,128)(2,1)S(1)} %get-tuple-element.55.own), channel_id=1, source_target_pairs={{0,32},{32,64},{64,96},{96,0},{1,33},{33,65},{65,97},{97,1},{2,34}... | collective-permute-start | bytes 1376264 | tf_op jit(solution)/shard_map/ppermute | solution.py:303
  50.0 11.6 %collective-permute-start.12 = (bf16[4,448,128]{2,1,0:T(8,128)(2,1)S(1)}, bf16[4,448,128]{2,1,0:T(8,128)(2,1)}, u32[]{:S(2)}, u32[]{:S(2)}) collective-permute-start(bf16[4,448,128]{2,1,0:T(8,128)(2,1)S(1)} %get-tuple-element.55.own), channel_id=1, source_target_pairs={{0,96},{32,0},{64,32},{96,64},{1,97},{33,1},{65,33},{97,65},{2,98}... | collective-permute-start | bytes 1376264 | tf_op jit(solution)/shard_map/ppermute | solution.py:303
  62.4 19.2 %all-to-all-start.1 = ((bf16[8,64,256]{2,1,0:T(8,128)(2,1)}), bf16[8,64,256]{2,1,0:T(8,128)(2,1)S(1)}, u32[]{:S(2)}, u32[]{:S(2)}) async-start(bf16[8,64,256]{2,1,0:T(8,128)(2,1)} %broadcast_in_dim.11), calls=%async_computation.1 | async-start | bytes 524288 | tf_op jit(solution)/shard_map/all_to_all | solution.py:48
  71.9 12.8 %collective-permute-start.2 = (bf16[1024,128]{1,0:T(8,128)(2,1)S(1)}, bf16[1024,128]{1,0:T(8,128)(2,1)}, u32[]{:S(2)}, u32[]{:S(2)}) collective-permute-start(bf16[1024,128]{1,0:T(8,128)(2,1)S(1)} %maximum_select_fusion.x), channel_id=1, source_target_pairs={{0,16},{16,0},{1,17},{17,1},{2,18},{18,2},{3,19},{19,3},{4,20},{20... | collective-permute-start | bytes 786440 | tf_op jit(solution)/shard_map/ppermute | solution.py:20
  92.5 13.2 %collective-permute-start.17 = (bf16[4,448,128]{2,1,0:T(8,128)(2,1)}, bf16[4,448,128]{2,1,0:T(8,128)(2,1)}, u32[]{:S(2)}, u32[]{:S(2)}) collective-permute-start(bf16[4,448,128]{2,1,0:T(8,128)(2,1)} %get-tuple-element.82.own), channel_id=1, source_target_pairs={{0,32},{32,64},{64,96},{96,0},{1,33},{33,65},{65,97},{97,1},{2,34}... | collective-permute-start | bytes 1376264 | tf_op jit(solution)/shard_map/ppermute | solution.py:303
  93.5 12.2 %collective-permute-start.18 = (bf16[4,448,128]{2,1,0:T(8,128)(2,1)}, bf16[4,448,128]{2,1,0:T(8,128)(2,1)}, u32[]{:S(2)}, u32[]{:S(2)}) collective-permute-start(bf16[4,448,128]{2,1,0:T(8,128)(2,1)} %get-tuple-element.82.own), channel_id=1, source_target_pairs={{0,96},{32,0},{64,32},{96,64},{1,97},{33,1},{65,33},{97,65},{2,98}... | collective-permute-start | bytes 1376264 | tf_op jit(solution)/shard_map/ppermute | solution.py:303
  98.4 12.8 %collective-permute-start.21 = (bf16[1024,128]{1,0:T(8,128)(2,1)}, bf16[1024,128]{1,0:T(8,128)(2,1)}, u32[]{:S(2)}, u32[]{:S(2)}) collective-permute-start(bf16[1024,128]{1,0:T(8,128)(2,1)} %get-tuple-element.74), channel_id=1, source_target_pairs={{0,4},{4,0},{1,5},{5,1},{2,6},{6,2},{3,7},{7,3},{8,12},{12,8},{9,1... | collective-permute-start | bytes 786440 | tf_op jit(solution)/shard_map/ppermute | solution.py:20
  98.7 12.5 %collective-permute-start.19 = (bf16[1024,128]{1,0:T(8,128)(2,1)}, bf16[1024,128]{1,0:T(8,128)(2,1)}, u32[]{:S(2)}, u32[]{:S(2)}) collective-permute-start(bf16[1024,128]{1,0:T(8,128)(2,1)} %get-tuple-element.72), channel_id=1, source_target_pairs={{0,128},{128,0},{1,129},{129,1},{2,130},{130,2},{3,131},{131,3},{4... | collective-permute-start | bytes 786440 | tf_op jit(solution)/shard_map/ppermute | solution.py:20
  101.8 15.7 %all-to-all-start.2 = ((bf16[8,80,256]{2,1,0:T(8,128)(2,1)}), bf16[8,80,256]{2,1,0:T(8,128)(2,1)S(1)}, u32[]{:S(2)}, u32[]{:S(2)}) async-start(bf16[8,80,256]{2,1,0:T(8,128)(2,1)} %add_convert_fusion), calls=%async_computation.2 | async-start | bytes 655360 | tf_op jit(solution)/shard_map/all_to_all | solution.py:237
  118.4 13.9 %all-to-all-start.3 = ((bf16[8,144,256]{2,1,0:T(8,128)(2,1)}), bf16[8,144,256]{2,1,0:T(8,128)(2,1)S(1)}, u32[]{:S(2)}, u32[]{:S(2)}) async-start(bf16[8,144,256]{2,1,0:T(8,128)(2,1)} %pad_maximum_fusion), calls=%async_computation.3 | async-start | bytes 1179648 | tf_op jit(solution)/shard_map/all_to_all | solution.py:370
  140.5 11.1 %all-to-all-start.4 = ((bf16[8,64,256]{2,1,0:T(8,128)(2,1)}), bf16[8,64,256]{2,1,0:T(8,128)(2,1)S(1)}, u32[]{:S(2)}, u32[]{:S(2)}) async-start(bf16[8,64,256]{2,1,0:T(8,128)(2,1)} %broadcast_in_dim.13), calls=%async_computation.4 | async-start | bytes 524288 | tf_op jit(solution)/shard_map/all_to_all | solution.py:48
  144.9 13.2 %collective-permute-start.27 = (bf16[1024,128]{1,0:T(8,128)(2,1)S(1)}, bf16[1024,128]{1,0:T(8,128)(2,1)S(1)}, u32[]{:S(2)}, u32[]{:S(2)}) collective-permute-start(bf16[1024,128]{1,0:T(8,128)(2,1)S(1)} %fusion.2.x), channel_id=1, source_target_pairs={{0,128},{128,0},{1,129},{129,1},{2,130},{130,2},{3,131},{131,3},{4... | collective-permute-start | bytes 786440 | tf_op jit(solution)/shard_map/ppermute | solution.py:20
  146.3 11.7 %collective-permute-start.28 = (bf16[1024,128]{1,0:T(8,128)(2,1)S(1)}, bf16[1024,128]{1,0:T(8,128)(2,1)S(1)}, u32[]{:S(2)}, u32[]{:S(2)}) collective-permute-start(bf16[1024,128]{1,0:T(8,128)(2,1)S(1)} %fusion.2.x), channel_id=1, source_target_pairs={{0,16},{16,0},{1,17},{17,1},{2,18},{18,2},{3,19},{19,3},{4,20},{20... | collective-permute-start | bytes 786440 | tf_op jit(solution)/shard_map/ppermute | solution.py:20
  148.8 15.2 %collective-permute-start.30 = (bf16[1024,128]{1,0:T(8,128)(2,1)S(1)}, bf16[1024,128]{1,0:T(8,128)(2,1)}, u32[]{:S(2)}, u32[]{:S(2)}) collective-permute-start(bf16[1024,128]{1,0:T(8,128)(2,1)S(1)} %fusion.2.x), channel_id=1, source_target_pairs={{0,8},{8,0},{1,9},{9,1},{2,10},{10,2},{3,11},{11,3},{4,12},{12,4},... | collective-permute-start | bytes 786440 | tf_op jit(solution)/shard_map/ppermute | solution.py:20
  151.6 12.4 %collective-permute-start.32 = (bf16[512,256]{1,0:T(8,128)(2,1)S(1)}, bf16[512,256]{1,0:T(8,128)(2,1)S(1)}, u32[]{:S(2)}, u32[]{:S(2)}) collective-permute-start(bf16[512,256]{1,0:T(8,128)(2,1)S(1)} %bitcast.43), channel_id=1, source_target_pairs={{0,16},{16,0},{1,17},{17,1},{2,18},{18,2},{3,19},{19,3},{4,20},{20... | collective-permute-start | bytes 786440 | tf_op jit(solution)/shard_map/ppermute | solution.py:20
  178.3 12.0 %collective-permute-start.36 = (bf16[1024,128]{1,0:T(8,128)(2,1)}, bf16[1024,128]{1,0:T(8,128)(2,1)S(1)}, u32[]{:S(2)}, u32[]{:S(2)}) collective-permute-start(bf16[1024,128]{1,0:T(8,128)(2,1)} %get-tuple-element.95), channel_id=1, source_target_pairs={{0,8},{8,0},{1,9},{9,1},{2,10},{10,2},{3,11},{11,3},{4,12},{12,4},... | collective-permute-start | bytes 786440 | tf_op jit(solution)/shard_map/ppermute | solution.py:20
  207.0 12.4 %collective-permute-start.39 = (bf16[1024,128]{1,0:T(8,128)(2,1)S(1)}, bf16[1024,128]{1,0:T(8,128)(2,1)S(1)}, u32[]{:S(2)}, u32[]{:S(2)}) collective-permute-start(bf16[1024,128]{1,0:T(8,128)(2,1)S(1)} %maximum_select_fusion.1), channel_id=1, source_target_pairs={{0,0},{128,1},{16,2},{144,3},{2,16},{130,17},{18,18},{146,19},{1,1... | collective-permute-start | bytes 786440 | tf_op jit(solution)/shard_map/ppermute | solution.py:36
  (42 other events, 406.6 us)

commit v5 on v4

--- a/solution.py
+++ b/solution.py
@@ -333,7 +333,14 @@
     )
     near = near_columns(planes[0])
     share = chip_sums(parts).astype(BF)
-    share = after(share, *near, partners[0], partners[2])
+    smalls = [
+        [
+            part.reshape(8, SMALL, RANK)
+            for part in share_of_core(dot(rank_out[i], rows_in[i + 1]).astype(BF))
+        ]
+        for i in range(layers - 1)
+    ]
+    share = after(share, *near, partners[0], partners[2], *sum(smalls, []))
     gathered = [near + far_columns(*near[1:])]
     latent = copied_all_to_all(share, 8, CUBE).reshape(HALF, RANK)
     for layer in range(layers):
@@ -342,10 +349,7 @@
         weights = prep(layer, level_bits, cols)
         if layer == 0:
             latent = after(latent, *weights)
-        small = []
-        if not last:
-            small = share_of_core(dot(rank_out[layer], rows_in[layer + 1]).astype(BF))
-            small = [part.reshape(8, SMALL, RANK) for part in small]
+        small = [] if last else smalls[layer]
         mine, other, own, *terms = mlp(
             x, partners, (latent, pair(latent, "core")), weights, small
         )

time: 222 us -> 222 us (level)
  no operation moved by 1% of the time
where the time goes in v5:
time: 222 us; the launch traced here: 220 us
  starting transfers between devices  120 us (54%)
  waiting for transfers between devices  47 us (21%)
  Pallas kernels  23.8 us (11%)
  local copies, waits for them, and re-layouts  14.9 us (7%)
  other arithmetic  7.61 us (3%)
  matrix products  5.75 us (3%)
    ppermute x25, starting transfers between devices, pair(): return lax.ppermute(value, axis, [(0, 1), (1, 0)])  39.5 us
    ppermute x6, starting transfers between devices, swap(): return lax.ppermute(value, SWAPPED, perm)  27.9 us
    ppermute x25, waiting for transfers between devices, pair(): return lax.ppermute(value, axis, [(0, 1), (1, 0)])  27 us
    all_to_all x3, starting transfers between devices, chip_sums(): return jnp.sum(lax.all_to_all(parts, CUBE, 0, 0).astype(F32), axis=0)  13 us
    pallas_call x2, Pallas kernels, mlp(): pl.pallas_call(mlp_kernel, grid=(TILES,), in_specs=[row, row, partner_row...  12.8 us
    all_to_all x3, starting transfers between devices, copied_all_to_all(): lax.all_to_all(jnp.broadcast_to(value[None], (count,) + value.shape), axe...  12.7 us
    ppermute x1, starting transfers between devices, swap_copied(): return lax.ppermute(value, SWAPPED, perm)  11.9 us
    ppermute x8, starting transfers between devices, along_y(): lax.ppermute(value, ('y1', 'y0'), [(i, (i + step) % 4) for i in range(4)])  11.2 us
  transfers between devices with their start and end apart: 47, of which 21 were waited for; matrix products, arithmetic and copies ran while one was open for 7% of the time, Pallas kernels for 3%

profile of v5, /device:TPU:1, one launch (start us, length us, event | category | flops | bytes accessed | tf_op | source)
XLA Modules:
  0.0 219.8 jit_solution(15695928251379697608)
XLA Ops:
  3.4 10.2 %collective-permute-start.7 = (bf16[2,448,128]{2,1,0:T(8,128)(2,1)}, bf16[2,448,128]{2,1,0:T(8,128)(2,1)S(1)}, u32[]{:S(2)}, u32[]{:S(2)}) collective-permute-start(bf16[2,448,128]{2,1,0:T(8,128)(2,1)} %pack.1), channel_id=1, source_target_pairs={{0,0},{128,1},{16,2},{144,3},{2,16},{130,17},{18,18},{146,19},{1,1... | collective-permute-start | bytes 688136 | tf_op jit(solution)/shard_map/ppermute | solution.py:36
  14.0 3.1 %collective-permute-start.10 = (bf16[2,448,128]{2,1,0:T(8,128)(2,1)}, bf16[2,448,128]{2,1,0:T(8,128)(2,1)S(1)}, u32[]{:S(2)}, u32[]{:S(2)}) collective-permute-start(bf16[2,448,128]{2,1,0:T(8,128)(2,1)} %pack.1), channel_id=1, source_target_pairs={{144,0},{16,1},{128,2},{0,3},{146,16},{18,17},{130,18},{2,19},{145... | collective-permute-start | bytes 688136 | tf_op jit(solution)/shard_map/ppermute | solution.py:36
  17.0 6.1 %collective-permute-start = (bf16[1024,128]{1,0:T(8,128)(2,1)}, bf16[1024,128]{1,0:T(8,128)(2,1)S(1)}, u32[]{:S(2)}, u32[]{:S(2)}) collective-permute-start(bf16[1024,128]{1,0:T(8,128)(2,1)} %param.8), channel_id=1, source_target_pairs={{0,0},{128,1},{16,2},{144,3},{2,16},{130,17},{18,18},{146,19},{1,1... | collective-permute-start | bytes 786440 | tf_op jit(solution)/shard_map/ppermute | solution.py:36
  23.2 11.9 %collective-permute-start.6 = (bf16[2,256,128]{2,1,0:T(8,128)(2,1)}, bf16[2,256,128]{2,1,0:T(8,128)(2,1)}, u32[]{:S(2)}, u32[]{:S(2)}) collective-permute-start(bf16[2,256,128]{2,1,0:T(8,128)(2,1)} %param.15), channel_id=1, source_target_pairs={{0,0},{128,1},{144,2},{16,3},{130,16},{2,17},{18,18},{146,19},{1,1... | collective-permute-start | bytes 393224 | tf_op jit(solution)/shard_map/ppermute | solution.py:44
  42.5 6.2 %all-to-all-start = ((bf16[8,64,256]{2,1,0:T(8,128)(2,1)}), bf16[8,64,256]{2,1,0:T(8,128)(2,1)S(1)}, u32[]{:S(2)}, u32[]{:S(2)}) async-start(bf16[8,64,256]{2,1,0:T(8,128)(2,1)} %bitcast.1), calls=%async_computation | async-start | bytes 524288 | tf_op jit(solution)/shard_map/all_to_all | solution.py:237
  62.4 4.8 %all-to-all-start.1 = ((bf16[8,64,256]{2,1,0:T(8,128)(2,1)}), bf16[8,64,256]{2,1,0:T(8,128)(2,1)S(1)}, u32[]{:S(2)}, u32[]{:S(2)}) async-start(bf16[8,64,256]{2,1,0:T(8,128)(2,1)} %broadcast_in_dim.11), calls=%async_computation.1 | async-start | bytes 524288 | tf_op jit(solution)/shard_map/all_to_all | solution.py:48
  74.5 3.2 %collective-permute-start.4 = (bf16[1024,128]{1,0:T(8,128)(2,1)S(1)}, bf16[1024,128]{1,0:T(8,128)(2,1)}, u32[]{:S(2)}, u32[]{:S(2)}) collective-permute-start(bf16[1024,128]{1,0:T(8,128)(2,1)S(1)} %maximum_select_fusion.x), channel_id=1, source_target_pairs={{0,8},{8,0},{1,9},{9,1},{2,10},{10,2},{3,11},{11,3},{4,12},{12,4},... | collective-permute-start | bytes 786440 | tf_op jit(solution)/shard_map/ppermute | solution.py:20
  77.8 3.8 %prep.2 = (bf16[512,640]{1,0:T(8,128)(2,1)}, bf16[640,512]{1,0:T(8,128)(2,1)}, bf16[256,512]{1,0:T(8,128)(2,1)}, bf16[512,256]{1,0:T(8,128)(2,1)}) custom-call(s32[2,4]{1,0:T(2,128)} %bits.3, s32[1]{0:T(128)} %bitcast.14.y, bf16[4,448,128]{2,1,0:T(8,128)(2,1)} %copy-done.4, bf16[4,448,128]{2,1,0:T(8,128)(2,1)} %collective-permute-done.11.before, ...), custom_call_target="tpu_custom_call" | custom-call | flops 2147483648 | bytes 6291456 | tf_op jit(solution)/shard_map/prep/pallas_call | solution.py:126
  85.3 6.5 %mlp.2 = (bf16[8,80,256]{2,1,0:T(8,128)(2,1)}, bf16[8,80,256]{2,1,0:T(8,128)(2,1)}, f32[1024,128]{1,0:T(8,128)}, bf16[1024,128]{1,0:T(8,128)(2,1)}, bf16[1024,12...) custom-call(bf16[1024,128]{1,0:T(8,128)(2,1)} %copy-done.2, bf16[1024,128]{1,0:T(8,128)(2,1)} %copy-done.8, ...), custom_call_target="tpu_custom_call" | custom-call | flops 1879048192 | bytes 6291456 | tf_op jit(solution)/shard_map/mlp/pallas_call | solution.py:186
  101.5 3.4 %all-to-all-start.2 = ((bf16[8,80,256]{2,1,0:T(8,128)(2,1)}), bf16[8,80,256]{2,1,0:T(8,128)(2,1)S(1)}, u32[]{:S(2)}, u32[]{:S(2)}) async-start(bf16[8,80,256]{2,1,0:T(8,128)(2,1)} %add_convert_fusion), calls=%async_computation.2 | async-start | bytes 655360 | tf_op jit(solution)/shard_map/all_to_all | solution.py:237
  105.7 4.9 %collective-permute-done.21 = bf16[1024,128]{1,0:T(8,128)(2,1)} collective-permute-done((bf16[1024,128]{1,0:T(8,128)(2,1)}, bf16[1024,128]{1,0:T(8,128)(2,1)}, u32[]{:S(2)}, u32[]{:S(2)}) %collective-permute-start.21) | collective-permute-done | bytes 262176 | tf_op jit(solution)/shard_map/ppermute | solution.py:20
  112.0 3.7 %collective-permute-start.23 = (bf16[512,256]{1,0:T(8,128)(2,1)S(1)}, bf16[512,256]{1,0:T(8,128)(2,1)S(1)}, u32[]{:S(2)}, u32[]{:S(2)}) collective-permute-start(bf16[512,256]{1,0:T(8,128)(2,1)S(1)} %convolution_convert_fusion), channel_id=1, source_target_pairs={{0,16},{16,0},{1,17},{17,1},{2,18},{18,2},{3,19},{19,3},{4,20},{20... | collective-permute-start | bytes 786440 | tf_op jit(solution)/shard_map/ppermute | solution.py:20
  118.1 4.0 %all-to-all-start.3 = ((bf16[8,144,256]{2,1,0:T(8,128)(2,1)}), bf16[8,144,256]{2,1,0:T(8,128)(2,1)S(1)}, u32[]{:S(2)}, u32[]{:S(2)}) async-start(bf16[8,144,256]{2,1,0:T(8,128)(2,1)} %pad_maximum_fusion), calls=%async_computation.3 | async-start | bytes 1179648 | tf_op jit(solution)/shard_map/all_to_all | solution.py:374
  126.8 4.0 %collective-permute-done.24.far0 = bf16[2,448,128]{2,1,0:T(8,128)(2,1)S(1)} collective-permute-done((bf16[2,448,128]{2,1,0:T(8,128)(2,1)S(1)}, bf16[2,448,128]{2,1,0:T(8,128)(2,1)S(1)}, u32[]{:S(2)}, u32[]{:S(2)}) %collective-permute-start.24) | collective-permute-done | bytes 229408 | tf_op jit(solution)/shard_map/ppermute | solution.py:303
  140.3 4.4 %all-to-all-start.4 = ((bf16[8,64,256]{2,1,0:T(8,128)(2,1)}), bf16[8,64,256]{2,1,0:T(8,128)(2,1)S(1)}, u32[]{:S(2)}, u32[]{:S(2)}) async-start(bf16[8,64,256]{2,1,0:T(8,128)(2,1)} %broadcast_in_dim.13), calls=%async_computation.4 | async-start | bytes 524288 | tf_op jit(solution)/shard_map/all_to_all | solution.py:48
  154.0 3.8 %prep.3 = (bf16[512,640]{1,0:T(8,128)(2,1)}, bf16[640,512]{1,0:T(8,128)(2,1)}, bf16[256,512]{1,0:T(8,128)(2,1)}, bf16[512,256]{1,0:T(8,128)(2,1)}) custom-call(s32[2,4]{1,0:T(2,128)} %bits.3, s32[1]{0:T(128)} %bitcast.14.y, bf16[4,448,128]{2,1,0:T(8,128)(2,1)} %get-tuple-element.82.own, bf16[4,448,128]{2,1,0:T(8,128)(2,1)} %collective-permute-done.17.before, ...), custom_call_target="tpu_custom_call" | custom-call | flops 2147483648 | bytes 6291456 | tf_op jit(solution)/shard_map/prep/pallas_call | solution.py:126
  157.8 5.9 %collective-permute-done.30.p_x1 = bf16[1024,128]{1,0:T(8,128)(2,1)} collective-permute-done((bf16[1024,128]{1,0:T(8,128)(2,1)S(1)}, bf16[1024,128]{1,0:T(8,128)(2,1)}, u32[]{:S(2)}, u32[]{:S(2)}) %collective-permute-start.30) | collective-permute-done | bytes 262176 | tf_op jit(solution)/shard_map/ppermute | solution.py:20
  164.4 6.4 %mlp.3 = (bf16[8,64,256]{2,1,0:T(8,128)(2,1)}, bf16[8,64,256]{2,1,0:T(8,128)(2,1)}, f32[1024,128]{1,0:T(8,128)}, bf16[1024,128]{1,0:T(8,128)(2,1)}, bf16[1024,12...) custom-call(bf16[1024,128]{1,0:T(8,128)(2,1)} %copy-done.10, bf16[1024,128]{1,0:T(8,128)(2,1)} %copy-done.12, ...), custom_call_target="tpu_custom_call" | custom-call | flops 1879048192 | bytes 6291456 | tf_op jit(solution)/shard_map/mlp/pallas_call | solution.py:186
  174.7 3.4 %all-to-all-start.5 = ((bf16[8,64,256]{2,1,0:T(8,128)(2,1)}), bf16[8,64,256]{2,1,0:T(8,128)(2,1)S(1)}, u32[]{:S(2)}, u32[]{:S(2)}) async-start(bf16[8,64,256]{2,1,0:T(8,128)(2,1)} %add_convert_fusion.2), calls=%async_computation.5 | async-start | bytes 524288 | tf_op jit(solution)/shard_map/all_to_all | solution.py:237
  185.1 5.0 %collective-permute-done.36 = bf16[1024,128]{1,0:T(8,128)(2,1)S(1)} collective-permute-done((bf16[1024,128]{1,0:T(8,128)(2,1)}, bf16[1024,128]{1,0:T(8,128)(2,1)S(1)}, u32[]{:S(2)}, u32[]{:S(2)}) %collective-permute-start.36) | collective-permute-done | bytes 262176 | tf_op jit(solution)/shard_map/ppermute | solution.py:20
  190.8 3.5 %all-to-all-start.6 = ((bf16[8,64,256]{2,1,0:T(8,128)(2,1)}), bf16[8,64,256]{2,1,0:T(8,128)(2,1)S(1)}, u32[]{:S(2)}, u32[]{:S(2)}) async-start(bf16[8,64,256]{2,1,0:T(8,128)(2,1)} %broadcast_in_dim.14), calls=%async_computation.6 | async-start | bytes 524288 | tf_op jit(solution)/shard_map/all_to_all | solution.py:48
  197.0 3.4 %all-to-all-done.6 = bf16[8,64,256]{2,1,0:T(8,128)(2,1)S(1)} async-done(((bf16[8,64,256]{2,1,0:T(8,128)(2,1)}), bf16[8,64,256]{2,1,0:T(8,128)(2,1)S(1)}, u32[]{:S(2)}, u32[]{:S(2)}) %all-to-all-start.6) | async-done | bytes 262176 | tf_op jit(solution)/shard_map/all_to_all | solution.py:48
  206.8 8.2 %collective-permute-start.39 = (bf16[1024,128]{1,0:T(8,128)(2,1)S(1)}, bf16[1024,128]{1,0:T(8,128)(2,1)S(1)}, u32[]{:S(2)}, u32[]{:S(2)}) collective-permute-start(bf16[1024,128]{1,0:T(8,128)(2,1)S(1)} %maximum_select_fusion.1), channel_id=1, source_target_pairs={{0,0},{128,1},{16,2},{144,3},{2,16},{130,17},{18,18},{146,19},{1,1... | collective-permute-start | bytes 786440 | tf_op jit(solution)/shard_map/ppermute | solution.py:36
  215.0 4.1 %collective-permute-done.39 = bf16[1024,128]{1,0:T(8,128)(2,1)S(1)} collective-permute-done((bf16[1024,128]{1,0:T(8,128)(2,1)S(1)}, bf16[1024,128]{1,0:T(8,128)(2,1)S(1)}, u32[]{:S(2)}, u32[]{:S(2)}) %collective-permute-start.39) | collective-permute-done | bytes 262176 | tf_op jit(solution)/shard_map/ppermute | solution.py:36
  (155 shorter events, 95.5 us)
Async XLA Ops:
  3.4 19.8 %collective-permute-start.7 = (bf16[2,448,128]{2,1,0:T(8,128)(2,1)}, bf16[2,448,128]{2,1,0:T(8,128)(2,1)S(1)}, u32[]{:S(2)}, u32[]{:S(2)}) collective-permute-start(bf16[2,448,128]{2,1,0:T(8,128)(2,1)} %pack.1), channel_id=1, source_target_pairs={{0,0},{128,1},{16,2},{144,3},{2,16},{130,17},{18,18},{146,19},{1,1... | collective-permute-start | bytes 688136 | tf_op jit(solution)/shard_map/ppermute | solution.py:36
  13.6 23.1 %collective-permute-start.8 = (bf16[2,448,128]{2,1,0:T(8,128)(2,1)}, bf16[2,448,128]{2,1,0:T(8,128)(2,1)}, u32[]{:S(2)}, u32[]{:S(2)}) collective-permute-start(bf16[2,448,128]{2,1,0:T(8,128)(2,1)} %pack.1), channel_id=1, source_target_pairs={{16,0},{144,1},{0,2},{128,3},{18,16},{146,17},{2,18},{130,19},{17,... | collective-permute-start | bytes 688136 | tf_op jit(solution)/shard_map/ppermute | solution.py:36
  13.7 26.3 %collective-permute-start.9 = (bf16[2,448,128]{2,1,0:T(8,128)(2,1)}, bf16[2,448,128]{2,1,0:T(8,128)(2,1)S(1)}, u32[]{:S(2)}, u32[]{:S(2)}) collective-permute-start(bf16[2,448,128]{2,1,0:T(8,128)(2,1)} %pack.1), channel_id=1, source_target_pairs={{128,0},{0,1},{144,2},{16,3},{130,16},{2,17},{146,18},{18,19},{129... | collective-permute-start | bytes 688136 | tf_op jit(solution)/shard_map/ppermute | solution.py:36
  14.0 26.7 %collective-permute-start.10 = (bf16[2,448,128]{2,1,0:T(8,128)(2,1)}, bf16[2,448,128]{2,1,0:T(8,128)(2,1)S(1)}, u32[]{:S(2)}, u32[]{:S(2)}) collective-permute-start(bf16[2,448,128]{2,1,0:T(8,128)(2,1)} %pack.1), channel_id=1, source_target_pairs={{144,0},{16,1},{128,2},{0,3},{146,16},{18,17},{130,18},{2,19},{145... | collective-permute-start | bytes 688136 | tf_op jit(solution)/shard_map/ppermute | solution.py:36
  17.0 22.5 %collective-permute-start = (bf16[1024,128]{1,0:T(8,128)(2,1)}, bf16[1024,128]{1,0:T(8,128)(2,1)S(1)}, u32[]{:S(2)}, u32[]{:S(2)}) collective-permute-start(bf16[1024,128]{1,0:T(8,128)(2,1)} %param.8), channel_id=1, source_target_pairs={{0,0},{128,1},{16,2},{144,3},{2,16},{130,17},{18,18},{146,19},{1,1... | collective-permute-start | bytes 786440 | tf_op jit(solution)/shard_map/ppermute | solution.py:36
  23.2 19.3 %collective-permute-start.6 = (bf16[2,256,128]{2,1,0:T(8,128)(2,1)}, bf16[2,256,128]{2,1,0:T(8,128)(2,1)}, u32[]{:S(2)}, u32[]{:S(2)}) collective-permute-start(bf16[2,256,128]{2,1,0:T(8,128)(2,1)} %param.15), channel_id=1, source_target_pairs={{0,0},{128,1},{144,2},{16,3},{130,16},{2,17},{18,18},{146,19},{1,1... | collective-permute-start | bytes 393224 | tf_op jit(solution)/shard_map/ppermute | solution.py:44
  42.5 13.3 %all-to-all-start = ((bf16[8,64,256]{2,1,0:T(8,128)(2,1)}), bf16[8,64,256]{2,1,0:T(8,128)(2,1)S(1)}, u32[]{:S(2)}, u32[]{:S(2)}) async-start(bf16[8,64,256]{2,1,0:T(8,128)(2,1)} %bitcast.1), calls=%async_computation | async-start | bytes 524288 | tf_op jit(solution)/shard_map/all_to_all | solution.py:237
  48.7 13.0 %collective-permute-start.11 = (bf16[4,448,128]{2,1,0:T(8,128)(2,1)S(1)}, bf16[4,448,128]{2,1,0:T(8,128)(2,1)}, u32[]{:S(2)}, u32[]{:S(2)}) collective-permute-start(bf16[4,448,128]{2,1,0:T(8,128)(2,1)S(1)} %get-tuple-element.56.own), channel_id=1, source_target_pairs={{0,32},{32,64},{64,96},{96,0},{1,33},{33,65},{65,97},{97,1},{2,34}... | collective-permute-start | bytes 1376264 | tf_op jit(solution)/shard_map/ppermute | solution.py:303
  50.0 11.7 %collective-permute-start.12 = (bf16[4,448,128]{2,1,0:T(8,128)(2,1)S(1)}, bf16[4,448,128]{2,1,0:T(8,128)(2,1)}, u32[]{:S(2)}, u32[]{:S(2)}) collective-permute-start(bf16[4,448,128]{2,1,0:T(8,128)(2,1)S(1)} %get-tuple-element.56.own), channel_id=1, source_target_pairs={{0,96},{32,0},{64,32},{96,64},{1,97},{33,1},{65,33},{97,65},{2,98}... | collective-permute-start | bytes 1376264 | tf_op jit(solution)/shard_map/ppermute | solution.py:303
  62.4 19.2 %all-to-all-start.1 = ((bf16[8,64,256]{2,1,0:T(8,128)(2,1)}), bf16[8,64,256]{2,1,0:T(8,128)(2,1)S(1)}, u32[]{:S(2)}, u32[]{:S(2)}) async-start(bf16[8,64,256]{2,1,0:T(8,128)(2,1)} %broadcast_in_dim.11), calls=%async_computation.1 | async-start | bytes 524288 | tf_op jit(solution)/shard_map/all_to_all | solution.py:48
  72.0 11.1 %collective-permute-start.2 = (bf16[1024,128]{1,0:T(8,128)(2,1)S(1)}, bf16[1024,128]{1,0:T(8,128)(2,1)}, u32[]{:S(2)}, u32[]{:S(2)}) collective-permute-start(bf16[1024,128]{1,0:T(8,128)(2,1)S(1)} %maximum_select_fusion.x), channel_id=1, source_target_pairs={{0,16},{16,0},{1,17},{17,1},{2,18},{18,2},{3,19},{19,3},{4,20},{20... | collective-permute-start | bytes 786440 | tf_op jit(solution)/shard_map/ppermute | solution.py:20
  92.5 13.2 %collective-permute-start.17 = (bf16[4,448,128]{2,1,0:T(8,128)(2,1)}, bf16[4,448,128]{2,1,0:T(8,128)(2,1)}, u32[]{:S(2)}, u32[]{:S(2)}) collective-permute-start(bf16[4,448,128]{2,1,0:T(8,128)(2,1)} %get-tuple-element.82.own), channel_id=1, source_target_pairs={{0,32},{32,64},{64,96},{96,0},{1,33},{33,65},{65,97},{97,1},{2,34}... | collective-permute-start | bytes 1376264 | tf_op jit(solution)/shard_map/ppermute | solution.py:303
  93.0 12.7 %collective-permute-start.18 = (bf16[4,448,128]{2,1,0:T(8,128)(2,1)}, bf16[4,448,128]{2,1,0:T(8,128)(2,1)}, u32[]{:S(2)}, u32[]{:S(2)}) collective-permute-start(bf16[4,448,128]{2,1,0:T(8,128)(2,1)} %get-tuple-element.82.own), channel_id=1, source_target_pairs={{0,96},{32,0},{64,32},{96,64},{1,97},{33,1},{65,33},{97,65},{2,98}... | collective-permute-start | bytes 1376264 | tf_op jit(solution)/shard_map/ppermute | solution.py:303
  98.2 12.5 %collective-permute-start.21 = (bf16[1024,128]{1,0:T(8,128)(2,1)}, bf16[1024,128]{1,0:T(8,128)(2,1)}, u32[]{:S(2)}, u32[]{:S(2)}) collective-permute-start(bf16[1024,128]{1,0:T(8,128)(2,1)} %get-tuple-element.74), channel_id=1, source_target_pairs={{0,4},{4,0},{1,5},{5,1},{2,6},{6,2},{3,7},{7,3},{8,12},{12,8},{9,1... | collective-permute-start | bytes 786440 | tf_op jit(solution)/shard_map/ppermute | solution.py:20
  98.4 12.2 %collective-permute-start.19 = (bf16[1024,128]{1,0:T(8,128)(2,1)}, bf16[1024,128]{1,0:T(8,128)(2,1)}, u32[]{:S(2)}, u32[]{:S(2)}) collective-permute-start(bf16[1024,128]{1,0:T(8,128)(2,1)} %get-tuple-element.72), channel_id=1, source_target_pairs={{0,128},{128,0},{1,129},{129,1},{2,130},{130,2},{3,131},{131,3},{4... | collective-permute-start | bytes 786440 | tf_op jit(solution)/shard_map/ppermute | solution.py:20
  101.5 15.7 %all-to-all-start.2 = ((bf16[8,80,256]{2,1,0:T(8,128)(2,1)}), bf16[8,80,256]{2,1,0:T(8,128)(2,1)S(1)}, u32[]{:S(2)}, u32[]{:S(2)}) async-start(bf16[8,80,256]{2,1,0:T(8,128)(2,1)} %add_convert_fusion), calls=%async_computation.2 | async-start | bytes 655360 | tf_op jit(solution)/shard_map/all_to_all | solution.py:237
  118.1 13.9 %all-to-all-start.3 = ((bf16[8,144,256]{2,1,0:T(8,128)(2,1)}), bf16[8,144,256]{2,1,0:T(8,128)(2,1)S(1)}, u32[]{:S(2)}, u32[]{:S(2)}) async-start(bf16[8,144,256]{2,1,0:T(8,128)(2,1)} %pad_maximum_fusion), calls=%async_computation.3 | async-start | bytes 1179648 | tf_op jit(solution)/shard_map/all_to_all | solution.py:374
  140.3 11.1 %all-to-all-start.4 = ((bf16[8,64,256]{2,1,0:T(8,128)(2,1)}), bf16[8,64,256]{2,1,0:T(8,128)(2,1)S(1)}, u32[]{:S(2)}, u32[]{:S(2)}) async-start(bf16[8,64,256]{2,1,0:T(8,128)(2,1)} %broadcast_in_dim.13), calls=%async_computation.4 | async-start | bytes 524288 | tf_op jit(solution)/shard_map/all_to_all | solution.py:48
  144.6 13.1 %collective-permute-start.27 = (bf16[1024,128]{1,0:T(8,128)(2,1)S(1)}, bf16[1024,128]{1,0:T(8,128)(2,1)S(1)}, u32[]{:S(2)}, u32[]{:S(2)}) collective-permute-start(bf16[1024,128]{1,0:T(8,128)(2,1)S(1)} %fusion.2.x), channel_id=1, source_target_pairs={{0,128},{128,0},{1,129},{129,1},{2,130},{130,2},{3,131},{131,3},{4... | collective-permute-start | bytes 786440 | tf_op jit(solution)/shard_map/ppermute | solution.py:20
  146.1 11.7 %collective-permute-start.28 = (bf16[1024,128]{1,0:T(8,128)(2,1)S(1)}, bf16[1024,128]{1,0:T(8,128)(2,1)S(1)}, u32[]{:S(2)}, u32[]{:S(2)}) collective-permute-start(bf16[1024,128]{1,0:T(8,128)(2,1)S(1)} %fusion.2.x), channel_id=1, source_target_pairs={{0,16},{16,0},{1,17},{17,1},{2,18},{18,2},{3,19},{19,3},{4,20},{20... | collective-permute-start | bytes 786440 | tf_op jit(solution)/shard_map/ppermute | solution.py:20
  148.5 15.2 %collective-permute-start.30 = (bf16[1024,128]{1,0:T(8,128)(2,1)S(1)}, bf16[1024,128]{1,0:T(8,128)(2,1)}, u32[]{:S(2)}, u32[]{:S(2)}) collective-permute-start(bf16[1024,128]{1,0:T(8,128)(2,1)S(1)} %fusion.2.x), channel_id=1, source_target_pairs={{0,8},{8,0},{1,9},{9,1},{2,10},{10,2},{3,11},{11,3},{4,12},{12,4},... | collective-permute-start | bytes 786440 | tf_op jit(solution)/shard_map/ppermute | solution.py:20
  151.3 12.4 %collective-permute-start.32 = (bf16[512,256]{1,0:T(8,128)(2,1)S(1)}, bf16[512,256]{1,0:T(8,128)(2,1)S(1)}, u32[]{:S(2)}, u32[]{:S(2)}) collective-permute-start(bf16[512,256]{1,0:T(8,128)(2,1)S(1)} %bitcast.43), channel_id=1, source_target_pairs={{0,16},{16,0},{1,17},{17,1},{2,18},{18,2},{3,19},{19,3},{4,20},{20... | collective-permute-start | bytes 786440 | tf_op jit(solution)/shard_map/ppermute | solution.py:20
  178.1 12.0 %collective-permute-start.36 = (bf16[1024,128]{1,0:T(8,128)(2,1)}, bf16[1024,128]{1,0:T(8,128)(2,1)S(1)}, u32[]{:S(2)}, u32[]{:S(2)}) collective-permute-start(bf16[1024,128]{1,0:T(8,128)(2,1)} %get-tuple-element.95), channel_id=1, source_target_pairs={{0,8},{8,0},{1,9},{9,1},{2,10},{10,2},{3,11},{11,3},{4,12},{12,4},... | collective-permute-start | bytes 786440 | tf_op jit(solution)/shard_map/ppermute | solution.py:20
  206.8 12.3 %collective-permute-start.39 = (bf16[1024,128]{1,0:T(8,128)(2,1)S(1)}, bf16[1024,128]{1,0:T(8,128)(2,1)S(1)}, u32[]{:S(2)}, u32[]{:S(2)}) collective-permute-start(bf16[1024,128]{1,0:T(8,128)(2,1)S(1)} %maximum_select_fusion.1), channel_id=1, source_target_pairs={{0,0},{128,1},{16,2},{144,3},{2,16},{130,17},{18,18},{146,19},{1,1... | collective-permute-start | bytes 786440 | tf_op jit(solution)/shard_map/ppermute | solution.py:36
  (43 other events, 408.9 us)
